TPU v7x, 32 devices: a whole 2x2x4 slice. The times are simulated.
32 devices in a mesh: dp: 8 (over z, x), section: 4 (over y, core).
Axes of the slice: x: 2, y: 2, z: 4, core: 2. Of those that a mesh axis runs over, the one named last changes fastest.
Arguments:
- latents: bfloat16 [16, 64, 1536], P('dp', None, 'section'), may hold values from -6 to 6
- media: bfloat16 [16, 1024, 1536], P('dp'), may hold values from -6 to 6
- frames: int32 [16], P('dp'), may hold values from 1 to 8, as said below
- cotangent: bfloat16 [16, 64, 1536], P('dp', None, 'section'), may hold values from -6 to 6
- w_query: bfloat16 [2, 1536, 1536], P(None, 'dp'), may hold values from -0.15625 to 0.15625
- w_keyval: bfloat16 [2, 1536, 3072], P(None, 'dp'), may hold values from -0.15625 to 0.15625
- w_output: bfloat16 [2, 1536, 1536], P(None, 'dp'), may hold values from -1.25 to 1.25
- w_inner: bfloat16 [2, 1536, 6144], P(None, 'dp'), may hold values from -0.15625 to 0.15625
- w_outer: bfloat16 [2, 6144, 1536], P(None, 'dp'), may hold values from -0.078125 to 0.078125
- norm_gains: bfloat16 [2, 3, 1536], P(None, None, 'dp'), may hold values from 0.25 to 1.75
- norm_biases: bfloat16 [2, 3, 1536], P(None, None, 'dp'), may hold values from -1 to 1
Outputs:
- latents_out: bfloat16 [16, 64, 1536], P('dp', None, 'section')
- media_grad: float32 [16, 1024, 1536], P('dp', None, 'section')
- latents_grad: float32 [16, 64, 1536], P('dp', None, 'section')
- grad_query: float32 [2, 1536, 1536], P(None, 'dp')
- grad_keyval: float32 [2, 1536, 3072], P(None, 'dp')
- grad_output: float32 [2, 1536, 1536], P(None, 'dp')
- grad_inner: float32 [2, 1536, 6144], P(None, 'dp')
- grad_outer: float32 [2, 6144, 1536], P(None, 'dp')
- grad_gains: float32 [2, 2, 1536], P(None, None, 'dp')
- grad_biases: float32 [2, 2, 1536], P(None, None, 'dp')
- grad_ffn_norm: float32 [2, 2, 1536], P(None, None, 'dp')
Inputs may be any that keep to these rules, and one draw needn't show every extreme that they name: In each aligned block of 2 videos in order, one video has 8 frames.
All inputs are finite; a program needn't handle non-finite values.
Results may differ from a plain program's by a relative error of at most 0.019.
Values may be sent and summed in bfloat16 or wider, within the bound.
No kernel may reach another device: no remote copies, remote signals or barrier semaphores. Data moves between devices by JAX's collectives and lax.ppermute only.
A program may use at most 448 MiB of HBM per device.

v0:
```python
import jax
import jax.numpy as jnp
from jax import lax
from jax.sharding import PartitionSpec as P

H = 16
MAXF = 8


eps = 1e-05


def shifted(array, axis, by):
    size = lax.axis_size(axis)
    pairs = [(i, i + by) for i in range(size) if 0 <= i + by < size]
    return lax.ppermute(array, axis, pairs)


def layer_norm(value, gain, shift):
    centred = value - jnp.mean(value, axis=-1, keepdims=True)
    spread = jnp.mean(centred * centred, axis=-1, keepdims=True)
    return centred * lax.rsqrt(spread + eps) * gain + shift


def contract_rows(left, right):
    return lax.dot_general(
        left, right, (((0,), (0,)), ((), ())), preferred_element_type=jnp.float32
    )


def contract_cols(left, right):
    return lax.dot_general(
        left, right, (((1,), (1,)), ((), ())), preferred_element_type=jnp.float32
    )


def attn_forward(state, pictures, count, weights):
    w_query, w_keyval, w_output = (weights[0], weights[1], weights[2])
    gains = weights[5].astype(jnp.float32)
    biases = weights[6].astype(jnp.float32)
    width = state.shape[1]
    size = width // H
    scale = size ** (-0.5)
    media_len = pictures.shape[0]
    lat_len = state.shape[0]
    media_f = pictures.astype(jnp.float32)
    media_norm = layer_norm(media_f, gains[0], biases[0]).astype(jnp.bfloat16)
    lat_norm = layer_norm(state, gains[1], biases[1]).astype(jnp.bfloat16)
    keys_in = jnp.concatenate([media_norm, lat_norm], axis=0)
    query = jnp.dot(lat_norm, w_query, preferred_element_type=jnp.float32).astype(jnp.bfloat16)
    keyval = jnp.dot(keys_in, w_keyval, preferred_element_type=jnp.float32).astype(jnp.bfloat16)
    query_h = query.reshape(lat_len, H, size)
    key_h = keyval[:, :width].reshape(-1, H, size)
    value_h = keyval[:, width:].reshape(-1, H, size)
    keep = jnp.concatenate(
        [jnp.arange(media_len) < count * (media_len // MAXF), jnp.ones((lat_len,), dtype=bool)]
    )
    scores = jnp.einsum("qhd,khd->hqk", query_h, key_h, preferred_element_type=jnp.float32) * scale
    scores = jnp.where(keep[None, None, :], scores, -1e30)
    expo = jnp.exp(scores - jnp.max(scores, axis=-1, keepdims=True))
    probs = expo / jnp.sum(expo, axis=-1, keepdims=True)
    probs_low = probs.astype(jnp.bfloat16)
    attended = jnp.einsum("hqk,khd->qhd", probs_low, value_h, preferred_element_type=jnp.float32)
    attended = attended.reshape(lat_len, width).astype(jnp.bfloat16)
    mid = (state + jnp.dot(attended, w_output, preferred_element_type=jnp.float32)).astype(
        jnp.bfloat16
    )
    kept = (
        media_f,
        lat_norm,
        keys_in,
        query_h,
        key_h,
        value_h,
        probs,
        probs_low,
        attended,
        gains,
        biases,
    )
    return (mid, kept)


def attn_back_input(seed, state, pictures, count, weights):
    w_query, w_keyval, w_output = (weights[0], weights[1], weights[2])
    unused_mid, kept = attn_forward(state, pictures, count, weights)
    (
        media_f,
        lat_norm,
        keys_in,
        query_h,
        key_h,
        value_h,
        probs,
        probs_low,
        attended,
        gains,
        biases,
    ) = kept
    width = state.shape[1]
    size = width // H
    scale = size ** (-0.5)
    media_len = pictures.shape[0]
    lat_len = state.shape[0]
    d_branch = seed.astype(jnp.bfloat16)
    d_attended = contract_cols(d_branch, w_output).astype(jnp.bfloat16).reshape(lat_len, H, size)
    d_probs = jnp.einsum("qhd,khd->hqk", d_attended, value_h, preferred_element_type=jnp.float32)
    d_scores = probs * (d_probs - jnp.sum(probs * d_probs, axis=-1, keepdims=True))
    d_scores = d_scores.astype(jnp.bfloat16)
    d_query = (
        jnp.einsum("hqk,khd->qhd", d_scores, key_h, preferred_element_type=jnp.float32) * scale
    )
    d_query = d_query.reshape(lat_len, width).astype(jnp.bfloat16)
    d_key = (
        jnp.einsum("hqk,qhd->khd", d_scores, query_h, preferred_element_type=jnp.float32) * scale
    )
    d_value = jnp.einsum("hqk,qhd->khd", probs_low, d_attended, preferred_element_type=jnp.float32)
    d_keyval = jnp.concatenate(
        [d_key.reshape(-1, width), d_value.reshape(-1, width)], axis=1
    ).astype(jnp.bfloat16)
    d_keys = contract_cols(d_keyval, w_keyval)
    d_latnorm = contract_cols(d_query, w_query) + d_keys[media_len:]
    unused_value, lat_back = jax.vjp(layer_norm, state, gains[1], biases[1])
    d_lat, d_gain_lat, d_bias_lat = lat_back(d_latnorm)
    unused_value, media_back = jax.vjp(layer_norm, media_f, gains[0], biases[0])
    d_media, d_gain_media, d_bias_media = media_back(d_keys[:media_len])
    zero_row = jnp.zeros_like(d_gain_lat)
    gain_part = jnp.stack([d_gain_media, d_gain_lat, zero_row])
    bias_part = jnp.stack([d_bias_media, d_bias_lat, zero_row])
    stash = (keys_in, d_keyval, lat_norm, d_query, attended, d_branch)
    return (seed + d_lat, d_media, gain_part, bias_part, stash)


def ffn_forward(state, weights):
    w_inner, w_outer = (weights[3], weights[4])
    gains = weights[5].astype(jnp.float32)
    biases = weights[6].astype(jnp.float32)
    mid_norm = layer_norm(state, gains[2], biases[2]).astype(jnp.bfloat16)
    hidden = jnp.dot(mid_norm, w_inner, preferred_element_type=jnp.float32)
    active = jax.nn.gelu(hidden, approximate=False).astype(jnp.bfloat16)
    result = (state + jnp.dot(active, w_outer, preferred_element_type=jnp.float32)).astype(
        jnp.bfloat16
    )
    return (result, (mid_norm, hidden, active, gains, biases))


def ffn_back_input(seed, state, weights):
    w_inner, w_outer = (weights[3], weights[4])
    unused_result, kept = ffn_forward(state, weights)
    mid_norm, hidden, active, gains, biases = kept
    grad_z = seed.astype(jnp.bfloat16)
    d_active = contract_cols(grad_z, w_outer)
    unused_value, gelu_back = jax.vjp(lambda v: jax.nn.gelu(v, approximate=False), hidden)
    d_hidden = gelu_back(d_active)[0].astype(jnp.bfloat16)
    d_midnorm = contract_cols(d_hidden, w_inner)
    unused_value, mid_back = jax.vjp(layer_norm, state, gains[2], biases[2])
    d_mid_part, d_gain_mid, d_bias_mid = mid_back(d_midnorm)
    zero_row = jnp.zeros_like(d_gain_mid)
    gain_part = jnp.stack([zero_row, zero_row, d_gain_mid])
    bias_part = jnp.stack([zero_row, zero_row, d_bias_mid])
    return (seed + d_mid_part, gain_part, bias_part, (active, grad_z, mid_norm, d_hidden))


def attn_weight_grads(sums, stash):
    keys_in, d_keyval, lat_norm, d_query, attended, d_branch = stash
    return (
        sums[0] + contract_rows(lat_norm, d_query),
        sums[1] + contract_rows(keys_in, d_keyval),
        sums[2] + contract_rows(attended, d_branch),
        sums[3],
        sums[4],
        sums[5],
        sums[6],
    )


def ffn_weight_grads(sums, stash):
    active, grad_z, mid_norm, d_hidden = stash
    return (
        sums[0],
        sums[1],
        sums[2],
        sums[3] + contract_rows(mid_norm, d_hidden),
        sums[4] + contract_rows(active, grad_z),
        sums[5],
        sums[6],
    )


def keep_sums(sums, stash):
    return sums


def stash_into():
    updated = []
    return tuple(updated)


def shards(
    latents,
    media,
    frames,
    cotangent,
    w_query,
    w_keyval,
    w_output,
    w_inner,
    w_outer,
    norm_gains,
    norm_biases,
):
    sections = lax.axis_size("section")
    section = lax.axis_index("section")
    level = section // 2
    attention = section % 2 == 0
    count_mb = media.shape[0]
    layers = w_query.shape[0]
    pick_query = lax.dynamic_index_in_dim(w_query, level, 0)
    pick_keyval = lax.dynamic_index_in_dim(w_keyval, level, 0)
    pick_output = lax.dynamic_index_in_dim(w_output, level, 0)
    pick_inner = lax.dynamic_index_in_dim(w_inner, level, 0)
    pick_outer = lax.dynamic_index_in_dim(w_outer, level, 0)
    pick_gains = lax.dynamic_index_in_dim(norm_gains, level, 0)
    pick_biases = lax.dynamic_index_in_dim(norm_biases, level, 0)
    gathered = (
        lax.all_gather(pick_query, "dp", axis=1, tiled=True),
        lax.all_gather(pick_keyval, "dp", axis=1, tiled=True),
        lax.all_gather(pick_output, "dp", axis=1, tiled=True),
        lax.all_gather(pick_inner, "dp", axis=1, tiled=True),
        lax.all_gather(pick_outer, "dp", axis=1, tiled=True),
        lax.all_gather(pick_gains, "dp", axis=2, tiled=True),
        lax.all_gather(pick_biases, "dp", axis=2, tiled=True),
    )
    weights = tuple((item[0] for item in gathered))
    starts, targets = (
        lax.all_gather(latents, "section", axis=2, tiled=True),
        lax.all_gather(cotangent, "section", axis=2, tiled=True),
    )
    lat_len = starts.shape[1]
    width = starts.shape[2]
    media_len = media.shape[1]
    hidden_len = w_inner.shape[2]
    keys_len = media_len + lat_len
    ticks = count_mb + sections - 1

    def forward_tick(tick, carry):
        incoming, saved, finals = carry
        micro = tick - section
        valid = (micro >= 0) & (micro < count_mb)
        slot = jnp.clip(micro, 0, count_mb - 1)
        first = lax.dynamic_index_in_dim(starts, slot, 0, keepdims=False)
        state = jnp.where(section == 0, first, incoming)
        pictures = lax.dynamic_index_in_dim(media, slot, 0, keepdims=False)
        count = frames[slot]

        def compute():
            state_f = state.astype(jnp.float32)
            return lax.cond(
                attention,
                lambda: attn_forward(state_f, pictures, count, weights)[0],
                lambda: ffn_forward(state_f, weights)[0],
            )

        result = lax.cond(valid, compute, lambda: jnp.zeros((lat_len, width), jnp.bfloat16))
        old_saved = lax.dynamic_index_in_dim(saved, slot, 0, keepdims=False)
        saved = lax.dynamic_update_index_in_dim(saved, jnp.where(valid, state, old_saved), slot, 0)
        old_final = lax.dynamic_index_in_dim(finals, slot, 0, keepdims=False)
        new_final = jnp.where(
            valid & (section == sections - 1), result.astype(jnp.float32), old_final
        )
        finals = lax.dynamic_update_index_in_dim(finals, new_final, slot, 0)
        incoming = shifted(result, "section", 1)
        return (incoming, saved, finals)

    carry = (
        jnp.zeros((lat_len, width), jnp.bfloat16),
        jnp.zeros((count_mb, lat_len, width), jnp.bfloat16),
        jnp.zeros((count_mb, lat_len, width), jnp.float32),
    )
    unused_incoming, saved, finals = lax.fori_loop(0, ticks, forward_tick, carry)
    narrow = jnp.zeros((lat_len, width), jnp.bfloat16)
    zero_attn = (
        jnp.zeros((keys_len, width), jnp.bfloat16),
        jnp.zeros((keys_len, 2 * width), jnp.bfloat16),
        narrow,
        narrow,
        narrow,
        narrow,
    )
    zero_ffn = (
        jnp.zeros((lat_len, hidden_len), jnp.bfloat16),
        narrow,
        narrow,
        jnp.zeros((lat_len, hidden_len), jnp.bfloat16),
    )
    zero_rows = jnp.zeros((3, width), jnp.float32)
    zero_media = jnp.zeros((media_len, width), jnp.float32)
    attn_store = ()
    ffn_store = ()

    def backward_tick(tick, carry):
        incoming, sums, media_grads, lat_grads, attn_store, ffn_store = carry
        micro = tick - (sections - 1 - section)
        valid = (micro >= 0) & (micro < count_mb)
        slot = jnp.clip(micro, 0, count_mb - 1)
        target = lax.dynamic_index_in_dim(targets, slot, 0, keepdims=False)
        seed = jnp.where(section == sections - 1, target, incoming).astype(jnp.float32)
        state = lax.dynamic_index_in_dim(saved, slot, 0, keepdims=False).astype(jnp.float32)
        pictures = lax.dynamic_index_in_dim(media, slot, 0, keepdims=False)
        count = frames[slot]

        def run_attn():
            d_input, d_media, gain_part, bias_part, stash = attn_back_input(
                seed, state, pictures, count, weights
            )
            return (d_input, d_media, gain_part, bias_part, stash, zero_ffn)

        def run_ffn():
            d_input, gain_part, bias_part, stash = ffn_back_input(seed, state, weights)
            return (d_input, zero_media, gain_part, bias_part, zero_attn, stash)

        def run():
            return lax.cond(attention, run_attn, run_ffn)

        def skip():
            return (
                jnp.zeros((lat_len, width), jnp.float32),
                zero_media,
                zero_rows,
                zero_rows,
                zero_attn,
                zero_ffn,
            )

        d_input, d_media, gain_part, bias_part, attn_stash, ffn_stash = lax.cond(valid, run, skip)
        sums = sums[:5] + (sums[5] + gain_part, sums[6] + bias_part)
        sums = lax.cond(valid & attention, attn_weight_grads, keep_sums, sums, attn_stash)
        sums = lax.cond(
            valid & jnp.logical_not(attention), ffn_weight_grads, keep_sums, sums, ffn_stash
        )
        attn_store = stash_into()
        ffn_store = stash_into()
        old_media = lax.dynamic_index_in_dim(media_grads, slot, 0, keepdims=False)
        media_grads = lax.dynamic_update_index_in_dim(
            media_grads, jnp.where(valid, d_media, old_media), slot, 0
        )
        old_lat = lax.dynamic_index_in_dim(lat_grads, slot, 0, keepdims=False)
        lat_grads = lax.dynamic_update_index_in_dim(
            lat_grads, jnp.where(valid & (section == 0), d_input, old_lat), slot, 0
        )
        incoming = shifted(d_input.astype(jnp.bfloat16), "section", -1)
        return (incoming, sums, media_grads, lat_grads, attn_store, ffn_store)

    zero_sums = tuple((jnp.zeros(w.shape, jnp.float32) for w in weights))
    carry = (
        narrow,
        zero_sums,
        jnp.zeros((count_mb, media_len, width), jnp.float32),
        jnp.zeros((count_mb, lat_len, width), jnp.float32),
        attn_store,
        ffn_store,
    )
    unused_incoming, sums, media_grads, lat_grads, attn_store, ffn_store = lax.fori_loop(
        0, ticks, backward_tick, carry
    )
    out_sum, lat_sum, media_sum = (
        lax.psum_scatter(
            finals.astype(jnp.bfloat16), "section", scatter_dimension=2, tiled=True
        ).astype(jnp.float32),
        lax.psum_scatter(
            lat_grads.astype(jnp.bfloat16), "section", scatter_dimension=2, tiled=True
        ).astype(jnp.float32),
        lax.psum_scatter(
            media_grads.astype(jnp.bfloat16), "section", scatter_dimension=2, tiled=True
        ).astype(jnp.float32),
    )
    shares = (
        lax.psum_scatter(sums[0][None], "dp", scatter_dimension=1, tiled=True),
        lax.psum_scatter(sums[1][None], "dp", scatter_dimension=1, tiled=True),
        lax.psum_scatter(sums[2][None], "dp", scatter_dimension=1, tiled=True),
        lax.psum_scatter(sums[3][None], "dp", scatter_dimension=1, tiled=True),
        lax.psum_scatter(sums[4][None], "dp", scatter_dimension=1, tiled=True),
        lax.psum_scatter(sums[5][None], "dp", scatter_dimension=2, tiled=True),
        lax.psum_scatter(sums[6][None], "dp", scatter_dimension=2, tiled=True),
    )
    placed = tuple(
        (
            lax.dynamic_update_index_in_dim(
                jnp.zeros((layers,) + share.shape[1:], jnp.float32), share, level, 0
            )
            for share in shares
        )
    )
    grads = (
        lax.psum(placed[0].astype(jnp.bfloat16), "section").astype(jnp.float32),
        lax.psum(placed[1].astype(jnp.bfloat16), "section").astype(jnp.float32),
        lax.psum(placed[2].astype(jnp.bfloat16), "section").astype(jnp.float32),
        lax.psum(placed[3].astype(jnp.bfloat16), "section").astype(jnp.float32),
        lax.psum(placed[4].astype(jnp.bfloat16), "section").astype(jnp.float32),
        lax.psum(placed[5].astype(jnp.bfloat16), "section").astype(jnp.float32),
        lax.psum(placed[6].astype(jnp.bfloat16), "section").astype(jnp.float32),
    )
    ffn_norm = jnp.stack([grads[5][:, 2], grads[6][:, 2]], axis=1)
    return (
        out_sum.astype(jnp.bfloat16),
        media_sum,
        lat_sum,
        grads[0],
        grads[1],
        grads[2],
        grads[3],
        grads[4],
        grads[5][:, :2],
        grads[6][:, :2],
        ffn_norm,
    )


def solution(mesh):
    return jax.shard_map(
        shards,
        mesh=mesh,
        in_specs=(
            P("dp", None, "section"),
            P("dp", None, None),
            P("dp"),
            P("dp", None, "section"),
            P(None, "dp", None),
            P(None, "dp", None),
            P(None, "dp", None),
            P(None, "dp", None),
            P(None, "dp", None),
            P(None, None, "dp"),
            P(None, None, "dp"),
        ),
        out_specs=(
            P("dp", None, "section"),
            P("dp", None, "section"),
            P("dp", None, "section"),
            P(None, "dp", None),
            P(None, "dp", None),
            P(None, "dp", None),
            P(None, "dp", None),
            P(None, "dp", None),
            P(None, None, "dp"),
            P(None, None, "dp"),
            P(None, None, "dp"),
        ),
        check_vma=False,
    )
```

profile of v0, /device:TPU:0, one launch (start us, length us, event | category | flops | bytes accessed | tf_op | source)
XLA Modules:
  0.0 4436.6 jit_solution(444170261152550410)
XLA Ops:
  19.6 36.0 all_gather.28
  56.2 34.3 all_gather.29
  90.9 6.4 all_gather.27
  97.3 7.0 all_gather.35
  104.3 8.0 all-gather.12.cloned.1.call-done
  112.4 82.3 %all-gather.14.cloned.1.call-done = bf16[1,1536,1536]{2,1,0:T(8,128)(2,1)} async-done(((bf16[1,192,1536]{2,1,0:T(8,128)(2,1)}), bf16[1,1536,1536]{2,1,0:T(8,128)(2,1)}) %all-gather.14.cloned.1.call-update) | async-done | bytes 4718608 | tf_op jit(solution)/shard_map/all_gather | solution.py:228
  194.6 139.0 %all-gather.10.cloned.1.call-done = bf16[1,1536,3072]{2,1,0:T(8,128)(2,1)} async-done(((bf16[1,192,3072]{2,1,0:T(8,128)(2,1)}), bf16[1,1536,3072]{2,1,0:T(8,128)(2,1)}) %all-gather.10.cloned.1.call-update) | async-done | bytes 9437200 | tf_op jit(solution)/shard_map/all_gather | solution.py:227
  333.6 362.6 %all-gather.6.cloned.1.call-done = bf16[1,1536,6144]{2,1,0:T(8,128)(2,1)} async-done(((bf16[1,192,6144]{2,1,0:T(8,128)(2,1)}), bf16[1,1536,6144]{2,1,0:T(8,128)(2,1)}) %all-gather.6.cloned.1.call-update) | async-done | bytes 18874384 | tf_op jit(solution)/shard_map/all_gather | solution.py:229
  696.3 364.4 %all-gather.8.cloned.1.call-done = bf16[1,6144,1536]{2,1,0:T(8,128)(2,1)} async-done(((bf16[1,768,1536]{2,1,0:T(8,128)(2,1)}), bf16[1,6144,1536]{2,1,0:T(8,128)(2,1)}) %all-gather.8.cloned.1.call-update) | async-done | bytes 18874384 | tf_op jit(solution)/shard_map/all_gather | solution.py:230
  1060.8 228.8 %while.52 = (s32[]{:T(128)}, bf16[64,1536]{1,0:T(8,128)(2,1)S(1)}, bf16[2,64,1536]{2,1,0:T(8,128)(2,1)S(1)}, bf16[2,64,1536]{2,1,0:T(8,128)(2,1)S(1)}, s32[]{:T(...) while((s32[]{:T(128)}, bf16[64,1536]{1,0:T(8,128)(2,1)S(1)}, ...), condition=%wide.region_13.14_spmd, body=%wide.region_0.13_spmd.sunk | while | flops 11553978368 | bytes 120965176 | solution.py:280
  1061.2 60.8 %conditional.20 = (bf16[64,1536]{1,0:T(8,128)(2,1)}, bf16[64,1536]{1,0:T(8,128)(2,1)S(1)}) conditional(s32[]{:T(128)} %convert_element_type.439, () %tuple.187, (pred[]{:T(512)}, bf16[64,1536]{1,0:T(8,128)(2,1)S(1)}, bf16[3,1536]{1,0:T(4,128)(2,1)S(1)}, bf16[3,1536]{1,0:T(4,128)(2,1)S(1)}, bf16[1536,6144]{1,0:T(8,128)(2,1)}, ...), branch_computations={%region_1.1_spmd, %region_2.12_spmd} | conditional | flops 11553683456 | bytes 117819040 | solution.py:264
  1061.3 59.8 %conditional.7 = (bf16[64,1536]{1,0:T(8,128)(2,1)}) conditional(s32[]{:T(128)} %convert_element_type.266, (f32[64,1536]{1,0:T(8,128)S(1)}, bf16[3,1536]{1,0:T(4,128)(2,1)S(1)}, bf16[3,1536]{1,0:T(4,128)(2,1)S(1)}, bf16[1536,6144]{1,0:T(8,128)(2,1)}, bf16[6144,1536]{1,0:T(8,128)(2,1)}) %tuple.92, (bf16[2,1024,1536]{2,1,0:T(8,128)(2,1)}, s32[]{:T(128)}, ...), branch_computations={%region_3.4_spmd, %region_6.11_spmd} | conditional | flops 11553585152 | bytes 116835864
  1068.9 13.2 convolution_convert_fusion
  1109.9 6.9 fusion.97
  1124.7 60.8 %conditional.20 = (bf16[64,1536]{1,0:T(8,128)(2,1)}, bf16[64,1536]{1,0:T(8,128)(2,1)S(1)}) conditional(s32[]{:T(128)} %convert_element_type.439, () %tuple.187, (pred[]{:T(512)}, bf16[64,1536]{1,0:T(8,128)(2,1)S(1)}, bf16[3,1536]{1,0:T(4,128)(2,1)S(1)}, bf16[3,1536]{1,0:T(4,128)(2,1)S(1)}, bf16[1536,6144]{1,0:T(8,128)(2,1)}, ...), branch_computations={%region_1.1_spmd, %region_2.12_spmd} | conditional | flops 11553683456 | bytes 117819040 | solution.py:264
  1124.8 59.8 %conditional.7 = (bf16[64,1536]{1,0:T(8,128)(2,1)}) conditional(s32[]{:T(128)} %convert_element_type.266, (f32[64,1536]{1,0:T(8,128)S(1)}, bf16[3,1536]{1,0:T(4,128)(2,1)S(1)}, bf16[3,1536]{1,0:T(4,128)(2,1)S(1)}, bf16[1536,6144]{1,0:T(8,128)(2,1)}, bf16[6144,1536]{1,0:T(8,128)(2,1)}) %tuple.92, (bf16[2,1024,1536]{2,1,0:T(8,128)(2,1)}, s32[]{:T(128)}, ...), branch_computations={%region_3.4_spmd, %region_6.11_spmd} | conditional | flops 11553585152 | bytes 116835864
  1132.4 13.2 convolution_convert_fusion
  1173.4 6.9 fusion.97
  1188.9 20.4 collective-permute-start
  1211.4 8.2 collective-permute-start
  1221.8 66.0 %collective-permute-start = (bf16[64,1536]{1,0:T(8,128)(2,1)}, bf16[64,1536]{1,0:T(8,128)(2,1)S(1)}, u32[]{:S(2)}, u32[]{:S(2)}) collective-permute-start(bf16[64,1536]{1,0:T(8,128)(2,1)} %get-tuple-element.1949), channel_id=1, source_target_pairs={{0,1},{1,2},{2,3},{4,5},{5,6},{6,7},{8,9},{9,10},{10,11},{12,13},{... | collective-permute-start | bytes 589832 | tf_op jit(solution)/shard_map/while/body/eval_jaxpr/ppermute | solution.py:16
  1295.3 8.8 broadcast_in_dim.178
  1309.0 12.5 broadcast_in_dim.179
  1321.6 12.6 broadcast_in_dim.180
  1338.0 724.1 %while.53 = (s32[]{:T(128)}, bf16[64,1536]{1,0:T(8,128)(2,1)}, f32[1536,1536]{1,0:T(8,128)}, f32[1536,3072]{1,0:T(8,128)}, f32[1536,1536]{1,0:T(8,128)}, /*index...) while((s32[]{:T(128)}, bf16[64,1536]{1,0:T(8,128)(2,1)}, ...), condition=%wide.region_45.46_spmd.clone, body=%wide.region_15.45_spmd.clone.sunk | while | flops 36139843584 | bytes 677025280 | solution.py:363
  1339.3 22.8 conditional.21
  1382.4 22.7 conditional.21
  1425.4 15.5 conditional.21
  1452.1 180.9 %collective-permute-done.1 = bf16[64,1536]{1,0:T(8,128)(2,1)} collective-permute-done((bf16[64,1536]{1,0:T(8,128)(2,1)}, bf16[64,1536]{1,0:T(8,128)(2,1)}, u32[]{:S(2)}, u32[]{:S(2)}) %collective-permute-start.1) | collective-permute-done | bytes 196640 | tf_op jit(solution)/shard_map/while/body/eval_jaxpr/ppermute | solution.py:16
  1634.0 149.1 %conditional.21 = ((bf16[64,1536]{1,0:T(8,128)(2,1)}, bf16[1024,1536]{1,0:T(8,128)(2,1)}, f32[3,1536]{1,0:T(4,128)}, f32[3,1536]{1,0:T(4,128)}, bf16[1088,1536]{...) conditional(s32[]{:T(128)} %convert_element_type.441, ...), branch_computations={%region_16.16_spmd, %region_17.40_spmd} | conditional | flops 22822088704 | bytes 415916352 | solution.py:335
  1634.1 141.7 %conditional.9 = (bf16[64,1536]{1,0:T(8,128)(2,1)}, bf16[1024,1536]{1,0:T(8,128)(2,1)}, f32[3,1536]{1,0:T(4,128)}, f32[3,1536]{1,0:T(4,128)}, bf16[1088,1536]{1,...) conditional(s32[]{:T(128)} %convert_element_type.292, ...), branch_computations={%region_18.23_spmd, %region_25.39_spmd} | conditional | flops 22821990400 | bytes 415326400 | solution.py:323
  1661.3 12.7 convolution_convert_fusion.2
  1687.8 5.8 exponential_reduce_fusion.1
  1720.9 5.9 copy.84
  1726.8 6.6 pad_maximum_fusion
  1733.4 16.5 fusion.159
  1796.3 40.2 conditional.22
  1796.3 9.1 convolution_add_fusion.2
  1805.4 22.1 convolution_add_fusion
  1827.5 9.1 convolution_add_fusion.1
  1845.6 147.6 %conditional.21 = ((bf16[64,1536]{1,0:T(8,128)(2,1)}, bf16[1024,1536]{1,0:T(8,128)(2,1)}, f32[3,1536]{1,0:T(4,128)}, f32[3,1536]{1,0:T(4,128)}, bf16[1088,1536]{...) conditional(s32[]{:T(128)} %convert_element_type.441, ...), branch_computations={%region_16.16_spmd, %region_17.40_spmd} | conditional | flops 22822088704 | bytes 415916352 | solution.py:335
  1845.7 140.4 %conditional.9 = (bf16[64,1536]{1,0:T(8,128)(2,1)}, bf16[1024,1536]{1,0:T(8,128)(2,1)}, f32[3,1536]{1,0:T(4,128)}, f32[3,1536]{1,0:T(4,128)}, bf16[1088,1536]{1,...) conditional(s32[]{:T(128)} %convert_element_type.292, ...), branch_computations={%region_18.23_spmd, %region_25.39_spmd} | conditional | flops 22821990400 | bytes 415326400 | solution.py:323
  1871.7 12.7 convolution_convert_fusion.2
  1898.1 5.8 exponential_reduce_fusion.1
  1931.3 5.8 copy.84
  1937.1 6.6 pad_maximum_fusion
  1943.7 16.5 fusion.159
  2006.4 40.2 conditional.22
  2006.4 9.1 convolution_add_fusion.2
  2015.5 22.1 convolution_add_fusion
  2037.5 9.1 convolution_add_fusion.1
  2072.4 16.5 copy.93
  2088.8 8.2 copy.103
  2097.1 127.8 %reduce-scatter.21.cloned.1.call-done = f32[1,192,1536]{2,1,0:T(8,128)} async-done(((f32[1,1536,1536]{2,1,0:T(8,128)}), f32[1,192,1536]{2,1,0:T(8,128)}) %reduce-scatter.21.cloned.1.call-update) | async-done | bytes 1179664 | tf_op jit(solution)/shard_map/reduce_scatter | solution.py:378
  2226.3 165.3 %reduce-scatter.25.cloned.1.call-done = f32[1,192,1536]{2,1,0:T(8,128)} async-done(((f32[1,1536,1536]{2,1,0:T(8,128)}), f32[1,192,1536]{2,1,0:T(8,128)}) %reduce-scatter.25.cloned.1.call-update) | async-done | bytes 1179664 | tf_op jit(solution)/shard_map/reduce_scatter | solution.py:380
  2394.1 313.8 %reduce-scatter.23.cloned.1.call-done = f32[1,192,3072]{2,1,0:T(8,128)} async-done(((f32[1,1536,3072]{2,1,0:T(8,128)}), f32[1,192,3072]{2,1,0:T(8,128)}) %reduce-scatter.23.cloned.1.call-update) | async-done | bytes 2359312 | tf_op jit(solution)/shard_map/reduce_scatter | solution.py:379
  2709.7 606.6 %reduce-scatter.29.cloned.1.call-done = f32[1,768,1536]{2,1,0:T(8,128)} async-done(((f32[1,6144,1536]{2,1,0:T(8,128)}), f32[1,768,1536]{2,1,0:T(8,128)}) %reduce-scatter.29.cloned.1.call-update) | async-done | bytes 4718608 | tf_op jit(solution)/shard_map/reduce_scatter | solution.py:382
  3322.1 601.7 %reduce-scatter.27.cloned.1.call-done = f32[1,192,6144]{2,1,0:T(8,128)} async-done(((f32[1,1536,6144]{2,1,0:T(8,128)}), f32[1,192,6144]{2,1,0:T(8,128)}) %reduce-scatter.27.cloned.1.call-update) | async-done | bytes 4718608 | tf_op jit(solution)/shard_map/reduce_scatter | solution.py:381
  3929.6 59.6 %reduce-scatter.37.cloned.1.call-done = f32[192,3]{1,0:T(8,128)} async-done(((f32[1536,3]{1,0:T(8,128)}), f32[192,3]{1,0:T(8,128)}) %reduce-scatter.37.cloned.1.call-update) | async-done | bytes 2320
  3990.2 64.5 %reduce-scatter.39.cloned.1.call-done = f32[192,3]{1,0:T(8,128)} async-done(((f32[1536,3]{1,0:T(8,128)}), f32[192,3]{1,0:T(8,128)}) %reduce-scatter.39.cloned.1.call-update) | async-done | bytes 2320
  4063.3 13.8 reduce-scatter.31.cloned.1.call-done
  4078.9 21.4 reduce-scatter.35.cloned.1.call-done
  4102.1 58.9 %reduce-scatter.33.cloned.1.call-done = bf16[384,2048]{1,0:T(8,128)(2,1)} async-done(((bf16[1536,2048]{1,0:T(8,128)(2,1)}), bf16[384,2048]{1,0:T(8,128)(2,1)}) %reduce-scatter.33.cloned.1.call-update) | async-done | bytes 1572880
  4170.2 242.1 %all-reduce.8.cloned.1.call-done = (bf16[2,192,1536]{2,1,0:T(8,128)(2,1)}, bf16[2,192,3072]{2,1,0:T(8,128)(2,1)}, bf16[2,192,1536]{2,1,0:T(8,128)(2,1)}, bf16[2,...) async-done(((bf16[2,192,1536]{2,1,0:T(8,128)(2,1)}, bf16[2,192,3072]{2,1,0:T(8,128)(2,1)}, bf16[2,192,1536]{2,1,0:T(8,128)(2,1)}, bf16[2,192,6144]{2,1,0:T(8,128)(2,1)}, ...) | async-done | bytes 14155792 | tf_op jit(solution)/shard_map/psum | solution.py:395
  (581 shorter events, 467.5 us)
Async XLA Ops:
  7.2 105.2 %all-gather.12.cloned.1.call-start = ((), (), s32[]{:S(2)}) async-start(), calls=%async_computation.13 | async-start | bytes 5308416 | tf_op jit(solution)/shard_map/all_gather | solution.py:226
  9.4 185.3 %all-gather.14.cloned.1.call-start = ((), (), s32[]{:S(2)}) async-start(), calls=%async_computation.14 | async-start | bytes 5308416 | tf_op jit(solution)/shard_map/all_gather | solution.py:228
  11.4 322.3 %all-gather.10.cloned.1.call-start = ((), (), s32[]{:S(2)}) async-start(), calls=%async_computation.12 | async-start | bytes 10616832 | tf_op jit(solution)/shard_map/all_gather | solution.py:227
  12.5 683.7 %all-gather.6.cloned.1.call-start = ((), (), s32[]{:S(2)}) async-start(), calls=%async_computation.10 | async-start | bytes 21233664 | tf_op jit(solution)/shard_map/all_gather | solution.py:229
  15.9 40.0 copy-start.31
  15.9 1044.7 %all-gather.8.cloned.1.call-start = ((), (), s32[]{:S(2)}) async-start(), calls=%async_computation.11 | async-start | bytes 21233664 | tf_op jit(solution)/shard_map/all_gather | solution.py:230
  19.2 71.7 %copy-start.28 = (bf16[2,64,384]{2,1,0:T(8,128)(2,1)S(1)}, bf16[2,64,384]{2,1,0:T(8,128)(2,1)}, u32[]{:S(2)}) copy-start(bf16[2,64,384]{2,1,0:T(8,128)(2,1)} %param.27) | copy-start | bytes 294916
  19.2 78.1 %copy-start.29 = (bf16[2,64,384]{2,1,0:T(8,128)(2,1)S(1)}, bf16[2,64,384]{2,1,0:T(8,128)(2,1)}, u32[]{:S(2)}) copy-start(bf16[2,64,384]{2,1,0:T(8,128)(2,1)} %param.30) | copy-start | bytes 294916
  19.2 1041.5 %copy-start.33 = (s32[2]{0:T(128)S(1)}, s32[2]{0:T(128)}, u32[]{:S(2)}) copy-start(s32[2]{0:T(128)} %param.29) | copy-start | bytes 28
  19.3 2205.6 %reduce-scatter.21.cloned.1.call-start = ((), (), s32[]{:S(2)}) async-start(), calls=%async_computation.15 | async-start | bytes 10616832 | tf_op jit(solution)/shard_map/reduce_scatter | solution.py:378
  1061.8 5.6 copy-start.2
  1122.1 2.5 collective-permute-start
  1125.3 5.6 copy-start.2
  1185.5 2.5 collective-permute-start
  1188.9 21.6 collective-permute-start
  1211.4 9.5 collective-permute-start
  1221.8 67.3 %collective-permute-start = (bf16[64,1536]{1,0:T(8,128)(2,1)}, bf16[64,1536]{1,0:T(8,128)(2,1)S(1)}, u32[]{:S(2)}, u32[]{:S(2)}) collective-permute-start(bf16[64,1536]{1,0:T(8,128)(2,1)} %get-tuple-element.1949), channel_id=1, source_target_pairs={{0,1},{1,2},{2,3},{4,5},{5,6},{6,7},{8,9},{9,10},{10,11},{12,13},{... | collective-permute-start | bytes 589832 | tf_op jit(solution)/shard_map/while/body/eval_jaxpr/ppermute | solution.py:16
  1289.6 5.7 copy-start.13
  1362.1 5.2 copy-start.10
  1362.1 11.4 collective-permute-start.1
  1405.1 5.2 copy-start.10
  1405.1 11.2 collective-permute-start.1
  1440.9 5.2 copy-start.10
  1440.9 192.1 %collective-permute-start.1 = (bf16[64,1536]{1,0:T(8,128)(2,1)}, bf16[64,1536]{1,0:T(8,128)(2,1)}, u32[]{:S(2)}, u32[]{:S(2)}) collective-permute-start(bf16[64,1536]{1,0:T(8,128)(2,1)} %get-tuple-element.1979), channel_id=1, source_target_pairs={{1,0},{2,1},{3,2},{5,4},{6,5},{7,6},{9,8},{10,9},{11,10},{13,12},{... | collective-permute-start | bytes 589832 | tf_op jit(solution)/shard_map/while/body/eval_jaxpr/ppermute | solution.py:16
  1452.1 180.9 %copy-start.35 = (s32[2]{0:T(128)S(1)}, s32[2]{0:T(128)}, u32[]{:S(2)}) copy-start(s32[2]{0:T(128)} %copy-done.34) | copy-start | bytes 28 | tf_op jit(solution)/shard_map/while
  1649.8 6.5 copy-start.3
  1704.5 10.4 slice-start.2
  1733.4 16.5 copy-start.6
  1733.4 16.5 copy-start.7
  1752.4 10.4 slice-start
  1757.8 6.3 copy-start.4
  1757.8 11.5 slice-start.4
  1764.1 5.2 slice-start.5
  1783.2 5.2 copy-start.10
  1783.2 54.0 %collective-permute-start.1 = (bf16[64,1536]{1,0:T(8,128)(2,1)}, bf16[64,1536]{1,0:T(8,128)(2,1)}, u32[]{:S(2)}, u32[]{:S(2)}) collective-permute-start(bf16[64,1536]{1,0:T(8,128)(2,1)} %get-tuple-element.1979), channel_id=1, source_target_pairs={{1,0},{2,1},{3,2},{5,4},{6,5},{7,6},{9,8},{10,9},{11,10},{13,12},{... | collective-permute-start | bytes 589832 | tf_op jit(solution)/shard_map/while/body/eval_jaxpr/ppermute | solution.py:16
  1788.4 6.4 copy-start.22
  1788.4 6.4 copy-start.25
  1860.1 6.5 copy-start.3
  1914.9 10.4 slice-start.2
  1943.7 16.5 copy-start.6
  1943.7 16.5 copy-start.7
  1962.7 10.4 slice-start
  1968.1 6.3 copy-start.4
  1968.1 11.5 slice-start.4
  1974.4 5.2 slice-start.5
  1993.2 5.2 copy-start.10
  1993.3 53.6 %collective-permute-start.1 = (bf16[64,1536]{1,0:T(8,128)(2,1)}, bf16[64,1536]{1,0:T(8,128)(2,1)}, u32[]{:S(2)}, u32[]{:S(2)}) collective-permute-start(bf16[64,1536]{1,0:T(8,128)(2,1)} %get-tuple-element.1979), channel_id=1, source_target_pairs={{1,0},{2,1},{3,2},{5,4},{6,5},{7,6},{9,8},{10,9},{11,10},{13,12},{... | collective-permute-start | bytes 589832 | tf_op jit(solution)/shard_map/while/body/eval_jaxpr/ppermute | solution.py:16
  1998.5 6.4 copy-start.22
  1998.5 6.4 copy-start.25
  2062.2 329.4 %reduce-scatter.25.cloned.1.call-start = ((), (), s32[]{:S(2)}) async-start(), calls=%async_computation.17 | async-start | bytes 10616832 | tf_op jit(solution)/shard_map/reduce_scatter | solution.py:380
  2062.9 644.9 %reduce-scatter.23.cloned.1.call-start = ((), (), s32[]{:S(2)}) async-start(), calls=%async_computation.16 | async-start | bytes 21233664 | tf_op jit(solution)/shard_map/reduce_scatter | solution.py:379
  2063.7 1252.7 %reduce-scatter.29.cloned.1.call-start = ((), (), s32[]{:S(2)}) async-start(), calls=%async_computation.19 | async-start | bytes 42467328 | tf_op jit(solution)/shard_map/reduce_scatter | solution.py:382
  2064.4 1859.4 %reduce-scatter.27.cloned.1.call-start = ((), (), s32[]{:S(2)}) async-start(), calls=%async_computation.18 | async-start | bytes 42467328 | tf_op jit(solution)/shard_map/reduce_scatter | solution.py:381
  2065.0 5.6 copy-start.12
  2065.0 1924.2 %reduce-scatter.37.cloned.1.call-start = ((), (), s32[]{:S(2)}) async-start(), calls=%async_computation.23 | async-start | bytes 884736
  2067.0 1987.8 %reduce-scatter.39.cloned.1.call-start = ((), (), s32[]{:S(2)}) async-start(), calls=%async_computation.24 | async-start | bytes 884736
  2068.8 2008.3 %reduce-scatter.31.cloned.1.call-start = ((), (), s32[]{:S(2)}) async-start(), calls=%async_computation.20 | async-start | bytes 491520
  2070.5 2029.7 %reduce-scatter.35.cloned.1.call-start = ((), (), s32[]{:S(2)}) async-start(), calls=%async_computation.22 | async-start | bytes 491520
  2072.3 2088.7 %reduce-scatter.33.cloned.1.call-start = ((), (), s32[]{:S(2)}) async-start(), calls=%async_computation.21 | async-start | bytes 7864320
  2097.0 2315.3 %all-reduce.8.cloned.1.call-start = ((), (), s32[]{:S(2)}) async-start(), calls=%async_computation.25 | async-start | bytes 28311552 | tf_op jit(solution)/shard_map/psum | solution.py:395
  2226.3 483.4 %copy-start.15 = (bf16[2,192,1536]{2,1,0:T(8,128)(2,1)}, bf16[2,192,1536]{2,1,0:T(8,128)(2,1)S(1)}, u32[]{:S(2)}) copy-start(bf16[2,192,1536]{2,1,0:T(8,128)(2,1)S(1)} %constant_dynamic-update-slice_fusion.6) | copy-start | bytes 3538948
  2709.7 612.4 %copy-start.9 = (bf16[2,192,3072]{2,1,0:T(8,128)(2,1)}, bf16[2,192,3072]{2,1,0:T(8,128)(2,1)S(1)}, u32[]{:S(2)}) copy-start(bf16[2,192,3072]{2,1,0:T(8,128)(2,1)S(1)} %constant_dynamic-update-slice_fusion.5) | copy-start | bytes 7077892
  4412.3 7.6 slice-start.8
  4418.2 6.6 slice-start.6
  (54 other events, 130.4 us)
Sparse Core Ops, SparseCore 0:
  10.8 101.5 all-gather.11
  115.1 79.4 all-gather.13
  197.4 136.1 all-gather.9
  335.6 360.6 all-gather.5
  698.2 362.4 all-gather.7
  2062.3 162.5 reduce-scatter.20
  2229.0 162.5 reduce-scatter.24
  2395.5 312.3 reduce-scatter.22
  2711.8 604.5 reduce-scatter.28
  3320.6 603.1 reduce-scatter.26
  3927.7 61.4 reduce-scatter.36
  3993.3 61.3 reduce-scatter.38
  4057.2 19.8 reduce-scatter.30
  4079.5 20.7 reduce-scatter.34
  4102.7 58.3 reduce-scatter.32
  4164.7 247.5 all-reduce.7
where the time goes:
time: 4440 us
  waiting for transfers between devices  3420 us (77%)
  local copies, waits for them, and re-layouts  298 us (7%)
  matrix products  278 us (6%)
  other arithmetic  137 us (3%)
  starting transfers between devices  105 us (2%)
  loops' own time  92.1 us (2%)
  blocking collectives  89.5 us (2%)
    reduce_scatter x1, waiting for transfers between devices, shards(): lax.psum_scatter(sums[4][None], 'dp', scatter_dimension=1, tiled=True)  607 us
    reduce_scatter x1, waiting for transfers between devices, shards(): lax.psum_scatter(sums[3][None], 'dp', scatter_dimension=1, tiled=True)  602 us
    all_gather x1, waiting for transfers between devices, shards(): lax.all_gather(pick_outer, 'dp', axis=1, tiled=True)  364 us
    all_gather x1, waiting for transfers between devices, shards(): lax.all_gather(pick_inner, 'dp', axis=1, tiled=True)  363 us
    reduce_scatter x1, waiting for transfers between devices, shards(): lax.psum_scatter(sums[1][None], 'dp', scatter_dimension=1, tiled=True)  314 us
    psum x1, waiting for transfers between devices, shards(): lax.psum(placed[0].astype(jnp.bfloat16), 'section').astype(jnp.float32)  242 us
    unnamed x21, waiting for transfers between devices  221 us
    ppermute x10, waiting for transfers between devices, shifted(): return lax.ppermute(array, axis, pairs)  187 us
  transfers between devices with their start and end apart: 26, of which 23 were waited for; matrix products, arithmetic and copies ran while one was open for 5% of the time, Pallas kernels for 0%

commit v1 on v0

v1 whole, which is shorter than its diff:
```python
import itertools

import jax
import jax.numpy as jnp
from jax import lax
from jax.experimental import pallas as pl
from jax.experimental.pallas import tpu as pltpu
from jax.sharding import PartitionSpec as P

H = 16
MAXF = 8
eps = 1e-05
bf16 = jnp.bfloat16
f32 = jnp.float32
AXES = ("dp", "section")


def dot(left, right):
    return jnp.dot(left, right, preferred_element_type=f32)


def dot_rows(left, right):
    return lax.dot_general(left, right, (((0,), (0,)), ((), ())), preferred_element_type=f32)


def dot_cols(left, right):
    return lax.dot_general(left, right, (((1,), (1,)), ((), ())), preferred_element_type=f32)


def at(array, index, axis=0):
    return lax.dynamic_index_in_dim(array, index, axis, keepdims=False)


def normed(value):
    centred = value - jnp.mean(value, axis=-1, keepdims=True)
    spread = jnp.mean(centred * centred, axis=-1, keepdims=True)
    rstd = lax.rsqrt(spread + eps)
    return centred * rstd, rstd


def norm_back(hat, rstd, grad):
    mean = jnp.mean(grad, axis=-1, keepdims=True)
    along = jnp.mean(grad * hat, axis=-1, keepdims=True)
    return rstd * (grad - mean - hat * along)


def place(parts, spots, count):
    total = sum(part.shape[0] for part in parts)

    def kernel(spots_ref, *refs):
        sources, out, sems = refs[:-2], refs[-2], refs[-1]
        copies = []
        for source in sources:
            for i in range(source.shape[0]):
                j = len(copies)
                copy = pltpu.make_async_copy(source.at[i], out.at[spots_ref[j]], sems.at[j])
                copy.start()
                copies.append(copy)
        for copy in copies:
            copy.wait()

    shape = parts[0].shape[1:]
    return pl.pallas_call(
        kernel,
        out_shape=jax.ShapeDtypeStruct((count,) + shape, parts[0].dtype),
        in_specs=[pl.BlockSpec(memory_space=pltpu.SMEM)]
        + [pl.BlockSpec(memory_space=pl.ANY)] * len(parts),
        out_specs=pl.BlockSpec(memory_space=pl.ANY),
        scratch_shapes=[pltpu.SemaphoreType.DMA((total,))],
    )(spots.astype(jnp.int32), *parts)


class Wires:
    def __init__(self, dp, section):
        assert section == 4 and dp % 2 == 0
        self.dp, self.section = dp, section
        self.depth = dp // 2
        self.hops = self.depth <= 4
        spots = list(itertools.product(range(self.depth), range(2), range(2), range(2)))

        def number(z, x, y, c):
            return (z * 2 + x) * section + y * 2 + c

        def pairs(move):
            return [(number(*spot), number(*move(*spot))) for spot in spots]

        n = self.depth
        self.swap_x = pairs(lambda z, x, y, c: (z, 1 - x, y, c))
        self.swap_y = pairs(lambda z, x, y, c: (z, x, 1 - y, c))
        self.swap_c = pairs(lambda z, x, y, c: (z, x, y, 1 - c))
        self.away_z = [pairs(lambda z, x, y, c, k=k: ((z + k) % n, x, y, c)) for k in range(n)]
        self.away = {
            (k, f): pairs(lambda z, x, y, c, k=k, f=f: ((z + k) % n, (x + f) % 2, y, c))
            for k in range(n)
            for f in range(2)
        }

    def enter(self):
        self.d = lax.axis_index("dp")
        self.s = lax.axis_index("section")
        self.z, self.x = self.d // 2, self.d % 2
        self.y, self.c = self.s // 2, self.s % 2

    def send(self, value, pairs):
        return lax.ppermute(value, AXES, pairs)

    def near_y(self, value):
        return self.send(value, self.swap_y)

    def near_c(self, value):
        return self.send(value, self.swap_c)

    def by_y(self, mine, other, axis):
        return jnp.where(
            self.y == 0,
            jnp.concatenate([mine, other], axis),
            jnp.concatenate([other, mine], axis),
        )

    def by_c(self, mine, other, axis):
        return jnp.where(
            self.c == 0,
            jnp.concatenate([mine, other], axis),
            jnp.concatenate([other, mine], axis),
        )

    def ring(self, k):
        return (self.z + k) % self.depth

    def gather_blocks(self, block):
        if not self.hops:
            return lax.all_gather(block, "dp", axis=0)
        n = self.depth
        got = [block] + [self.send(block, self.away_z[n - k]) for k in range(1, n)]
        here = jnp.stack(got)
        there = self.send(here, self.swap_x)
        spots = [self.ring(k) * 2 + self.x for k in range(n)]
        spots += [self.ring(k) * 2 + 1 - self.x for k in range(n)]
        return place([g[None] for g in got] + [there], jnp.stack(spots), self.dp)

    def sum_blocks(self, blocks):
        if not self.hops:
            return lax.psum_scatter(
                blocks.astype(f32), "dp", scatter_dimension=0, tiled=False
            )
        n = self.depth
        pairs = blocks.reshape((n, 2) + blocks.shape[1:])
        got = self.send(at(pairs, 1 - self.x, 1), self.swap_x)
        half = at(pairs, self.x, 1).astype(f32) + got.astype(f32)
        low = half.astype(bf16)
        total = at(half, self.z)
        for k in range(1, n):
            total = total + self.send(at(low, self.ring(k)), self.away_z[k]).astype(f32)
        return total

    def gather_rows(self, rows):
        if not self.hops:
            return lax.all_gather(rows, "dp", axis=0, tiled=True)
        n = self.depth
        got = [rows] + [self.send(rows, self.away_z[n - k]) for k in range(1, n)]
        got += [self.send(item, self.swap_x) for item in got]
        return jnp.concatenate(got, 0)

    def sum_rows(self, partial):
        if not self.hops:
            return lax.psum_scatter(partial, "dp", scatter_dimension=0, tiled=True)
        n = self.depth
        half = partial.shape[0] // 2
        got = self.send(partial[half:].astype(bf16), self.swap_x)
        near = partial[:half] + got.astype(f32)
        low = near.astype(bf16).reshape((n, half // n) + partial.shape[1:])
        total = near[: half // n]
        for k in range(1, n):
            total = total + self.send(low[k], self.away_z[k]).astype(f32)
        return total

    def trade(self, blocks):
        if not self.hops:
            mine = jnp.stack([blocks(d) for d in range(self.dp)])
            got = lax.all_to_all(mine, "dp", 0, 0, tiled=True)
            return got, jnp.arange(self.dp)
        n = self.depth
        got, order = [], []
        for f in range(2):
            for k in range(n):
                block = blocks(self.ring(k) * 2 + (self.x + f) % 2)
                got.append(block if k == f == 0 else self.send(block, self.away[k, f]))
                order.append(self.ring(n - k) * 2 + (self.x + f) % 2)
        return jnp.stack(got), jnp.stack(order)

    def spread(self, rows, fill):
        width = rows.shape[1]
        wide = at(rows.reshape(rows.shape[0], 2, width // 2), 1 - self.y, 1)
        got = self.near_y(wide.astype(bf16)).astype(fill)
        mine = at(rows.reshape(rows.shape[0], 2, width // 2), self.y, 1).astype(fill)
        return self.spread_c(self.by_y(mine, got, 0))

    def spread_c(self, cols):
        parts = cols.reshape(cols.shape[0], 2, cols.shape[1] // 2)
        got = self.near_c(at(parts, 1 - self.c, 1).astype(bf16)).astype(cols.dtype)
        return self.by_c(at(parts, self.c, 1)[None], got[None], 0)


def expand(value, heads):
    rows, width = value.shape
    size = width // heads
    owner = lax.broadcasted_iota(jnp.int32, (heads, 1, width), 2) // size
    index = lax.broadcasted_iota(jnp.int32, (heads, 1, width), 0)
    return jnp.where(owner == index, value[None], jnp.zeros((), value.dtype)).reshape(
        heads * rows, width
    )


def collapse(value, heads):
    width = value.shape[1]
    size = width // heads
    owner = lax.broadcasted_iota(jnp.int32, (heads, 1, width), 2) // size
    index = lax.broadcasted_iota(jnp.int32, (heads, 1, width), 0)
    return jnp.sum(
        jnp.where(owner == index, value.reshape(heads, -1, width), 0.0), axis=0
    )


def gelu(hidden):
    return jax.nn.gelu(hidden, approximate=False)


def shards(wires):
    def run(
        latents,
        media,
        frames,
        cotangent,
        w_query,
        w_keyval,
        w_output,
        w_inner,
        w_outer,
        norm_gains,
        norm_biases,
    ):
        wires.enter()
        y, c, s = wires.y, wires.c, wires.s
        dp = wires.dp
        layers, shard, width = w_query.shape
        size = width // H
        scale = size ** (-0.5)
        half = width // 2
        media_len = media.shape[1]
        lat_len = latents.shape[1]
        rows = lat_len // 2
        local = H // 4
        quarter = local * size

        vectors = jnp.concatenate([norm_gains, norm_biases], 1).reshape(layers * 6, shard)
        vectors = lax.all_gather(vectors, "dp", axis=1, tiled=True).astype(f32)
        vectors = vectors.reshape(layers, 2, 3, width)
        gains, biases = vectors[:, 0], vectors[:, 1]

        column = lax.broadcasted_iota(jnp.int32, (width, quarter), 1)
        row = lax.broadcasted_iota(jnp.int32, (width, quarter), 0)
        wanted = (2 * (local * c + column // size) + y) * size + column % size
        pick = (row == wanted).astype(bf16)
        stacked = jnp.stack([w_query, w_keyval[:, :, :width], w_keyval[:, :, width:]], 1)
        picked = dot(stacked.reshape(-1, width), pick).astype(bf16)
        picked = picked.reshape(layers, 3, shard, quarter)
        if wires.hops:
            out_piece = lax.dynamic_slice(
                w_output, (0, size * y, half * c), (layers, size, half)
            )

        def fetch(level):
            got = []
            if level == 0:
                for j in range(3):
                    got.append(wires.gather_blocks(picked[level, j]))
            else:
                both = jnp.concatenate([picked[level, j] for j in range(3)], 1)
                both = wires.gather_blocks(both)
                got = [both[:, :, j * quarter : (j + 1) * quarter] for j in range(3)]
            if wires.hops:
                out = wires.gather_blocks(out_piece[level]).reshape(half, half)
            else:
                out = lax.all_gather(w_output[level], "dp", axis=0, tiled=True)
                out = at(out.reshape(H // 2, 2, size, 2, half), y, 1)
                out = at(out, c, 2).reshape(half, half)
            got = [item.reshape(width, quarter) for item in got] + [out]
            far = [wires.near_c(item) for item in got]
            return [(a, b) for a, b in zip(got, far)]

        def inner_block(d):
            span = w_inner.shape[2] // dp
            part = shard // 4
            if not wires.hops:
                return w_inner[:, :, d * span : (d + 1) * span]
            return lax.dynamic_slice(w_inner, (0, part * s, span * d), (layers, part, span))

        def fetch_inner():
            got, order = wires.trade(inner_block)
            span = w_inner.shape[2] // dp
            if not wires.hops:
                return jnp.transpose(got, (1, 0, 2, 3)).reshape(layers, width, span)
            part = shard // 4
            over_y = wires.near_y(got)
            over_c, over_yc = wires.near_c(got), wires.near_c(over_y)
            spots = []
            for section in (s, s ^ 2, s ^ 1, s ^ 3):
                for i in range(dp):
                    for level in range(layers):
                        spots.append((level * dp + order[i]) * 4 + section)
            parts = [v.reshape(dp * layers, part, span) for v in (got, over_y, over_c, over_yc)]
            out = place(parts, jnp.stack(spots), layers * dp * 4)
            return out.reshape(layers, width, span)

        both = jnp.stack([latents, cotangent])
        got = wires.near_c(at(both, 1 - c, 1))
        wide = wires.by_c(at(both, c, 1), got, 2)
        whole = wires.by_y(wide, wires.near_y(wide), 2)
        whole = jnp.where(y == 0, whole, jnp.roll(whole, rows, axis=1))
        state = whole[0].astype(f32)
        target = whole[1, :rows]

        hat_f, rstd_media = normed(at(media, c).astype(f32))
        hat = hat_f.astype(bf16)
        keep = jnp.arange(media_len) < at(frames, c) * (media_len // MAXF)

        def attention(state, lat_norm, weights, level):
            (q_a, q_b), (k_a, k_b), (v_a, v_b), (o_a, o_b) = weights
            gain, bias = gains[level, 0], biases[level, 0]
            query = [dot(lat_norm, w).astype(bf16) for w in (q_a, q_b)]
            query_x = [expand(q, local) for q in query]
            lifted = jnp.concatenate([dot_cols(q, k) for q, k in zip(query_x, (k_a, k_b))], 0)
            lifted = lifted * scale
            key_g = (lifted * gain).astype(bf16)
            key_l = lifted.astype(bf16)
            shift = jnp.sum(lifted * bias, axis=-1, keepdims=True)
            scores = dot_cols(key_g, hat) + shift
            scores = jnp.where(keep[None], scores, -1e30)
            scores_l = dot_cols(key_l, lat_norm)
            top = jnp.maximum(
                jnp.max(scores, axis=-1, keepdims=True), jnp.max(scores_l, axis=-1, keepdims=True)
            )
            expo, expo_l = jnp.exp(scores - top), jnp.exp(scores_l - top)
            total = jnp.sum(expo, axis=-1, keepdims=True) + jnp.sum(expo_l, axis=-1, keepdims=True)
            probs, probs_l = expo / total, expo_l / total
            low, low_l = probs.astype(bf16), probs_l.astype(bf16)
            mass = jnp.sum(low.astype(f32), axis=-1, keepdims=True)
            mixed_hat = dot(low, hat)
            mixed = (mixed_hat * gain + mass * bias + dot(low_l, lat_norm)).astype(bf16)
            group = local * lat_len
            att = [
                collapse(dot(mixed[i * group : (i + 1) * group], v), local).astype(bf16)
                for i, v in enumerate((v_a, v_b))
            ]
            attended = wires.by_c(att[0], att[1], 1)
            branch = wires.by_c(dot(attended, o_a), dot(attended, o_b), 1)
            kept = (query, query_x, lifted, key_g, key_l, probs, probs_l, low, low_l, mass)
            return branch, kept + (mixed_hat, mixed, attended)

        def attention_back(d_mid, lat_norm, weights, level, kept):
            (q_a, q_b), (k_a, k_b), (v_a, v_b), (o_a, o_b) = weights
            query, query_x, lifted, key_g, key_l, probs, probs_l, low, low_l, mass = kept[:10]
            mixed_hat, mixed, attended = kept[10:]
            gain, bias = gains[level, 0], biases[level, 0]
            group = local * lat_len
            d_cols = d_mid.reshape(lat_len, 2, half)
            d_mine, d_other = at(d_cols, c, 1), at(d_cols, 1 - c, 1)
            d_att = (dot_cols(d_mine, o_a) + dot_cols(d_other, o_b)).astype(bf16)
            d_parts = d_att.reshape(lat_len, 2, quarter)
            d_att = [at(d_parts, c, 1), at(d_parts, 1 - c, 1)]
            d_att_x = [expand(v, local) for v in d_att]
            raised = jnp.concatenate([dot_cols(a, v) for a, v in zip(d_att_x, (v_a, v_b))], 0)
            val_g = (raised * gain).astype(bf16)
            val_l = raised.astype(bf16)
            d_probs = dot_cols(val_g, hat) + jnp.sum(raised * bias, axis=-1, keepdims=True)
            d_probs_l = dot_cols(val_l, lat_norm)
            along = jnp.sum(probs * d_probs, axis=-1, keepdims=True)
            along = along + jnp.sum(probs_l * d_probs_l, axis=-1, keepdims=True)
            ds = (probs * (d_probs - along)).astype(bf16)
            ds_l = (probs_l * (d_probs_l - along)).astype(bf16)
            ds_mass = jnp.sum(ds.astype(f32), axis=-1, keepdims=True)
            ds_hat = dot(ds, hat)
            d_lift = (ds_hat * gain + ds_mass * bias + dot(ds_l, lat_norm)).astype(bf16)
            d_query = [
                (collapse(dot(d_lift[i * group : (i + 1) * group], k), local) * scale).astype(bf16)
                for i, k in enumerate((k_a, k_b))
            ]
            d_lat = dot_cols(d_query[0], q_a) + dot_cols(d_query[1], q_b)
            d_lat = d_lat + dot_rows(
                jnp.concatenate([ds_l, low_l], 0), jnp.concatenate([key_l, val_l], 0)
            )
            d_gain = jnp.sum(lifted * ds_hat + raised * mixed_hat, axis=0)
            d_bias = jnp.sum(lifted * ds_mass + raised * mass, axis=0)
            pairs = (jnp.concatenate([ds, low], 0), jnp.concatenate([key_g, val_g], 0))
            return d_lat, (d_att, d_att_x, d_lift, d_query), (d_gain, d_bias), pairs

        def attention_grads(d_mid, lat_norm, kept, more, extra):
            query, query_x, mixed, attended = kept[0], kept[1], kept[11], kept[12]
            d_att, d_att_x, d_lift, d_query = more
            group = local * lat_len
            cols = d_mid.reshape(lat_len, 2, half)

            def both(mine, other):
                return jnp.concatenate([mine, wires.near_c(other)], 0)

            lat = both(lat_norm, lat_norm)
            mixed_b = both(mixed[:group], mixed[group:])
            d_att_b = both(d_att_x[0], d_att_x[1])
            att_b = both(attended, attended)
            d_mid_b = both(at(cols, c, 1), at(cols, 1 - c, 1))
            lift_b = both(d_lift[:group], d_lift[group:])
            query_b = both(query_x[0], query_x[1])
            d_query_b = both(d_query[0], d_query[1])
            g_value = dot_rows(mixed_b, d_att_b).astype(bf16)
            g_output = dot_rows(att_b, d_mid_b).astype(bf16)
            g_key = (dot_rows(lift_b, query_b) * scale).astype(bf16)
            g_query = dot_rows(lat, d_query_b).astype(bf16)
            parts = []
            g_query = jnp.concatenate([g_query, extra.astype(bf16)], 1)
            for grad in (g_value, g_key, g_query):
                blocks = grad.reshape(dp, shard, grad.shape[1])
                parts.append(wires.sum_blocks(blocks).astype(bf16))
            if wires.hops:
                out = wires.sum_blocks(g_output.reshape(dp, size, half)).astype(bf16)
            else:
                whole = g_output.reshape(H // 2, 1, size, half)
                zero = jnp.zeros_like(whole)
                whole = wires.by_y(whole, zero, 1)
                whole = whole.reshape(dp, shard, half)
                out = wires.sum_blocks(whole).astype(bf16)

            def join(v):
                pair = wires.by_c(v[None], wires.near_c(v)[None], 0)
                return wires.by_y(pair[None], wires.near_y(pair)[None], 0)

            value, key, query_g, out = [join(v) for v in parts + [out]]
            extra_sum = jnp.sum(query_g[..., quarter:].astype(f32), axis=(0, 1))
            query_g = query_g[..., :quarter]
            index = lax.broadcasted_iota(jnp.int32, (half, half), 0)
            goal = lax.broadcasted_iota(jnp.int32, (half, half), 1)
            head, within = index // size, index % size
            order = ((head % local) * 2 + head // local) * size + within
            shuffle = (order == goal).astype(bf16)

            def columns(v):
                v = jnp.transpose(v, (1, 2, 0, 3)).reshape(2 * shard, half)
                v = dot(v, shuffle).reshape(2, shard, half)
                return jnp.concatenate([v[0], v[1]], 1)

            g_keyval = jnp.concatenate([columns(key), columns(value)], 1)
            if wires.hops:
                g_out = jnp.transpose(out, (0, 2, 1, 3)).reshape(shard, width).astype(f32)
            else:
                g_out = jnp.sum(out.astype(f32), 0)
                g_out = jnp.concatenate([g_out[0], g_out[1]], 1)
            return columns(query_g), g_keyval, g_out, extra_sum

        def ffn_grads(active, dz_all, mn_all, d_hidden):
            span = active.shape[1]
            g_outer = dot_rows(active, dz_all).astype(bf16)
            g_inner = dot_rows(mn_all, d_hidden).astype(bf16)
            g_outer = g_outer.reshape(2, 2, span // 4, width)
            g_inner = g_inner.reshape(dp, 2, 2, shard // 4, span)

            def share(v, axis_y, axis_c):
                got = wires.near_c(at(v, 1 - c, axis_c))
                v = (at(v, c, axis_c).astype(f32) + got.astype(f32)).astype(bf16)
                got = wires.near_y(at(v, 1 - y, axis_y))
                return (at(v, y, axis_y).astype(f32) + got.astype(f32)).astype(bf16)

            g_outer = share(g_outer, 0, 1)
            g_inner = share(g_inner, 1, 2)

            def join(v):
                pair = wires.by_y(v[None], wires.near_y(v)[None], 0)
                return wires.by_c(pair[:, None], wires.near_c(pair)[:, None], 1)

            g_outer = join(g_outer).reshape(span, width).astype(f32)
            got, order = wires.trade(lambda d: at(g_inner, d))
            if wires.hops:
                got = place([got], order, dp)
            g_inner = jnp.transpose(got, (1, 0, 2)).reshape(shard // 4, dp * span)
            g_inner = join(g_inner).reshape(shard, dp * span).astype(f32)
            return g_inner, g_outer

        w_attn = [fetch(level) for level in range(layers)]
        w_in = fetch_inner()
        target_all = wires.gather_rows(target)
        x_rows = state[:rows]
        kept, norms = [], []
        for level in range(layers):
            if level == 0:
                x_hat, x_rstd = normed(state)
                lat_norm = (x_hat * gains[0, 1] + biases[0, 1]).astype(bf16)
                x_hat, x_rstd = x_hat[:rows], x_rstd[:rows]
            else:
                x_hat, x_rstd = normed(x_rows)
                mine = (x_hat * gains[level, 1] + biases[level, 1]).astype(bf16)
                lat_norm = jnp.concatenate([mine, wires.near_y(mine)], 0)
            branch, attn_kept = attention(state, lat_norm, w_attn[level], level)
            branch = branch[:rows] + wires.near_y(branch[rows:].astype(bf16)).astype(f32)
            mid = (x_rows + branch).astype(bf16).astype(f32)
            mid_hat, mid_rstd = normed(mid)
            mn = (mid_hat * gains[level, 2] + biases[level, 2]).astype(bf16)
            mn_all = wires.gather_rows(mn)
            hidden = dot(mn_all, w_in[level])
            active = gelu(hidden).astype(bf16)
            result = wires.sum_rows(dot(active, w_outer[level]))
            x_low = (mid + result).astype(bf16)
            x_rows = x_low.astype(f32)
            kept.append((attn_kept, lat_norm, x_hat, x_rstd, mid_hat, mid_rstd))
            norms.append((mn_all, hidden, active))
        latents_out = wires.spread(x_low, bf16)

        grad = target.astype(f32)
        dz_all = target_all
        zero = jnp.zeros((width,), f32)
        out_grads = [None] * layers
        media_pairs = []
        vector_grads = [None] * layers
        pending = None
        for level in reversed(range(layers)):
            attn_kept, lat_norm, x_hat, x_rstd, mid_hat, mid_rstd = kept[level]
            mn_all, hidden, active = norms[level]
            if level < layers - 1:
                dz_all = wires.gather_rows(grad.astype(bf16))
            d_active = dot_cols(dz_all, w_outer[level])
            d_hidden = jax.vjp(gelu, hidden)[1](d_active)[0].astype(bf16)
            d_mn = wires.sum_rows(dot_cols(d_hidden, w_in[level]))
            g_inner, g_outer = ffn_grads(active, dz_all, mn_all, d_hidden)
            d_mid_rows = grad + norm_back(mid_hat, mid_rstd, d_mn * gains[level, 2])
            d_low = d_mid_rows.astype(bf16)
            d_mid = jnp.concatenate([d_low, wires.near_y(d_low)], 0)
            d_lat, more, (d_gain0, d_bias0), pairs = attention_back(
                d_mid, lat_norm, w_attn[level], level, attn_kept
            )
            media_pairs.append(pairs)
            d_norm = d_lat[:rows] + wires.near_y(d_lat[rows:].astype(bf16)).astype(f32)
            grad = d_low.astype(f32) + norm_back(x_hat, x_rstd, d_norm * gains[level, 1])
            if level > 0:
                grad = grad.astype(bf16).astype(f32)
            vector_grads[level] = jnp.stack(
                [
                    d_gain0,
                    jnp.sum(d_norm * x_hat, 0),
                    jnp.sum(d_mn * mid_hat, 0),
                    d_bias0,
                    jnp.sum(d_norm, 0),
                    jnp.sum(d_mn, 0),
                ]
            )
            extra = jnp.zeros((128, width), f32).at[:6].set(vector_grads[level]).T
            g_query, g_keyval, g_out, sums = attention_grads(
                d_mid, lat_norm, attn_kept, more, extra
            )
            out_grads[level] = (g_query, g_keyval, g_out, g_inner, g_outer, sums[:, :6].T)
        latents_grad = wires.spread(grad, f32)

        left = jnp.concatenate([p[0] for p in media_pairs], 0)
        right = jnp.concatenate([p[1] for p in media_pairs], 0)
        d_media = norm_back(hat.astype(f32), rstd_media, dot_rows(left, right))
        d_media = d_media.reshape(media_len, 2, half)
        got = wires.near_y(at(d_media, 1 - y, 1).astype(bf16))
        media_grad = wires.spread_c(at(d_media, y, 1) + got.astype(f32))

        outs = [jnp.stack([out_grads[level][i] for level in range(layers)]) for i in range(6)]
        vec = outs[5].reshape(layers, 2, 3, shard)
        return (
            latents_out,
            media_grad,
            latents_grad,
            outs[0],
            outs[1],
            outs[2],
            outs[3],
            outs[4],
            vec[:, 0, :2],
            vec[:, 1, :2],
            vec[:, :, 2],
        )

    return run


def solution(mesh):
    wires = Wires(mesh.shape["dp"], mesh.shape["section"])
    return jax.shard_map(
        shards(wires),
        mesh=mesh,
        in_specs=(
            P("dp", None, "section"),
            P("dp", None, None),
            P("dp"),
            P("dp", None, "section"),
            P(None, "dp", None),
            P(None, "dp", None),
            P(None, "dp", None),
            P(None, "dp", None),
            P(None, "dp", None),
            P(None, None, "dp"),
            P(None, None, "dp"),
        ),
        out_specs=(
            P("dp", None, "section"),
            P("dp", None, "section"),
            P("dp", None, "section"),
            P(None, "dp", None),
            P(None, "dp", None),
            P(None, "dp", None),
            P(None, "dp", None),
            P(None, "dp", None),
            P(None, None, "dp"),
            P(None, None, "dp"),
            P(None, None, "dp"),
        ),
        check_vma=False,
    )
```

time: 4440 us -> 1570 us (0.35)
  waiting for transfers between devices: 3420 us -> 427 us
  Pallas kernels: 0 us -> 482 us
  local copies, waits for them, and re-layouts: 298 us -> 154 us
  matrix products: 278 us -> 135 us
  loops' own time: 92.1 us -> 0 us
  starting transfers between devices: 105 us -> 172 us
  blocking collectives: 89.5 us -> 30.6 us
    reduce_scatter x5 -> x0, waiting for transfers between devices: 1820 us -> none  [the longest x1 607 us: shards(): lax.psum_scatter(sums[4][None], 'dp', scatter_dimension=1, tiled=True)]
    all_gather x5 -> x0, waiting for transfers between devices: 956 us -> none  [the longest x1 364 us: shards(): lax.all_gather(pick_outer, 'dp', axis=1, tiled=True)]
    pallas_call x0 -> x9, Pallas kernels: none -> 482 us  [place(): pl.pallas_call(kernel, out_shape=jax.ShapeDtypeStruct((count,) + shape, p...]
    psum x1 -> x0, waiting for transfers between devices: 242 us -> none  [shards(): lax.psum(placed[0].astype(jnp.bfloat16), 'section').astype(jnp.float32)]
    ppermute x10 -> x195, waiting for transfers between devices: 187 us -> 427 us  [send(): return lax.ppermute(value, AXES, pairs)]
    unnamed x21 -> x0, waiting for transfers between devices: 221 us -> none
    dot_general x36 -> x78, matrix products: 259 us -> 135 us  [the longest x35 52.4 us: dot(): return jnp.dot(left, right, preferred_element_type=f32)]
    another operation x24 -> x0, loops' own time: 90.5 us -> none  [the longest x1 37.9 us: shards(): lax.fori_loop(0, ticks, backward_tick, carry)]
  transfers between devices with their start and end apart: 26 -> 195, of which waited for: 23 -> 80; matrix products, arithmetic and copies ran while one was open for 5% -> 25% of each run, Pallas kernels for 0% -> 31%
where the time goes in v1:
time: 1570 us; the launch traced here: 1560 us
  Pallas kernels  482 us (31%)
  waiting for transfers between devices  427 us (27%)
  starting transfers between devices  172 us (11%)
  local copies, waits for them, and re-layouts  154 us (10%)
  other arithmetic  148 us (9%)
  matrix products  135 us (9%)
  blocking collectives  30.6 us (2%)
    pallas_call x9, Pallas kernels, place(): pl.pallas_call(kernel, out_shape=jax.ShapeDtypeStruct((count,) + shape, p...  482 us
    ppermute x195, waiting for transfers between devices, send(): return lax.ppermute(value, AXES, pairs)  427 us
    ppermute x195, starting transfers between devices, send(): return lax.ppermute(value, AXES, pairs)  172 us
    dot_general x35, matrix products, dot(): return jnp.dot(left, right, preferred_element_type=f32)  52.4 us
    dot_general x28, matrix products, dot_cols(): lax.dot_general(left, right, (((1,), (1,)), ((), ())), preferred_element_...  42.7 us
    unnamed x630, local copies, waits for them, and re-layouts  41.4 us
    dot_general x15, matrix products, dot_rows(): lax.dot_general(left, right, (((0,), (0,)), ((), ())), preferred_element_...  39.8 us
  transfers between devices with their start and end apart: 195, of which 80 were waited for; matrix products, arithmetic and copies ran while one was open for 25% of the time, Pallas kernels for 31%

profile of v1, /device:TPU:0, one launch (start us, length us, event | category | flops | bytes accessed | tf_op | source)
XLA Modules:
  0.0 1555.0 jit_solution(10092342306004447511)
XLA Ops:
  7.3 5.1 collective-permute-start.12
  21.3 30.6 %all-gather = bf16[8,192,12]{1,2,0:T(8,128)(2,1)S(1)} all-gather(bf16[1,192,12]{1,2,0:T(8,128)(2,1)S(1)} %bitcast.1026), channel_id=1, replica_groups=mesh['dp'=8,'section'=4] {'dp'}, dimensions={0}, use_global_device_ids=true | all-gather | bytes 41472 | tf_op jit(solution)/shard_map/all_gather | solution.py:256
  59.2 4.3 fusion.4
  72.9 6.9 collective-permute-done.31
  87.8 4.2 collective-permute-done.33
  92.2 9.1 collective-permute-done.34
  106.0 15.1 collective-permute-done.35
  121.2 4.4 collective-permute-done.18
  134.7 4.9 collective-permute-done.3
  144.9 4.9 collective-permute-start.36
  161.0 15.2 collective-permute-done.5.refs_4_
  176.2 37.6 %shard_map.194 = bf16[8,192,384]{2,1,0:T(8,128)(2,1)} custom-call(s32[8]{0:T(128)} %stack.556.spots_ref, bf16[1,192,384]{2,1,0:T(8,128)(2,1)} %copy-done.100, bf16[1,192,384]{2,1,0:T(8,128)(2,1)} %bitcast.977, bf16[1,192,384]{2,1,0:T(8,128)(2,1)} %bitcast.981, bf16[1,192,384]{2,1,0:T(8,128)(2,1)} %bitcast.983, ...), custom_call_target="tpu_custom_call" | custom-call | tf_op jit(solution)/shard_map/pallas_call | solution.py:63
  220.6 4.6 collective-permute-start.72
  227.0 37.6 %shard_map.195 = bf16[8,192,384]{2,1,0:T(8,128)(2,1)} custom-call(s32[8]{0:T(128)} %stack.556.spots_ref, bf16[1,192,384]{2,1,0:T(8,128)(2,1)} %copy-done.99, bf16[1,192,384]{2,1,0:T(8,128)(2,1)} %bitcast.973, bf16[1,192,384]{2,1,0:T(8,128)(2,1)} %bitcast.975, bf16[1,192,384]{2,1,0:T(8,128)(2,1)} %bitcast.979, bf16[4,192,384]{2,1,0:T(8,128)(2,1)} %collective-permute-done.9.refs_4_), custom_call_target="tpu_custom_call" | custom-call | tf_op jit(solution)/shard_map/pallas_call | solution.py:63
  265.9 37.7 %shard_map.196 = bf16[8,192,384]{2,1,0:T(8,128)(2,1)} custom-call(s32[8]{0:T(128)} %stack.556.spots_ref, bf16[1,192,384]{2,1,0:T(8,128)(2,1)} %copy-done.98, bf16[1,192,384]{2,1,0:T(8,128)(2,1)} %bitcast.955, bf16[1,192,384]{2,1,0:T(8,128)(2,1)} %bitcast.957, bf16[1,192,384]{2,1,0:T(8,128)(2,1)} %bitcast.959, ...), custom_call_target="tpu_custom_call" | custom-call | tf_op jit(solution)/shard_map/pallas_call | solution.py:63
  304.8 37.6 %shard_map.197 = bf16[8,96,768]{2,1,0:T(8,128)(2,1)} custom-call(s32[8]{0:T(128)} %stack.556.spots_ref, bf16[1,96,768]{2,1,0:T(8,128)(2,1)} %copy-done.102, bf16[1,96,768]{2,1,0:T(8,128)(2,1)} %bitcast.967, bf16[1,96,768]{2,1,0:T(8,128)(2,1)} %bitcast.969, bf16[1,96,768]{2,1,0:T(8,128)(2,1)} %bitcast.971, bf16[4,96,768]{2,1,0:T(8,128)(2,1)} %collective-permute-done.20.refs_4_), custom_call_target="tpu_custom_call" | custom-call | tf_op jit(solution)/shard_map/pallas_call | solution.py:63
  386.4 6.8 collective-permute-done.24
  393.2 6.5 collective-permute-done.25
  421.7 145.3 %shard_map.198 = bf16[64,48,768]{2,1,0:T(8,128)(2,1)} custom-call(s32[64]{0:T(128)} %stack.629.spots_ref, bf16[16,48,768]{2,1,0:T(8,128)(2,1)} %bitcast.901, bf16[16,48,768]{2,1,0:T(8,128)(2,1)} %bitcast.918, bf16[16,48,768]{2,1,0:T(8,128)(2,1)} %bitcast.919, bf16[16,48,768]{2,1,0:T(8,128)(2,1)} %bitcast.920), custom_call_target="tpu_custom_call" | custom-call | tf_op jit(solution)/shard_map/pallas_call | solution.py:63
  567.0 4.3 fusion.347
  578.8 109.0 %shard_map.199 = bf16[8,192,1152]{2,1,0:T(8,128)(2,1)} custom-call(s32[8]{0:T(128)} %stack.556.spots_ref, bf16[1,192,1152]{2,1,0:T(8,128)(2,1)} %copy-done.63, bf16[1,192,1152]{2,1,0:T(8,128)(2,1)} %bitcast.137.refs_1_, bf16[1,192,1152]{2,1,0:T(8,128)(2,1)} %bitcast.138.refs_2_, bf16[1,192,1152]{2,1,0:T(8,128)(2,1)} %bitcast.139.refs_3_, ...), custom_call_target="tpu_custom_call" | custom-call | tf_op jit(solution)/shard_map/pallas_call | solution.py:63
  703.3 37.6 %shard_map.200 = bf16[8,96,768]{2,1,0:T(8,128)(2,1)} custom-call(s32[8]{0:T(128)} %stack.556.spots_ref, bf16[1,96,768]{2,1,0:T(8,128)(2,1)} %copy-done.101, bf16[1,96,768]{2,1,0:T(8,128)(2,1)} %bitcast.961, bf16[1,96,768]{2,1,0:T(8,128)(2,1)} %bitcast.963, bf16[1,96,768]{2,1,0:T(8,128)(2,1)} %bitcast.965, bf16[4,96,768]{2,1,0:T(8,128)(2,1)} %collective-permute-done.55.refs_4_), custom_call_target="tpu_custom_call" | custom-call | tf_op jit(solution)/shard_map/pallas_call | solution.py:63
  779.1 6.2 collective-permute-done.59
  813.7 6.1 collective-permute-done.65
  906.0 6.7 collective-permute-done.85
  912.7 6.5 collective-permute-done.86
  939.4 4.2 add_convert_fusion
  954.8 27.7 %collective-permute-done.159 = bf16[4,96,768]{2,1,0:T(8,128)(2,1)S(1)} collective-permute-done((bf16[4,96,768]{2,1,0:T(8,128)(2,1)S(1)}, bf16[4,96,768]{2,1,0:T(8,128)(2,1)S(1)}, u32[]{:S(2)}, u32[]{:S(2)}) %collective-permute-start.159) | collective-permute-done | bytes 589856 | tf_op jit(solution)/shard_map/ppermute | solution.py:105
  984.0 9.2 collective-permute-done.91
  997.8 9.5 collective-permute-done.143
  1017.2 7.9 collective-permute-done.161
  1044.5 14.8 fusion.324
  1059.4 5.7 fusion.7
  1065.0 8.3 reshape.1534
  1073.3 7.3 constant_dynamic-slice_fusion.8
  1088.3 5.0 add_reduce_fusion.2
  1110.2 10.3 collective-permute-done.98
  1136.5 7.1 collective-permute-done.112
  1152.8 8.4 collective-permute-done.192
  1161.3 6.0 collective-permute-done.178
  1167.3 5.4 collective-permute-done.179
  1172.8 4.3 collective-permute-done.180
  1182.7 5.9 collective-permute-done.182
  1189.5 5.3 collective-permute-done.183
  1201.1 19.7 %shard_map.202 = bf16[8,48,768]{2,1,0:T(8,128)(2,1)} custom-call(s32[8]{0:T(128)} %stack.671.spots_ref, bf16[8,48,768]{2,1,0:T(8,128)(2,1)} %copy-done.165), custom_call_target="tpu_custom_call" | custom-call | tf_op jit(solution)/shard_map/pallas_call | solution.py:63
  1239.7 4.4 collective-permute-start.138
  1251.6 5.3 collective-permute-done.137
  1263.4 4.5 collective-permute-done.116
  1272.2 16.7 %collective-permute-done.127 = bf16[4,192,384]{2,1,0:T(8,128)(2,1)S(1)} collective-permute-done((bf16[4,192,384]{2,1,0:T(8,128)(2,1)S(1)}, bf16[4,192,384]{2,1,0:T(8,128)(2,1)S(1)}, u32[]{:S(2)}, u32[]{:S(2)}) %collective-permute-start.127) | collective-permute-done | bytes 589856 | tf_op jit(solution)/shard_map/ppermute | solution.py:105
  1297.9 5.2 collective-permute-done.153
  1320.3 27.0 %collective-permute-done.185 = bf16[48,6144]{1,0:T(8,128)(2,1)S(1)} collective-permute-done((bf16[48,6144]{1,0:T(8,128)(2,1)}, bf16[48,6144]{1,0:T(8,128)(2,1)S(1)}, u32[]{:S(2)}, u32[]{:S(2)}) %collective-permute-start.185) | collective-permute-done | bytes 589856 | tf_op jit(solution)/shard_map/ppermute | solution.py:105
  1354.1 9.3 collective-permute-done.140
  1378.8 9.6 collective-permute-done.188
  1390.4 4.2 collective-permute-done.167
  1394.6 5.6 collective-permute-done.168
  1400.2 4.3 collective-permute-done.169
  1408.9 7.0 collective-permute-done.171
  1415.9 6.1 collective-permute-done.172
  1422.3 5.0 collective-permute-done.173
  1428.9 19.7 %shard_map.201 = bf16[8,48,768]{2,1,0:T(8,128)(2,1)} custom-call(s32[8]{0:T(128)} %stack.671.spots_ref, bf16[8,48,768]{2,1,0:T(8,128)(2,1)} %copy-done.164), custom_call_target="tpu_custom_call" | custom-call | tf_op jit(solution)/shard_map/pallas_call | solution.py:63
  1467.9 8.9 collective-permute-done.121
  1494.2 7.7 collective-permute-done.108
  1543.5 4.4 maximum_convert_fusion.1
  1550.2 4.4 maximum_convert_fusion
  (1399 shorter events, 622.0 us)
Async XLA Ops:
  7.3 95.4 %collective-permute-start.12 = (bf16[192,384]{1,0:T(8,128)(2,1)}, bf16[192,384]{1,0:T(8,128)(2,1)S(1)}, u32[]{:S(2)}, u32[]{:S(2)}) collective-permute-start(bf16[192,384]{1,0:T(8,128)(2,1)} %get-tuple-element.213), channel_id=1, source_target_pairs={{0,24},{1,25},{2,26},{3,27},{4,28},{5,29},{6,30},{7,31},{8,0},{9,1... | collective-permute-start | bytes 442376 | tf_op jit(solution)/shard_map/ppermute | solution.py:105
  12.4 92.3 %collective-permute-start.13 = (bf16[192,384]{1,0:T(8,128)(2,1)}, bf16[192,384]{1,0:T(8,128)(2,1)S(1)}, u32[]{:S(2)}, u32[]{:S(2)}) collective-permute-start(bf16[192,384]{1,0:T(8,128)(2,1)} %get-tuple-element.213), channel_id=1, source_target_pairs={{0,16},{1,17},{2,18},{3,19},{4,20},{5,21},{6,22},{7,23},{8,24},{9,... | collective-permute-start | bytes 442376 | tf_op jit(solution)/shard_map/ppermute | solution.py:105
  12.4 117.9 %collective-permute-start.14 = (bf16[192,384]{1,0:T(8,128)(2,1)}, bf16[192,384]{1,0:T(8,128)(2,1)S(1)}, u32[]{:S(2)}, u32[]{:S(2)}) collective-permute-start(bf16[192,384]{1,0:T(8,128)(2,1)} %get-tuple-element.213), channel_id=1, source_target_pairs={{0,8},{1,9},{2,10},{3,11},{4,12},{5,13},{6,14},{7,15},{8,16},{9,17... | collective-permute-start | bytes 442376 | tf_op jit(solution)/shard_map/ppermute | solution.py:105
  14.1 56.1 %collective-permute-start = (bf16[2,64,384]{2,1,0:T(8,128)(2,1)}, bf16[2,64,384]{2,1,0:T(8,128)(2,1)S(1)}, u32[]{:S(2)}, u32[]{:S(2)}) collective-permute-start(bf16[2,64,384]{2,1,0:T(8,128)(2,1)} %get-tuple-element.283), channel_id=1, source_target_pairs={{0,1},{1,0},{2,3},{3,2},{4,5},{5,4},{6,7},{7,6},{8,9},{9,8},{10,11... | collective-permute-start | bytes 294920 | tf_op jit(solution)/shard_map/ppermute | solution.py:105
  16.4 55.5 %collective-permute-start.30 = (bf16[2,48,768]{2,1,0:T(8,128)(2,1)}, bf16[2,48,768]{2,1,0:T(8,128)(2,1)}, u32[]{:S(2)}, u32[]{:S(2)}) collective-permute-start(bf16[2,48,768]{2,1,0:T(8,128)(2,1)} %get-tuple-element.168), channel_id=1, source_target_pairs={{0,8},{1,9},{2,10},{3,11},{4,12},{5,13},{6,14},{7,15},{8,16},{9,17... | collective-permute-start | bytes 442376 | tf_op jit(solution)/shard_map/ppermute | solution.py:105
  70.2 50.9 %collective-permute-start.17 = (bf16[96,768]{1,0:T(8,128)(2,1)S(1)}, bf16[96,768]{1,0:T(8,128)(2,1)S(1)}, u32[]{:S(2)}, u32[]{:S(2)}) collective-permute-start(bf16[96,768]{1,0:T(8,128)(2,1)S(1)} %bitcast.905), channel_id=1, source_target_pairs={{0,24},{1,25},{2,26},{3,27},{4,28},{5,29},{6,30},{7,31},{8,0},{9,1... | collective-permute-start | bytes 442376 | tf_op jit(solution)/shard_map/ppermute | solution.py:105
  152.4 113.5 %collective-permute-start.15 = (bf16[4,192,384]{2,1,0:T(8,128)(2,1)}, bf16[4,192,384]{2,1,0:T(8,128)(2,1)}, u32[]{:S(2)}, u32[]{:S(2)}) collective-permute-start(bf16[4,192,384]{2,1,0:T(8,128)(2,1)} %pad_maximum_fusion.12), channel_id=1, source_target_pairs={{0,4},{1,5},{2,6},{3,7},{4,0},{5,1},{6,2},{7,3},{8,12},{9,13},{10,... | collective-permute-start | bytes 1769480 | tf_op jit(solution)/shard_map/ppermute | solution.py:105
  154.5 71.3 %collective-permute-start.9 = (bf16[4,192,384]{2,1,0:T(8,128)(2,1)}, bf16[4,192,384]{2,1,0:T(8,128)(2,1)}, u32[]{:S(2)}, u32[]{:S(2)}) collective-permute-start(bf16[4,192,384]{2,1,0:T(8,128)(2,1)} %pad_maximum_fusion.11), channel_id=1, source_target_pairs={{0,4},{1,5},{2,6},{3,7},{4,0},{5,1},{6,2},{7,3},{8,12},{9,13},{10,... | collective-permute-start | bytes 1769480 | tf_op jit(solution)/shard_map/ppermute | solution.py:105
  156.1 147.5 %collective-permute-start.20 = (bf16[4,96,768]{2,1,0:T(8,128)(2,1)}, bf16[4,96,768]{2,1,0:T(8,128)(2,1)}, u32[]{:S(2)}, u32[]{:S(2)}) collective-permute-start(bf16[4,96,768]{2,1,0:T(8,128)(2,1)} %pad_maximum_fusion.13), channel_id=1, source_target_pairs={{0,4},{1,5},{2,6},{3,7},{4,0},{5,1},{6,2},{7,3},{8,12},{9,13},{10,... | collective-permute-start | bytes 1769480 | tf_op jit(solution)/shard_map/ppermute | solution.py:105
  213.8 128.9 %collective-permute-start.10 = (bf16[1536,384]{1,0:T(8,128)(2,1)}, bf16[1536,384]{1,0:T(8,128)(2,1)S(1)}, u32[]{:S(2)}, u32[]{:S(2)}) collective-permute-start(bf16[1536,384]{1,0:T(8,128)(2,1)} %bitcast.868), channel_id=1, source_target_pairs={{0,1},{1,0},{2,3},{3,2},{4,5},{5,4},{6,7},{7,6},{8,9},{9,8},{10,11... | collective-permute-start | bytes 3538952 | tf_op jit(solution)/shard_map/ppermute | solution.py:105
  220.6 44.0 %collective-permute-start.72 = (bf16[32,1536]{1,0:T(8,128)(2,1)}, bf16[32,1536]{1,0:T(8,128)(2,1)S(1)}, u32[]{:S(2)}, u32[]{:S(2)}) collective-permute-start(bf16[32,1536]{1,0:T(8,128)(2,1)} %slice_bitcast_fusion.16), channel_id=1, source_target_pairs={{0,16},{1,17},{2,18},{3,19},{4,20},{5,21},{6,22},{7,23},{8,24},{9,... | collective-permute-start | bytes 294920 | tf_op jit(solution)/shard_map/ppermute | solution.py:105
  225.8 152.8 %collective-permute-start.45 = (bf16[192,1152]{1,0:T(8,128)(2,1)}, bf16[192,1152]{1,0:T(8,128)(2,1)}, u32[]{:S(2)}, u32[]{:S(2)}) collective-permute-start(bf16[192,1152]{1,0:T(8,128)(2,1)} %get-tuple-element.260), channel_id=1, source_target_pairs={{0,24},{1,25},{2,26},{3,27},{4,28},{5,29},{6,30},{7,31},{8,0},{9,1... | collective-permute-start | bytes 1327112 | tf_op jit(solution)/shard_map/ppermute | solution.py:105
  264.6 81.5 %collective-permute-start.11 = (bf16[1536,384]{1,0:T(8,128)(2,1)}, bf16[1536,384]{1,0:T(8,128)(2,1)}, u32[]{:S(2)}, u32[]{:S(2)}) collective-permute-start(bf16[1536,384]{1,0:T(8,128)(2,1)} %bitcast.874), channel_id=1, source_target_pairs={{0,1},{1,0},{2,3},{3,2},{4,5},{5,4},{6,7},{7,6},{8,9},{9,8},{10,11... | collective-permute-start | bytes 3538952 | tf_op jit(solution)/shard_map/ppermute | solution.py:105
  265.8 114.3 %collective-permute-start.46 = (bf16[192,1152]{1,0:T(8,128)(2,1)}, bf16[192,1152]{1,0:T(8,128)(2,1)}, u32[]{:S(2)}, u32[]{:S(2)}) collective-permute-start(bf16[192,1152]{1,0:T(8,128)(2,1)} %get-tuple-element.260), channel_id=1, source_target_pairs={{0,16},{1,17},{2,18},{3,19},{4,20},{5,21},{6,22},{7,23},{8,24},{9,... | collective-permute-start | bytes 1327112 | tf_op jit(solution)/shard_map/ppermute | solution.py:105
  303.6 77.1 %collective-permute-start.47 = (bf16[192,1152]{1,0:T(8,128)(2,1)}, bf16[192,1152]{1,0:T(8,128)(2,1)}, u32[]{:S(2)}, u32[]{:S(2)}) collective-permute-start(bf16[192,1152]{1,0:T(8,128)(2,1)} %get-tuple-element.260), channel_id=1, source_target_pairs={{0,8},{1,9},{2,10},{3,11},{4,12},{5,13},{6,14},{7,15},{8,16},{9,17... | collective-permute-start | bytes 1327112 | tf_op jit(solution)/shard_map/ppermute | solution.py:105
  342.8 42.3 %collective-permute-start.37 = (bf16[8,2,48,768]{3,2,1,0:T(8,128)(2,1)}, bf16[8,2,48,768]{3,2,1,0:T(8,128)(2,1)S(1)}, u32[]{:S(2)}, u32[]{:S(2)}) collective-permute-start(bf16[8,2,48,768]{3,2,1,0:T(8,128)(2,1)} %copy-done.96), channel_id=1, source_target_pairs={{0,2},{1,3},{2,0},{3,1},{4,6},{5,7},{6,4},{7,5},{8,10},{9,11},{10,... | collective-permute-start | bytes 3538952 | tf_op jit(solution)/shard_map/ppermute | solution.py:105
  378.1 41.1 %collective-permute-start.38 = (bf16[8,2,48,768]{3,2,1,0:T(8,128)(2,1)S(1)}, bf16[8,2,48,768]{3,2,1,0:T(8,128)(2,1)S(1)}, u32[]{:S(2)}, u32[]{:S(2)}) collective-permute-start(bf16[8,2,48,768]{3,2,1,0:T(8,128)(2,1)S(1)} %copy-done.97), channel_id=1, source_target_pairs={{0,1},{1,0},{2,3},{3,2},{4,5},{5,4},{6,7},{7,6},{8,9},{9,8},{10,11... | collective-permute-start | bytes 3538952 | tf_op jit(solution)/shard_map/ppermute | solution.py:105
  378.6 323.9 %collective-permute-start.55 = (bf16[4,96,768]{2,1,0:T(8,128)(2,1)}, bf16[4,96,768]{2,1,0:T(8,128)(2,1)}, u32[]{:S(2)}, u32[]{:S(2)}) collective-permute-start(bf16[4,96,768]{2,1,0:T(8,128)(2,1)} %pad_maximum_fusion.14), channel_id=1, source_target_pairs={{0,4},{1,5},{2,6},{3,7},{4,0},{5,1},{6,2},{7,3},{8,12},{9,13},{10,... | collective-permute-start | bytes 1769480 | tf_op jit(solution)/shard_map/ppermute | solution.py:105
  380.1 196.3 %collective-permute-start.74 = (bf16[32,1536]{1,0:T(8,128)(2,1)}, bf16[32,1536]{1,0:T(8,128)(2,1)S(1)}, u32[]{:S(2)}, u32[]{:S(2)}) collective-permute-start(bf16[32,1536]{1,0:T(8,128)(2,1)} %slice_bitcast_fusion.16), channel_id=1, source_target_pairs={{0,4},{1,5},{2,6},{3,7},{4,0},{5,1},{6,2},{7,3},{8,12},{9,13},{10,... | collective-permute-start | bytes 294920 | tf_op jit(solution)/shard_map/ppermute | solution.py:105
  385.0 35.6 %collective-permute-start.39 = (bf16[8,2,48,768]{3,2,1,0:T(8,128)(2,1)S(1)}, bf16[8,2,48,768]{3,2,1,0:T(8,128)(2,1)S(1)}, u32[]{:S(2)}, u32[]{:S(2)}) collective-permute-start(bf16[8,2,48,768]{3,2,1,0:T(8,128)(2,1)S(1)} %collective-permute-done.37), channel_id=1, source_target_pairs={{0,1},{1,0},{2,3},{3,2},{4,5},{5,4},{6,7},{7,6},{8,9},{9,8},{10,11... | collective-permute-start | bytes 3538952 | tf_op jit(solution)/shard_map/ppermute | solution.py:105
  419.1 683.3 %collective-permute-start.101 = (bf16[64,1536]{1,0:T(8,128)(2,1)}, bf16[64,1536]{1,0:T(8,128)(2,1)}, u32[]{:S(2)}, u32[]{:S(2)}) collective-permute-start(bf16[64,1536]{1,0:T(8,128)(2,1)} %get-tuple-element.263), channel_id=1, source_target_pairs={{0,1},{1,0},{2,3},{3,2},{4,5},{5,4},{6,7},{7,6},{8,9},{9,8},{10,11... | collective-permute-start | bytes 589832 | tf_op jit(solution)/shard_map/ppermute | solution.py:105
  419.2 159.0 %collective-permute-start.75 = (bf16[32,1536]{1,0:T(8,128)(2,1)S(1)}, bf16[32,1536]{1,0:T(8,128)(2,1)S(1)}, u32[]{:S(2)}, u32[]{:S(2)}) collective-permute-start(bf16[32,1536]{1,0:T(8,128)(2,1)S(1)} %collective-permute-done.71), channel_id=1, source_target_pairs={{0,4},{1,5},{2,6},{3,7},{4,0},{5,1},{6,2},{7,3},{8,12},{9,13},{10,... | collective-permute-start | bytes 294920 | tf_op jit(solution)/shard_map/ppermute | solution.py:105
  420.7 158.2 %collective-permute-start.48 = (bf16[4,192,1152]{2,1,0:T(8,128)(2,1)}, bf16[4,192,1152]{2,1,0:T(8,128)(2,1)}, u32[]{:S(2)}, u32[]{:S(2)}) collective-permute-start(bf16[4,192,1152]{2,1,0:T(8,128)(2,1)} %pad_maximum_fusion.7), channel_id=1, source_target_pairs={{0,4},{1,5},{2,6},{3,7},{4,0},{5,1},{6,2},{7,3},{8,12},{9,13},{10,... | collective-permute-start | bytes 5308424 | tf_op jit(solution)/shard_map/ppermute | solution.py:105
  576.4 111.5 %collective-permute-start.40 = (bf16[128,1536]{1,0:T(8,128)(2,1)S(1)}, bf16[128,1536]{1,0:T(8,128)(2,1)S(1)}, u32[]{:S(2)}, u32[]{:S(2)}) collective-permute-start(bf16[128,1536]{1,0:T(8,128)(2,1)S(1)} %slice.732), channel_id=1, source_target_pairs={{0,4},{1,5},{2,6},{3,7},{4,0},{5,1},{6,2},{7,3},{8,12},{9,13},{10,... | collective-permute-start | bytes 1179656 | tf_op jit(solution)/shard_map/ppermute | solution.py:105
  699.3 42.0 %collective-permute-start.49 = (bf16[1536,384]{1,0:T(8,128)(2,1)S(1)}, bf16[1536,384]{1,0:T(8,128)(2,1)}, u32[]{:S(2)}, u32[]{:S(2)}) collective-permute-start(bf16[1536,384]{1,0:T(8,128)(2,1)S(1)} %bitcast.836), channel_id=1, source_target_pairs={{0,1},{1,0},{2,3},{3,2},{4,5},{5,4},{6,7},{7,6},{8,9},{9,8},{10,11... | collective-permute-start | bytes 3538952 | tf_op jit(solution)/shard_map/ppermute | solution.py:105
  699.3 46.8 %collective-permute-start.50 = (bf16[1536,384]{1,0:T(8,128)(2,1)}, bf16[1536,384]{1,0:T(8,128)(2,1)}, u32[]{:S(2)}, u32[]{:S(2)}) collective-permute-start(bf16[1536,384]{1,0:T(8,128)(2,1)} %bitcast.142), channel_id=1, source_target_pairs={{0,1},{1,0},{2,3},{3,2},{4,5},{5,4},{6,7},{7,6},{8,9},{9,8},{10,11... | collective-permute-start | bytes 3538952 | tf_op jit(solution)/shard_map/ppermute | solution.py:105
  700.7 40.2 %collective-permute-start.44 = (bf16[32,1536]{1,0:T(8,128)(2,1)S(1)}, bf16[32,1536]{1,0:T(8,128)(2,1)S(1)}, u32[]{:S(2)}, u32[]{:S(2)}) collective-permute-start(bf16[32,1536]{1,0:T(8,128)(2,1)S(1)} %fusion.202), channel_id=1, source_target_pairs={{0,2},{1,3},{2,0},{3,1},{4,6},{5,7},{6,4},{7,5},{8,10},{9,11},{10,... | collective-permute-start | bytes 294920 | tf_op jit(solution)/shard_map/ppermute | solution.py:105
  702.5 65.5 %collective-permute-start.77 = (bf16[32,1536]{1,0:T(8,128)(2,1)}, bf16[32,1536]{1,0:T(8,128)(2,1)}, u32[]{:S(2)}, u32[]{:S(2)}) collective-permute-start(bf16[32,1536]{1,0:T(8,128)(2,1)} %collective-permute-done.73), channel_id=1, source_target_pairs={{0,4},{1,5},{2,6},{3,7},{4,0},{5,1},{6,2},{7,3},{8,12},{9,13},{10,... | collective-permute-start | bytes 294920 | tf_op jit(solution)/shard_map/ppermute | solution.py:105
  775.3 114.3 %collective-permute-start.109 = (bf16[64,1536]{1,0:T(8,128)(2,1)}, bf16[64,1536]{1,0:T(8,128)(2,1)}, u32[]{:S(2)}, u32[]{:S(2)}) collective-permute-start(bf16[64,1536]{1,0:T(8,128)(2,1)} %pad_maximum_fusion.16), channel_id=1, source_target_pairs={{0,1},{1,0},{2,3},{3,2},{4,5},{5,4},{6,7},{7,6},{8,9},{9,8},{10,11... | collective-permute-start | bytes 589832 | tf_op jit(solution)/shard_map/ppermute | solution.py:105
  827.6 167.1 %collective-permute-start.134 = (bf16[256,384]{1,0:T(8,128)(2,1)}, bf16[256,384]{1,0:T(8,128)(2,1)}, u32[]{:S(2)}, u32[]{:S(2)}) collective-permute-start(bf16[256,384]{1,0:T(8,128)(2,1)} %bitcast.143), channel_id=1, source_target_pairs={{0,1},{1,0},{2,3},{3,2},{4,5},{5,4},{6,7},{7,6},{8,9},{9,8},{10,11... | collective-permute-start | bytes 589832 | tf_op jit(solution)/shard_map/ppermute | solution.py:105
  831.1 69.6 %collective-permute-start.157 = (bf16[64,768]{1,0:T(8,128)(2,1)}, bf16[64,768]{1,0:T(8,128)(2,1)}, u32[]{:S(2)}, u32[]{:S(2)}) collective-permute-start(bf16[64,768]{1,0:T(8,128)(2,1)} %maximum_select_fusion.43), channel_id=1, source_target_pairs={{0,1},{1,0},{2,3},{3,2},{4,5},{5,4},{6,7},{7,6},{8,9},{9,8},{10,11... | collective-permute-start | bytes 294920 | tf_op jit(solution)/shard_map/ppermute | solution.py:105
  889.5 34.3 %collective-permute-start.141 = (bf16[256,1536]{1,0:T(8,128)(2,1)}, bf16[256,1536]{1,0:T(8,128)(2,1)}, u32[]{:S(2)}, u32[]{:S(2)}) collective-permute-start(bf16[256,1536]{1,0:T(8,128)(2,1)} %get-tuple-element.195), channel_id=1, source_target_pairs={{0,1},{1,0},{2,3},{3,2},{4,5},{5,4},{6,7},{7,6},{8,9},{9,8},{10,11... | collective-permute-start | bytes 2359304 | tf_op jit(solution)/shard_map/ppermute | solution.py:105
  900.7 49.1 %collective-permute-start.176 = (bf16[8,2,48,768]{3,2,0,1:T(8,128)(2,1)S(1)}, bf16[8,2,48,768]{3,2,0,1:T(8,128)(2,1)S(1)}, u32[]{:S(2)}, u32[]{:S(2)}) collective-permute-start(bf16[8,2,48,768]{3,2,0,1:T(8,128)(2,1)S(1)} %bitcast.922), channel_id=1, source_target_pairs={{0,1},{1,0},{2,3},{3,2},{4,5},{5,4},{6,7},{7,6},{8,9},{9,8},{10,11... | collective-permute-start | bytes 3538952 | tf_op jit(solution)/shard_map/ppermute | solution.py:105
  939.4 55.4 %collective-permute-start.133 = (bf16[256,1536]{1,0:T(8,128)(2,1)S(1)}, bf16[256,1536]{1,0:T(8,128)(2,1)S(1)}, u32[]{:S(2)}, u32[]{:S(2)}) collective-permute-start(bf16[256,1536]{1,0:T(8,128)(2,1)S(1)} %copy-done.162), channel_id=1, source_target_pairs={{0,1},{1,0},{2,3},{3,2},{4,5},{5,4},{6,7},{7,6},{8,9},{9,8},{10,11... | collective-permute-start | bytes 2359304 | tf_op jit(solution)/shard_map/ppermute | solution.py:105
  949.9 76.9 %collective-permute-start.111 = (bf16[4,192,512]{2,1,0:T(8,128)(2,1)S(1)}, bf16[4,192,512]{2,1,0:T(8,128)(2,1)S(1)}, u32[]{:S(2)}, u32[]{:S(2)}) collective-permute-start(bf16[4,192,512]{2,1,0:T(8,128)(2,1)S(1)} %dynamic-slice_bitcast_fusion.3), channel_id=1, source_target_pairs={{0,4},{1,5},{2,6},{3,7},{4,0},{5,1},{6,2},{7,3},{8,12},{9,13},{10,... | collective-permute-start | bytes 2359304 | tf_op jit(solution)/shard_map/ppermute | solution.py:105
  952.4 30.1 %collective-permute-start.159 = (bf16[4,96,768]{2,1,0:T(8,128)(2,1)S(1)}, bf16[4,96,768]{2,1,0:T(8,128)(2,1)S(1)}, u32[]{:S(2)}, u32[]{:S(2)}) collective-permute-start(bf16[4,96,768]{2,1,0:T(8,128)(2,1)S(1)} %dynamic-slice_bitcast_fusion.9), channel_id=1, source_target_pairs={{0,4},{1,5},{2,6},{3,7},{4,0},{5,1},{6,2},{7,3},{8,12},{9,13},{10,... | collective-permute-start | bytes 1769480 | tf_op jit(solution)/shard_map/ppermute | solution.py:105
  1017.2 106.4 %collective-permute-start.149 = (bf16[64,768]{1,0:T(8,128)(2,1)}, bf16[64,768]{1,0:T(8,128)(2,1)}, u32[]{:S(2)}, u32[]{:S(2)}) collective-permute-start(bf16[64,768]{1,0:T(8,128)(2,1)} %maximum_select_fusion.42), channel_id=1, source_target_pairs={{0,1},{1,0},{2,3},{3,2},{4,5},{5,4},{6,7},{7,6},{8,9},{9,8},{10,11... | collective-permute-start | bytes 294920 | tf_op jit(solution)/shard_map/ppermute | solution.py:105
  1025.1 75.3 %collective-permute-start.146 = (bf16[192,384]{1,0:T(8,128)(2,1)}, bf16[192,384]{1,0:T(8,128)(2,1)}, u32[]{:S(2)}, u32[]{:S(2)}) collective-permute-start(bf16[192,384]{1,0:T(8,128)(2,1)} %get-tuple-element.258), channel_id=1, source_target_pairs={{0,24},{1,25},{2,26},{3,27},{4,28},{5,29},{6,30},{7,31},{8,0},{9,1... | collective-permute-start | bytes 442376 | tf_op jit(solution)/shard_map/ppermute | solution.py:105
  1025.3 75.2 %collective-permute-start.145 = (bf16[192,384]{1,0:T(8,128)(2,1)}, bf16[192,384]{1,0:T(8,128)(2,1)}, u32[]{:S(2)}, u32[]{:S(2)}) collective-permute-start(bf16[192,384]{1,0:T(8,128)(2,1)} %get-tuple-element.259), channel_id=1, source_target_pairs={{0,16},{1,17},{2,18},{3,19},{4,20},{5,21},{6,22},{7,23},{8,24},{9,... | collective-permute-start | bytes 442376 | tf_op jit(solution)/shard_map/ppermute | solution.py:105
  1031.4 69.6 %collective-permute-start.144 = (bf16[192,384]{1,0:T(8,128)(2,1)}, bf16[192,384]{1,0:T(8,128)(2,1)}, u32[]{:S(2)}, u32[]{:S(2)}) collective-permute-start(bf16[192,384]{1,0:T(8,128)(2,1)} %get-tuple-element.257), channel_id=1, source_target_pairs={{0,8},{1,9},{2,10},{3,11},{4,12},{5,13},{6,14},{7,15},{8,16},{9,17... | collective-permute-start | bytes 442376 | tf_op jit(solution)/shard_map/ppermute | solution.py:105
  1100.5 44.3 %collective-permute-start.125 = (bf16[256,1536]{1,0:T(8,128)(2,1)}, bf16[256,1536]{1,0:T(8,128)(2,1)}, u32[]{:S(2)}, u32[]{:S(2)}) collective-permute-start(bf16[256,1536]{1,0:T(8,128)(2,1)} %get-tuple-element.191), channel_id=1, source_target_pairs={{0,1},{1,0},{2,3},{3,2},{4,5},{5,4},{6,7},{7,6},{8,9},{9,8},{10,11... | collective-permute-start | bytes 2359304 | tf_op jit(solution)/shard_map/ppermute | solution.py:105
  1102.4 47.8 %collective-permute-start.177 = (bf16[8,48,768]{2,1,0:T(8,128)(2,1)}, bf16[8,48,768]{2,1,0:T(8,128)(2,1)}, u32[]{:S(2)}, u32[]{:S(2)}) collective-permute-start(bf16[8,48,768]{2,1,0:T(8,128)(2,1)} %dynamic-slice_bitcast_fusion.7), channel_id=1, source_target_pairs={{0,2},{1,3},{2,0},{3,1},{4,6},{5,7},{6,4},{7,5},{8,10},{9,11},{10,... | collective-permute-start | bytes 1769480 | tf_op jit(solution)/shard_map/ppermute | solution.py:105
  1103.7 31.8 %collective-permute-start.114 = (bf16[192,512]{1,0:T(8,128)(2,1)}, bf16[192,512]{1,0:T(8,128)(2,1)}, u32[]{:S(2)}, u32[]{:S(2)}) collective-permute-start(bf16[192,512]{1,0:T(8,128)(2,1)} %get-tuple-element.224), channel_id=1, source_target_pairs={{0,24},{1,25},{2,26},{3,27},{4,28},{5,29},{6,30},{7,31},{8,0},{9,1... | collective-permute-start | bytes 589832 | tf_op jit(solution)/shard_map/ppermute | solution.py:105
  1135.5 155.4 %collective-permute-start.118 = (bf16[256,384]{1,0:T(8,128)(2,1)}, bf16[256,384]{1,0:T(8,128)(2,1)}, u32[]{:S(2)}, u32[]{:S(2)}) collective-permute-start(bf16[256,384]{1,0:T(8,128)(2,1)} %bitcast.39), channel_id=1, source_target_pairs={{0,1},{1,0},{2,3},{3,2},{4,5},{5,4},{6,7},{7,6},{8,9},{9,8},{10,11... | collective-permute-start | bytes 589832 | tf_op jit(solution)/shard_map/ppermute | solution.py:105
  1136.5 111.3 %collective-permute-start.165 = (bf16[8,2,48,768]{3,2,0,1:T(8,128)(2,1)}, bf16[8,2,48,768]{3,2,0,1:T(8,128)(2,1)}, u32[]{:S(2)}, u32[]{:S(2)}) collective-permute-start(bf16[8,2,48,768]{3,2,0,1:T(8,128)(2,1)} %bitcast.814), channel_id=1, source_target_pairs={{0,1},{1,0},{2,3},{3,2},{4,5},{5,4},{6,7},{7,6},{8,9},{9,8},{10,11... | collective-permute-start | bytes 3538952 | tf_op jit(solution)/shard_map/ppermute | solution.py:105
  1145.6 92.7 %collective-permute-start.135 = (bf16[4,192,384]{2,1,0:T(8,128)(2,1)}, bf16[4,192,384]{2,1,0:T(8,128)(2,1)}, u32[]{:S(2)}, u32[]{:S(2)}) collective-permute-start(bf16[4,192,384]{2,1,0:T(8,128)(2,1)} %dynamic-slice_bitcast_fusion.12), channel_id=1, source_target_pairs={{0,4},{1,5},{2,6},{3,7},{4,0},{5,1},{6,2},{7,3},{8,12},{9,13},{10,... | collective-permute-start | bytes 1769480 | tf_op jit(solution)/shard_map/ppermute | solution.py:105
  1150.2 74.9 %collective-permute-start.164 = (bf16[2,96,768]{2,1,0:T(8,128)(2,1)}, bf16[2,96,768]{2,1,0:T(8,128)(2,1)}, u32[]{:S(2)}, u32[]{:S(2)}) collective-permute-start(bf16[2,96,768]{2,1,0:T(8,128)(2,1)} %maximum_select_fusion.38), channel_id=1, source_target_pairs={{0,2},{1,3},{2,0},{3,1},{4,6},{5,7},{6,4},{7,5},{8,10},{9,11},{10,... | collective-permute-start | bytes 884744 | tf_op jit(solution)/shard_map/ppermute | solution.py:105
  1200.3 28.9 %collective-permute-start.115 = (bf16[192,512]{1,0:T(8,128)(2,1)S(1)}, bf16[192,512]{1,0:T(8,128)(2,1)}, u32[]{:S(2)}, u32[]{:S(2)}) collective-permute-start(bf16[192,512]{1,0:T(8,128)(2,1)S(1)} %fusion.151), channel_id=1, source_target_pairs={{0,1},{1,0},{2,3},{3,2},{4,5},{5,4},{6,7},{7,6},{8,9},{9,8},{10,11... | collective-permute-start | bytes 589832 | tf_op jit(solution)/shard_map/ppermute | solution.py:105
  1251.6 39.4 %collective-permute-start.117 = (bf16[256,1536]{1,0:T(8,128)(2,1)S(1)}, bf16[256,1536]{1,0:T(8,128)(2,1)S(1)}, u32[]{:S(2)}, u32[]{:S(2)}) collective-permute-start(bf16[256,1536]{1,0:T(8,128)(2,1)S(1)} %copy-done.159), channel_id=1, source_target_pairs={{0,1},{1,0},{2,3},{3,2},{4,5},{5,4},{6,7},{7,6},{8,9},{9,8},{10,11... | collective-permute-start | bytes 2359304 | tf_op jit(solution)/shard_map/ppermute | solution.py:105
  1257.0 54.7 %collective-permute-start.103 = (bf16[4,192,512]{2,1,0:T(8,128)(2,1)}, bf16[4,192,512]{2,1,0:T(8,128)(2,1)}, u32[]{:S(2)}, u32[]{:S(2)}) collective-permute-start(bf16[4,192,512]{2,1,0:T(8,128)(2,1)} %dynamic-slice_bitcast_fusion.4), channel_id=1, source_target_pairs={{0,4},{1,5},{2,6},{3,7},{4,0},{5,1},{6,2},{7,3},{8,12},{9,13},{10,... | collective-permute-start | bytes 2359304 | tf_op jit(solution)/shard_map/ppermute | solution.py:105
  1267.9 37.1 %collective-permute-start.193 = (bf16[192,1536]{1,0:T(8,128)(2,1)S(1)}, bf16[192,1536]{1,0:T(8,128)(2,1)}, u32[]{:S(2)}, u32[]{:S(2)}) collective-permute-start(bf16[192,1536]{1,0:T(8,128)(2,1)S(1)} %fusion.84), channel_id=1, source_target_pairs={{0,2},{1,3},{2,0},{3,1},{4,6},{5,7},{6,4},{7,5},{8,10},{9,11},{10,... | collective-permute-start | bytes 1769480 | tf_op jit(solution)/shard_map/ppermute | solution.py:105
  1297.1 182.6 %collective-permute-start.96 = (bf16[1024,768]{1,0:T(8,128)(2,1)}, bf16[1024,768]{1,0:T(8,128)(2,1)}, u32[]{:S(2)}, u32[]{:S(2)}) collective-permute-start(bf16[1024,768]{1,0:T(8,128)(2,1)} %bitcast.900), channel_id=1, source_target_pairs={{0,2},{1,3},{2,0},{3,1},{4,6},{5,7},{6,4},{7,5},{8,10},{9,11},{10,... | collective-permute-start | bytes 4718600 | tf_op jit(solution)/shard_map/ppermute | solution.py:105
  1303.0 44.3 %collective-permute-start.185 = (bf16[48,6144]{1,0:T(8,128)(2,1)}, bf16[48,6144]{1,0:T(8,128)(2,1)S(1)}, u32[]{:S(2)}, u32[]{:S(2)}) collective-permute-start(bf16[48,6144]{1,0:T(8,128)(2,1)} %bitcast.984), channel_id=1, source_target_pairs={{0,2},{1,3},{2,0},{3,1},{4,6},{5,7},{6,4},{7,5},{8,10},{9,11},{10,... | collective-permute-start | bytes 1769480 | tf_op jit(solution)/shard_map/ppermute | solution.py:105
  1315.5 62.3 %collective-permute-start.166 = (bf16[8,48,768]{2,1,0:T(8,128)(2,1)S(1)}, bf16[8,48,768]{2,1,0:T(8,128)(2,1)S(1)}, u32[]{:S(2)}, u32[]{:S(2)}) collective-permute-start(bf16[8,48,768]{2,1,0:T(8,128)(2,1)S(1)} %copy-done.182), channel_id=1, source_target_pairs={{0,2},{1,3},{2,0},{3,1},{4,6},{5,7},{6,4},{7,5},{8,10},{9,11},{10,... | collective-permute-start | bytes 1769480 | tf_op jit(solution)/shard_map/ppermute | solution.py:105
  1316.3 47.2 %collective-permute-start.140 = (bf16[2,192,384]{2,1,0:T(8,128)(2,1)S(1)}, bf16[2,192,384]{2,1,0:T(8,128)(2,1)S(1)}, u32[]{:S(2)}, u32[]{:S(2)}) collective-permute-start(bf16[2,192,384]{2,1,0:T(8,128)(2,1)S(1)} %copy-done.191), channel_id=1, source_target_pairs={{0,2},{1,3},{2,0},{3,1},{4,6},{5,7},{6,4},{7,5},{8,10},{9,11},{10,... | collective-permute-start | bytes 884744 | tf_op jit(solution)/shard_map/ppermute | solution.py:105
  1319.2 33.0 %collective-permute-start.155 = (bf16[96,768]{1,0:T(8,128)(2,1)S(1)}, bf16[96,768]{1,0:T(8,128)(2,1)S(1)}, u32[]{:S(2)}, u32[]{:S(2)}) collective-permute-start(bf16[96,768]{1,0:T(8,128)(2,1)S(1)} %fusion.161), channel_id=1, source_target_pairs={{0,1},{1,0},{2,3},{3,2},{4,5},{5,4},{6,7},{7,6},{8,9},{9,8},{10,11... | collective-permute-start | bytes 442376 | tf_op jit(solution)/shard_map/ppermute | solution.py:105
  1373.0 86.7 %collective-permute-start.119 = (bf16[4,192,384]{2,1,0:T(8,128)(2,1)}, bf16[4,192,384]{2,1,0:T(8,128)(2,1)}, u32[]{:S(2)}, u32[]{:S(2)}) collective-permute-start(bf16[4,192,384]{2,1,0:T(8,128)(2,1)} %dynamic-slice_bitcast_fusion.14), channel_id=1, source_target_pairs={{0,4},{1,5},{2,6},{3,7},{4,0},{5,1},{6,2},{7,3},{8,12},{9,13},{10,... | collective-permute-start | bytes 1769480 | tf_op jit(solution)/shard_map/ppermute | solution.py:105
  1377.7 149.5 %collective-permute-start.194 = (bf16[2,192,1536]{2,1,0:T(8,128)(2,1)}, bf16[2,192,1536]{2,1,0:T(8,128)(2,1)}, u32[]{:S(2)}, u32[]{:S(2)}) collective-permute-start(bf16[2,192,1536]{2,1,0:T(8,128)(2,1)} %maximum_select_fusion.10), channel_id=1, source_target_pairs={{0,1},{1,0},{2,3},{3,2},{4,5},{5,4},{6,7},{7,6},{8,9},{9,8},{10,11... | collective-permute-start | bytes 3538952 | tf_op jit(solution)/shard_map/ppermute | solution.py:105
  1377.8 75.3 %collective-permute-start.156 = (bf16[2,96,768]{2,1,0:T(8,128)(2,1)}, bf16[2,96,768]{2,1,0:T(8,128)(2,1)S(1)}, u32[]{:S(2)}, u32[]{:S(2)}) collective-permute-start(bf16[2,96,768]{2,1,0:T(8,128)(2,1)} %maximum_select_fusion.36), channel_id=1, source_target_pairs={{0,2},{1,3},{2,0},{3,1},{4,6},{5,7},{6,4},{7,5},{8,10},{9,11},{10,... | collective-permute-start | bytes 884744 | tf_op jit(solution)/shard_map/ppermute | solution.py:105
  1427.3 30.4 %collective-permute-start.132 = (bf16[2,192,384]{2,1,0:T(8,128)(2,1)}, bf16[2,192,384]{2,1,0:T(8,128)(2,1)}, u32[]{:S(2)}, u32[]{:S(2)}) collective-permute-start(bf16[2,192,384]{2,1,0:T(8,128)(2,1)} %maximum_select_fusion.30), channel_id=1, source_target_pairs={{0,2},{1,3},{2,0},{3,1},{4,6},{5,7},{6,4},{7,5},{8,10},{9,11},{10,... | collective-permute-start | bytes 884744 | tf_op jit(solution)/shard_map/ppermute | solution.py:105
  1467.9 62.9 %collective-permute-start.186 = (bf16[2,48,6144]{2,1,0:T(8,128)(2,1)}, bf16[2,48,6144]{2,1,0:T(8,128)(2,1)}, u32[]{:S(2)}, u32[]{:S(2)}) collective-permute-start(bf16[2,48,6144]{2,1,0:T(8,128)(2,1)} %maximum_select_fusion.7), channel_id=1, source_target_pairs={{0,1},{1,0},{2,3},{3,2},{4,5},{5,4},{6,7},{7,6},{8,9},{9,8},{10,11... | collective-permute-start | bytes 3538952 | tf_op jit(solution)/shard_map/ppermute | solution.py:105
  1476.9 32.5 %collective-permute-start.189 = (bf16[192,1536]{1,0:T(8,128)(2,1)}, bf16[192,1536]{1,0:T(8,128)(2,1)}, u32[]{:S(2)}, u32[]{:S(2)}) collective-permute-start(bf16[192,1536]{1,0:T(8,128)(2,1)} %fusion.85), channel_id=1, source_target_pairs={{0,2},{1,3},{2,0},{3,1},{4,6},{5,7},{6,4},{7,5},{8,10},{9,11},{10,... | collective-permute-start | bytes 1769480 | tf_op jit(solution)/shard_map/ppermute | solution.py:105
  1501.9 32.8 %collective-permute-start.97 = (bf16[1024,384]{0,1:T(8,128)(2,1)}, bf16[1024,384]{0,1:T(8,128)(2,1)}, u32[]{:S(2)}, u32[]{:S(2)}) collective-permute-start(bf16[1024,384]{0,1:T(8,128)(2,1)} %fusion.108), channel_id=1, source_target_pairs={{0,1},{1,0},{2,3},{3,2},{4,5},{5,4},{6,7},{7,6},{8,9},{9,8},{10,11... | collective-permute-start | bytes 2359304 | tf_op jit(solution)/shard_map/ppermute | solution.py:105
  1519.2 28.7 %collective-permute-start.175 = (bf16[2,48,6144]{2,1,0:T(8,128)(2,1)}, bf16[2,48,6144]{2,1,0:T(8,128)(2,1)}, u32[]{:S(2)}, u32[]{:S(2)}) collective-permute-start(bf16[2,48,6144]{2,1,0:T(8,128)(2,1)} %maximum_select_fusion.5), channel_id=1, source_target_pairs={{0,1},{1,0},{2,3},{3,2},{4,5},{5,4},{6,7},{7,6},{8,9},{9,8},{10,11... | collective-permute-start | bytes 3538952 | tf_op jit(solution)/shard_map/ppermute | solution.py:105
  (412 other events, 5466.2 us)

commit v2 on v1

v2 whole, which is shorter than its diff:
```python
import itertools

import jax
import jax.numpy as jnp
from jax import lax
from jax.experimental import pallas as pl
from jax.experimental.pallas import tpu as pltpu
from jax.sharding import PartitionSpec as P

H = 16
MAXF = 8
eps = 1e-05
bf16 = jnp.bfloat16
f32 = jnp.float32
AXES = ("dp", "section")


def dot(left, right):
    return jnp.dot(left, right, preferred_element_type=f32)


def dot_rows(left, right):
    return lax.dot_general(left, right, (((0,), (0,)), ((), ())), preferred_element_type=f32)


def dot_cols(left, right):
    return lax.dot_general(left, right, (((1,), (1,)), ((), ())), preferred_element_type=f32)


def at(array, index, axis=0):
    return lax.dynamic_index_in_dim(array, index, axis, keepdims=False)


def normed(value):
    centred = value - jnp.mean(value, axis=-1, keepdims=True)
    spread = jnp.mean(centred * centred, axis=-1, keepdims=True)
    rstd = lax.rsqrt(spread + eps)
    return centred * rstd, rstd


def norm_back(hat, rstd, grad):
    mean = jnp.mean(grad, axis=-1, keepdims=True)
    along = jnp.mean(grad * hat, axis=-1, keepdims=True)
    return rstd * (grad - mean - hat * along)


class Zero:
    def __init__(self, value, index):
        self.value, self.index = value, index


def gate(needed, carried=()):
    needed, carried = list(needed), list(carried)
    count = len(needed) + len(carried)

    def kernel(*refs):
        refs[count][...] = jnp.zeros((1, 1), f32)
        refs[count + 1][0, 0] = jnp.int32(0)

    anywhere = pl.BlockSpec(memory_space=pl.ANY)
    out = pl.pallas_call(
        kernel,
        out_shape=[jax.ShapeDtypeStruct((1, 1), f32), jax.ShapeDtypeStruct((1, 1), jnp.int32)]
        + [jax.ShapeDtypeStruct(v.shape, v.dtype) for v in carried],
        in_specs=[anywhere] * count,
        out_specs=[
            pl.BlockSpec(memory_space=pltpu.VMEM),
            pl.BlockSpec(memory_space=pltpu.SMEM),
        ]
        + [anywhere] * len(carried),
        input_output_aliases={len(needed) + i: i + 2 for i in range(len(carried))},
    )(*needed, *carried)
    return Zero(out[0], out[1].reshape(())), list(out[2:])


def later(value, zero):
    return value + zero.value.astype(value.dtype).reshape((1,) * value.ndim)


def line_up(blocks, order):
    rows, lanes = blocks[0].shape
    count = len(blocks)

    def kernel(order_ref, *refs):
        out = refs[-1]
        for i in range(count):
            spot = pl.multiple_of(order_ref[i] * lanes, lanes)
            out[:, pl.ds(spot, lanes)] = refs[i][...]

    return pl.pallas_call(
        kernel,
        out_shape=jax.ShapeDtypeStruct((rows, count * lanes), blocks[0].dtype),
        in_specs=[pl.BlockSpec(memory_space=pltpu.SMEM)]
        + [pl.BlockSpec(memory_space=pltpu.VMEM)] * count,
        out_specs=pl.BlockSpec(memory_space=pltpu.VMEM),
    )(jnp.stack(order).astype(jnp.int32), *blocks)


def cut(array, start, size, axis=1):
    return lax.dynamic_slice_in_dim(array, start, size, axis)


def place(blocks, spots, count):
    out = jnp.zeros((count,) + blocks[0].shape, blocks[0].dtype)
    for block, spot in zip(blocks, spots):
        out = lax.dynamic_update_index_in_dim(out, block, spot, 0)
    return out


class Wires:
    def __init__(self, dp, section):
        assert section == 4 and dp % 2 == 0
        self.dp, self.section = dp, section
        self.depth = dp // 2
        self.hops = self.depth <= 4
        spots = list(itertools.product(range(self.depth), range(2), range(2), range(2)))

        def number(z, x, y, c):
            return (z * 2 + x) * section + y * 2 + c

        def pairs(move):
            return [(number(*spot), number(*move(*spot))) for spot in spots]

        n = self.depth
        self.swap_x = pairs(lambda z, x, y, c: (z, 1 - x, y, c))
        self.swap_y = pairs(lambda z, x, y, c: (z, x, 1 - y, c))
        self.swap_c = pairs(lambda z, x, y, c: (z, x, y, 1 - c))
        self.away_z = [pairs(lambda z, x, y, c, k=k: ((z + k) % n, x, y, c)) for k in range(n)]
        self.away = {
            (k, f): pairs(lambda z, x, y, c, k=k, f=f: ((z + k) % n, (x + f) % 2, y, c))
            for k in range(n)
            for f in range(2)
        }

    def enter(self):
        self.d = lax.axis_index("dp")
        self.s = lax.axis_index("section")
        self.z, self.x = self.d // 2, self.d % 2
        self.y, self.c = self.s // 2, self.s % 2

    def send(self, value, pairs):
        return lax.ppermute(value, AXES, pairs)

    def near_y(self, value):
        return self.send(value, self.swap_y)

    def near_c(self, value):
        return self.send(value, self.swap_c)

    def by_y(self, mine, other, axis):
        return jnp.where(
            self.y == 0,
            jnp.concatenate([mine, other], axis),
            jnp.concatenate([other, mine], axis),
        )

    def by_c(self, mine, other, axis):
        return jnp.where(
            self.c == 0,
            jnp.concatenate([mine, other], axis),
            jnp.concatenate([other, mine], axis),
        )

    def ring(self, k):
        return (self.z + k) % self.depth

    def gather_near(self, block):
        n = self.depth
        return [block] + [self.send(block, self.away_z[n - k]) for k in range(1, n)]

    def gather_far(self, got):
        n = self.depth
        there = [self.send(got[0], self.swap_x)[None], self.send(jnp.stack(got[1:]), self.swap_x)]
        there = jnp.concatenate(there, 0)
        spots = [self.ring(k) * 2 + self.x for k in range(n)]
        spots += [self.ring(k) * 2 + 1 - self.x for k in range(n)]
        return place(got + [there[k] for k in range(n)], spots, self.dp)

    def sum_far(self, blocks, start=0):
        pairs = blocks.reshape((self.depth, 2) + blocks.shape[1:])
        got = self.send(at(pairs, 1 - self.x + start, 1), self.swap_x)
        return at(pairs, self.x, 1), got

    def sum_near(self, mine, got, start=0):
        half = mine.astype(f32) + got.astype(f32)
        low = half.astype(bf16)
        parts = [
            self.send(at(low, self.ring(k) + start), self.away_z[k]) for k in range(1, self.depth)
        ]
        return at(half, self.z), parts

    def gather_rows(self, rows):
        if not self.hops:
            return lax.all_gather(rows, "dp", axis=0, tiled=True)
        n = self.depth
        got = [rows] + [self.send(rows, self.away_z[n - k]) for k in range(1, n)]
        got += [self.send(item, self.swap_x) for item in got]
        return jnp.concatenate(got, 0)

    def row_order(self):
        n = self.depth
        return [self.ring(k) * 2 + (self.x + f) % 2 for f in range(2) for k in range(n)]

    def sum_rows(self, partial):
        if not self.hops:
            return lax.psum_scatter(partial, "dp", scatter_dimension=0, tiled=True)
        n = self.depth
        half = partial.shape[0] // 2
        got = self.send(partial[half:].astype(bf16), self.swap_x)
        near = partial[:half] + got.astype(f32)
        low = near.astype(bf16).reshape((n, half // n) + partial.shape[1:])
        total = near[: half // n]
        for k in range(1, n):
            total = total + self.send(low[k], self.away_z[k]).astype(f32)
        return total

    def trade_near(self, blocks):
        n = self.depth
        got = []
        for k in range(n):
            pair = [blocks(self.ring(k) * 2 + (self.x + f) % 2) for f in range(2)]
            pair = jnp.stack(pair)
            got.append(pair if k == 0 else self.send(pair, self.away_z[k]))
        return got

    def trade_far(self, got, zero):
        far = later(jnp.stack([pair[1] for pair in got]), zero)
        return [pair[0] for pair in got], self.send(far, self.swap_x)

    def trade_order(self):
        n = self.depth
        return [self.ring(n - k) * 2 + (self.x + f) % 2 for f in range(2) for k in range(n)]

    def trade_all(self, blocks):
        mine = jnp.stack([blocks(d) for d in range(self.dp)])
        return lax.all_to_all(mine, "dp", 0, 0, tiled=True)

    def spread(self, rows, fill):
        half = rows.shape[1] // 2
        got = self.near_y(cut(rows, half * (1 - self.y), half).astype(bf16)).astype(fill)
        mine = cut(rows, half * self.y, half).astype(fill)
        return self.spread_c(self.by_y(mine, got, 0))

    def spread_c(self, cols):
        half = cols.shape[1] // 2
        got = self.near_c(cut(cols, half * (1 - self.c), half).astype(bf16)).astype(cols.dtype)
        return self.by_c(cut(cols, half * self.c, half)[None], got[None], 0)


def expand(value, heads):
    rows, width = value.shape
    size = width // heads
    owner = lax.broadcasted_iota(jnp.int32, (heads, 1, width), 2) // size
    index = lax.broadcasted_iota(jnp.int32, (heads, 1, width), 0)
    return jnp.where(owner == index, value[None], jnp.zeros((), value.dtype)).reshape(
        heads * rows, width
    )


def collapse(value, heads):
    width = value.shape[1]
    size = width // heads
    owner = lax.broadcasted_iota(jnp.int32, (heads, 1, width), 2) // size
    index = lax.broadcasted_iota(jnp.int32, (heads, 1, width), 0)
    return jnp.sum(
        jnp.where(owner == index, value.reshape(heads, -1, width), 0.0), axis=0
    )


def gelu(hidden):
    return jax.nn.gelu(hidden, approximate=False)


def shards(wires):
    def run(
        latents,
        media,
        frames,
        cotangent,
        w_query,
        w_keyval,
        w_output,
        w_inner,
        w_outer,
        norm_gains,
        norm_biases,
    ):
        wires.enter()
        y, c, s = wires.y, wires.c, wires.s
        dp = wires.dp
        layers, shard, width = w_query.shape
        size = width // H
        scale = size ** (-0.5)
        half = width // 2
        media_len = media.shape[1]
        lat_len = latents.shape[1]
        rows = lat_len // 2
        local = H // 4
        quarter = local * size
        group = local * lat_len
        span = w_inner.shape[2] // dp
        part = shard // 4
        top = layers - 1

        column = lax.broadcasted_iota(jnp.int32, (width, quarter), 1)
        row = lax.broadcasted_iota(jnp.int32, (width, quarter), 0)
        wanted = (2 * (local * c + column // size) + y) * size + column % size
        pick = (row == wanted).astype(bf16)
        stacked = jnp.concatenate([w_query, w_keyval[:, :, :width], w_keyval[:, :, width:]], 1)
        picked = dot(stacked.reshape(-1, width), pick).astype(bf16)
        picked = picked.reshape(layers, 3, shard, quarter)
        vectors = jnp.concatenate([norm_gains, norm_biases], 1).reshape(layers * 6, shard)

        def inner_block(level, parts, index, start):
            count = shard // parts

            def block(d):
                at_row = count * index + start
                block = lax.dynamic_slice(w_inner, (level, at_row, span * d), (1, count, span))
                return block[0]

            return block

        def weights_of(whole):
            whole = whole.reshape(-1, whole.shape[2])
            return [whole, wires.near_c(whole)]

        def joined(whole):
            whole = whole.reshape(dp, 2, size, quarter)
            return jnp.concatenate([whole[:, h].reshape(half, quarter) for h in range(2)], 1)[None]

        w_attn = [None] * layers
        if wires.hops:
            out_piece = lax.dynamic_slice(
                w_output, (0, size * y, half * c), (layers, size, half)
            )
            padded = jnp.zeros((128, shard), bf16).at[: layers * 6].set(vectors)
            first = jnp.concatenate([picked[0, 0], picked[0, 1], padded.T], 1)
            first = wires.gather_near(first)
            out_piece = jnp.concatenate([out_piece[..., :quarter], out_piece[..., quarter:]], 1)
            second = lax.all_gather(jnp.stack([picked[0, 2], out_piece[0]]), "dp", axis=1)
            zero, _ = gate(first[1:])
            inner0 = wires.trade_near(inner_block(0, 2, c, zero.index))
            first = wires.gather_far(first)
            first = [first[:, :, i * quarter : (i + 1) * quarter] for i in range(2)] + [
                first[:, :, 2 * quarter :]
            ]
            one = lax.broadcasted_iota(jnp.int32, (layers * 6, 128), 0)
            one = (one == lax.broadcasted_iota(jnp.int32, (layers * 6, 128), 1)).astype(bf16)
            vectors = dot_cols(one, first[2].reshape(width, 128))
        else:
            vectors = lax.all_gather(vectors, "dp", axis=1, tiled=True)
        vectors = vectors.astype(f32).reshape(layers, 2, 3, width)
        gains, biases = vectors[:, 0], vectors[:, 1]

        both = jnp.stack([latents, cotangent])
        got = wires.near_c(at(both, 1 - c, 1))
        wide = wires.by_c(at(both, c, 1), got, 2)
        whole = wires.by_y(wide, wires.near_y(wide), 2)
        whole = jnp.where(y == 0, whole, jnp.roll(whole, rows, axis=1))
        state = whole[0].astype(f32)
        target = whole[1, :rows]

        hat_f, rstd_media = normed(at(media, c).astype(f32))
        hat = hat_f.astype(bf16)
        keep = jnp.arange(media_len) < at(frames, c) * (media_len // MAXF)

        def look(lat_norm, w_q, w_k, level):
            gain, bias = gains[level, 0], biases[level, 0]
            query = [dot(lat_norm, w).astype(bf16) for w in w_q]
            query_x = [expand(q, local) for q in query]
            lifted = jnp.concatenate([dot_cols(q, k) for q, k in zip(query_x, w_k)], 0)
            lifted = lifted * scale
            key_g = (lifted * gain).astype(bf16)
            key_l = lifted.astype(bf16)
            shift = jnp.sum(lifted * bias, axis=-1, keepdims=True)
            scores = dot_cols(key_g, hat) + shift
            scores = jnp.where(keep[None], scores, -1e30)
            scores_l = dot_cols(key_l, lat_norm)
            high = jnp.maximum(
                jnp.max(scores, axis=-1, keepdims=True), jnp.max(scores_l, axis=-1, keepdims=True)
            )
            expo, expo_l = jnp.exp(scores - high), jnp.exp(scores_l - high)
            total = jnp.sum(expo, axis=-1, keepdims=True) + jnp.sum(expo_l, axis=-1, keepdims=True)
            low, low_l = (expo / total).astype(bf16), (expo_l / total).astype(bf16)
            mass = jnp.sum(low.astype(f32), axis=-1, keepdims=True)
            mixed_hat = dot(low, hat)
            mixed = (mixed_hat * gain + mass * bias + dot(low_l, lat_norm)).astype(bf16)
            mixed_hat = mixed_hat.astype(bf16)
            return dict(
                query=query, query_x=query_x, key_g=key_g, key_l=key_l,
                low=low, low_l=low_l, mass=mass, mixed_hat=mixed_hat, mixed=mixed,
            )

        def answer(kept, w_v, w_o):
            mixed = kept["mixed"]
            att = [
                collapse(dot(mixed[i * group : (i + 1) * group], v), local).astype(bf16)
                for i, v in enumerate(w_v)
            ]
            attended = wires.by_c(att[0], att[1], 1)
            kept["attended"] = attended
            return wires.by_c(dot(attended, w_o[0]), dot(attended, w_o[1]), 1)

        def answer_back(d_mid, lat_norm, weights, level, kept):
            w_v, w_o = weights[2], weights[3]
            gain, bias = gains[level, 0], biases[level, 0]
            d_mine, d_other = cut(d_mid, half * c, half), cut(d_mid, half * (1 - c), half)
            d_att = (dot_cols(d_mine, w_o[0]) + dot_cols(d_other, w_o[1])).astype(bf16)
            d_att = [cut(d_att, quarter * c, quarter), cut(d_att, quarter * (1 - c), quarter)]
            d_att_x = [expand(v, local) for v in d_att]
            raised = jnp.concatenate([dot_cols(a, v) for a, v in zip(d_att_x, w_v)], 0)
            val_g = (raised * gain).astype(bf16)
            val_l = raised.astype(bf16)
            shift = jnp.sum(raised * bias, axis=-1, keepdims=True)
            kept.update(d_att=d_att, d_att_x=d_att_x, val_g=val_g, val_l=val_l)
            kept.update(shift=shift, d_mine=d_mine, d_other=d_other)

        def look_back(lat_norm, weights, level, kept):
            w_q, w_k = weights[0], weights[1]
            gain, bias = gains[level, 0], biases[level, 0]
            probs, probs_l = kept["low"].astype(f32), kept["low_l"].astype(f32)
            d_probs = dot_cols(kept["val_g"], hat) + kept["shift"]
            d_probs_l = dot_cols(kept["val_l"], lat_norm)
            along = jnp.sum(probs * d_probs, axis=-1, keepdims=True)
            along = along + jnp.sum(probs_l * d_probs_l, axis=-1, keepdims=True)
            ds = (probs * (d_probs - along)).astype(bf16)
            ds_l = (probs_l * (d_probs_l - along)).astype(bf16)
            ds_mass = jnp.sum(ds.astype(f32), axis=-1, keepdims=True)
            ds_hat = dot(ds, hat)
            d_lift = (ds_hat * gain + ds_mass * bias + dot(ds_l, lat_norm)).astype(bf16)
            d_query = [
                (collapse(dot(d_lift[i * group : (i + 1) * group], k), local) * scale).astype(bf16)
                for i, k in enumerate(w_k)
            ]
            d_lat = dot_cols(d_query[0], w_q[0]) + dot_cols(d_query[1], w_q[1])
            d_lat = d_lat + dot_rows(
                jnp.concatenate([ds_l, kept["low_l"]], 0),
                jnp.concatenate([kept["key_l"], kept["val_l"]], 0),
            )
            lifted, raised = kept["key_l"].astype(f32), kept["val_l"].astype(f32)
            d_gain = jnp.sum(lifted * ds_hat + raised * kept["mixed_hat"].astype(f32), axis=0)
            d_bias = jnp.sum(lifted * ds_mass + raised * kept["mass"], axis=0)
            kept.update(ds=ds, d_lift=d_lift, d_query=d_query, d_gain=d_gain, d_bias=d_bias)
            return d_lat

        def value_grads(kept, zero):
            small = [kept["attended"], kept["d_other"], kept["d_att"][1]]
            got = wires.near_c(later(jnp.concatenate(small, 1), zero))
            attended, d_mine, d_att = got[:, :half], got[:, half:width], got[:, width:]
            mixed = wires.near_c(later(kept["mixed"][group:], zero))
            mixed = jnp.concatenate([kept["mixed"][:group], mixed], 0)
            d_att = jnp.concatenate([kept["d_att_x"][0], expand(d_att, local)], 0)
            g_value = dot_rows(mixed, d_att).astype(bf16)
            attended = jnp.concatenate([kept["attended"], attended], 0)
            d_mine = jnp.concatenate([kept["d_mine"], d_mine], 0)
            g_output = dot_rows(attended, d_mine).astype(bf16)
            return [g_value, g_output]

        def query_grads(lat_norm, kept, zero):
            small = [lat_norm, kept["query"][1], kept["d_query"][1]]
            got = wires.near_c(later(jnp.concatenate(small, 1), zero))
            lat, query, d_query = got[:, :width], got[:, width : width + quarter], got[:, width + quarter :]
            lift = wires.near_c(later(kept["d_lift"][group:], zero))
            lift = jnp.concatenate([kept["d_lift"][:group], lift], 0)
            query = jnp.concatenate([kept["query_x"][0], expand(query, local)], 0)
            g_key = (dot_rows(lift, query) * scale).astype(bf16)
            lat = jnp.concatenate([lat_norm, lat], 0)
            d_query = jnp.concatenate([kept["d_query"][0], d_query], 0)
            return [dot_rows(lat, d_query).astype(bf16), g_key]

        index = lax.broadcasted_iota(jnp.int32, (half, half), 0)
        goal = lax.broadcasted_iota(jnp.int32, (half, half), 1)
        head, within = index // size, index % size
        order = ((head % local) * 2 + head // local) * size + within
        shuffle = (order == goal).astype(bf16)

        def columns(v):
            n = v.shape[2]
            both = [jnp.concatenate([v[0, i], v[1, i]], 1) for i in range(2)]
            out = dot(jnp.concatenate(both, 0), shuffle)
            return jnp.concatenate([out[:n], out[n:]], 1)

        def finish(query, key, value, out):
            out = jnp.concatenate([out[:, 0], out[:, 1]], 2).reshape(shard, width).astype(f32)
            key_value = jnp.concatenate([columns(key), columns(value)], 1)
            return columns(query), key_value, out

        def finish_generic(query_key, g_value, g_output):
            blocks = jnp.concatenate(query_key + [g_value], 1).reshape(dp, shard, 3 * quarter)
            parts = lax.psum_scatter(blocks, "dp", scatter_dimension=0, tiled=False)
            whole = g_output.reshape(H // 2, 1, size, half)
            whole = wires.by_y(whole, jnp.zeros_like(whole), 1).reshape(dp, shard, half)
            out = lax.psum_scatter(whole, "dp", scatter_dimension=0, tiled=False)
            parts = lax.all_gather(parts, "section", axis=0).reshape(2, 2, shard, 3 * quarter)
            out = lax.all_gather(out, "section", axis=0).reshape(2, 2, shard, half)
            out = jnp.sum(out.astype(f32), 0)
            parts = [columns(parts[..., j * quarter : (j + 1) * quarter]) for j in range(3)]
            out = jnp.concatenate([out[0], out[1]], 1)
            return parts[0], jnp.concatenate(parts[1:], 1), out

        def ffn_grads(active, dz_all, mn_all, d_hidden):
            g_inner = dot_rows(mn_all, d_hidden).astype(bf16)
            return g_inner, dot_rows(active, dz_all).astype(bf16)

        def norm_latents(x_hat, level):
            return (x_hat * gains[level, 1] + biases[level, 1]).astype(bf16)

        def middle(x_rows, branch, level):
            branch = branch[:rows] + wires.near_y(branch[rows:].astype(bf16)).astype(f32)
            mid = (x_rows + branch).astype(bf16).astype(f32)
            hat_m, rstd_m = normed(mid)
            mn = (hat_m * gains[level, 2] + biases[level, 2]).astype(bf16)
            return mid, hat_m, rstd_m, mn

        def ffn_back(dz_all, hidden, level):
            d_active = dot_cols(dz_all, w_outer[level])
            return jax.vjp(gelu, hidden)[1](d_active)[0].astype(bf16)

        def middle_back(grad, hat_m, rstd_m, d_mn, level):
            d_low = (grad + norm_back(hat_m, rstd_m, d_mn * gains[level, 2])).astype(bf16)
            return d_low, jnp.concatenate([d_low, wires.near_y(d_low)], 0)

        def latents_back(d_low, d_lat, x_hat, x_rstd, level):
            d_norm = d_lat[:rows] + wires.near_y(d_lat[rows:].astype(bf16)).astype(f32)
            grad = d_low.astype(f32) + norm_back(x_hat, x_rstd, d_norm * gains[level, 1])
            if level > 0:
                grad = grad.astype(bf16).astype(f32)
            return d_norm, grad

        def vector_rows(attn, d_norm, x_hat, d_mn, hat_m):
            return [
                attn["d_gain"],
                jnp.sum(d_norm * x_hat, 0),
                jnp.sum(d_mn * hat_m, 0),
                attn["d_bias"],
                jnp.sum(d_norm, 0),
                jnp.sum(d_mn, 0),
            ]

        def media_pair(attn):
            left = jnp.concatenate([attn["ds"], attn["low"]], 0)
            return left, jnp.concatenate([attn["key_g"], attn["val_g"]], 0)

        def outputs(x_low, grad, media_grad, attn_out, ffn_out, sums):
            sums = sums.reshape(layers, 2, 3, shard)
            outs = [jnp.stack([attn_out[level][i] for level in range(layers)]) for i in range(3)]
            outs += [jnp.stack([ffn_out[level][i] for level in range(layers)]) for i in range(2)]
            return (
                wires.spread(x_low, bf16),
                media_grad,
                wires.spread(grad, f32),
                *outs,
                sums[:, 0, :2],
                sums[:, 1, :2],
                sums[:, :, 2],
            )

        x_hat0, x_rstd0 = normed(state)
        lat_norm0 = norm_latents(x_hat0, 0)
        x_hat0, x_rstd0 = x_hat0[:rows], x_rstd0[:rows]
        x_rows0 = state[:rows]

        if not wires.hops:
            nil = Zero(jnp.zeros((1, 1), f32), 0)
            x_rows, x_hat, x_rstd, lat_norm = x_rows0, x_hat0, x_rstd0, lat_norm0
            kept = []
            for level in range(layers):
                got = [
                    lax.all_gather(picked[level, j], "dp", axis=0).reshape(width, quarter)
                    for j in range(3)
                ]
                out = lax.all_gather(w_output[level], "dp", axis=0, tiled=True)
                out = at(out.reshape(H // 2, 2, size, 2, half), y, 1)
                got.append(at(out, c, 2).reshape(half, half))
                weights = [[item, wires.near_c(item)] for item in got]
                w_in = wires.trade_all(inner_block(level, 1, 0, 0)).reshape(width, span)
                if level > 0:
                    x_hat, x_rstd = normed(x_rows)
                    mine = norm_latents(x_hat, level)
                    lat_norm = jnp.concatenate([mine, wires.near_y(mine)], 0)
                attn = look(lat_norm, weights[0], weights[1], level)
                branch = answer(attn, weights[2], weights[3])
                mid, hat_m, rstd_m, mn = middle(x_rows, branch, level)
                mn_all = wires.gather_rows(mn)
                hidden = dot(mn_all, w_in)
                active = gelu(hidden).astype(bf16)
                x_low = (mid + wires.sum_rows(dot(active, w_outer[level]))).astype(bf16)
                x_rows = x_low.astype(f32)
                kept.append(
                    (attn, lat_norm, x_hat, x_rstd, hat_m, rstd_m, mn_all, hidden, active, weights, w_in)
                )
            grad = target.astype(f32)
            ffn_out, attn_out, vector_grads, media_sum = [], [], [], 0.0
            for level in reversed(range(layers)):
                attn, lat_norm, x_hat, x_rstd, hat_m, rstd_m, mn_all, hidden, active, weights, w_in = kept[level]
                dz_all = wires.gather_rows(grad.astype(bf16))
                d_hidden = ffn_back(dz_all, hidden, level)
                d_mn = wires.sum_rows(dot_cols(d_hidden, w_in))
                share = ffn_grads(active, dz_all, mn_all, d_hidden)
                share = [lax.psum(v.astype(f32), "section") for v in share]
                inner = share[0].reshape(dp, shard, span).astype(bf16)
                inner = wires.trade_all(lambda d: inner[d])
                inner = jnp.transpose(inner, (1, 0, 2)).reshape(shard, dp * span)
                ffn_out.insert(0, (inner.astype(f32), share[1]))
                d_low, d_mid = middle_back(grad, hat_m, rstd_m, d_mn, level)
                answer_back(d_mid, lat_norm, weights, level, attn)
                d_lat = look_back(lat_norm, weights, level, attn)
                d_norm, grad = latents_back(d_low, d_lat, x_hat, x_rstd, level)
                vector_grads = vector_rows(attn, d_norm, x_hat, d_mn, hat_m) + vector_grads
                attn_out.insert(
                    0, finish_generic(query_grads(lat_norm, attn, nil), *value_grads(attn, nil))
                )
                media_sum = media_sum + dot_rows(*media_pair(attn))
            d_media = norm_back(hat.astype(f32), rstd_media, media_sum)
            got = wires.near_y(cut(d_media, half * (1 - y), half).astype(bf16))
            media_grad = wires.spread_c(cut(d_media, half * y, half) + got.astype(f32))
            extra = lax.psum(jnp.stack(vector_grads), "section")
            sums = lax.psum_scatter(extra, "dp", scatter_dimension=1, tiled=True)
            return outputs(x_low, grad, media_grad, attn_out, ffn_out, sums)

        order = wires.trade_order()
        w_q, w_k = [weights_of(v) for v in first[:2]]
        attn0 = look(lat_norm0, w_q, w_k, 0)
        zero, (second,) = gate([attn0["low"]] + inner0[1:], [second])
        piece = jnp.concatenate([picked[1], out_piece[1][None]], 0)
        rest = lax.all_gather(later(piece, zero), "dp", axis=1)
        inner0 = wires.trade_far(inner0, zero)
        w_v, w_o = [weights_of(v) for v in (second[0], joined(second[1]))]
        weights0 = [w_q, w_k, w_v, w_o]
        branch = answer(attn0, w_v, w_o)
        zero, (branch,) = gate([inner0[1]], [branch])
        step = zero.index
        mid0, hat_m0, rstd_m0, mn = middle(x_rows0, branch, 0)
        mn_all0 = wires.gather_rows(mn)
        inner0 = place(inner0[0] + list(inner0[1]), [v + step for v in order], dp)
        inner0 = wires.by_c(inner0[:, None], wires.near_c(inner0)[:, None], 1)
        w_in0 = inner0.reshape(width, span)
        hidden0 = dot(mn_all0, w_in0)
        active0 = gelu(hidden0).astype(bf16)
        x_low = (mid0 + wires.sum_rows(dot(active0, w_outer[0]))).astype(bf16)

        zero, (x_low, rest) = gate([], [x_low, rest])
        inner1 = wires.trade_near(inner_block(1, 4, s, zero.index))
        targets = wires.gather_near(later(target, zero))
        x_rows1 = x_low.astype(f32)
        x_hat1, x_rstd1 = normed(x_rows1)
        mine = norm_latents(x_hat1, 1)
        lat_norm1 = jnp.concatenate([mine, wires.near_y(mine)], 0)
        weights1 = [weights_of(v) for v in (rest[0], rest[1], rest[2], joined(rest[3]))]
        attn1 = look(lat_norm1, weights1[0], weights1[1], 1)
        zero, _ = gate([attn1["low"]])
        inner1 = wires.trade_far(inner1, zero)
        targets = later(jnp.concatenate(targets, 0), zero)
        target_all = jnp.concatenate([targets, wires.send(targets, wires.swap_x)], 0)
        branch = answer(attn1, weights1[2], weights1[3])
        zero, (branch,) = gate([], [branch])
        step = zero.index
        mid1, hat_m1, rstd_m1, mn = middle(x_rows1, branch, 1)
        mn_all1 = wires.gather_rows(mn)
        inner1 = place(inner1[0] + list(inner1[1]), [v + step for v in order], dp)
        inner1 = wires.by_y(inner1[:, None], wires.near_y(inner1)[:, None], 1)
        inner1 = wires.by_c(inner1[:, :, None], wires.near_c(inner1)[:, :, None], 2)
        w_in1 = inner1.reshape(width, span)
        hidden1 = dot(mn_all1, w_in1)
        active1 = gelu(hidden1).astype(bf16)
        x_part = dot(active1, w_outer[1]).astype(bf16)

        d_hidden = ffn_back(target_all, hidden1, 1)
        d_mn1 = wires.sum_rows(dot_cols(d_hidden, w_in1))
        g_ffn = ffn_grads(active1, target_all, mn_all1, d_hidden)
        zero, (d_mn1,) = gate(g_ffn, [d_mn1])

        def shared(grads):
            g_inner = jnp.transpose(grads[0].reshape(dp, 4, part, span), (1, 0, 2, 3))
            parts = [g_inner, grads[1].reshape(4, span // 4, width)]
            return [lax.psum_scatter(v, "section", scatter_dimension=0) for v in parts]

        def output_blocks(grad):
            grad = grad.reshape(dp, size, half)
            return jnp.concatenate([grad[:, :, :quarter], grad[:, :, quarter:]], 1)

        def output_columns(v):
            v = v.reshape(2, 2, 2, size, quarter)
            return jnp.concatenate([v[:, :, 0], v[:, :, 1]], 3)

        share1 = shared(g_ffn)
        d_low1, d_mid1 = middle_back(target.astype(f32), hat_m1, rstd_m1, d_mn1, 1)
        answer_back(d_mid1, lat_norm1, weights1, 1, attn1)
        d_lat = look_back(lat_norm1, weights1, 1, attn1)
        zero, (d_lat,) = gate([], [d_lat])
        d_norm1, grad = latents_back(d_low1, d_lat, x_hat1, x_rstd1, 1)
        dz_all = wires.gather_rows(grad.astype(bf16))
        g_attn = query_grads(lat_norm1, attn1, zero) + value_grads(attn1, zero)

        zero, (dz_all,) = gate(g_attn, [dz_all])
        blocks = [v.reshape(dp, shard, quarter) for v in g_attn[:3]] + [output_blocks(g_attn[3])]
        blocks = jnp.concatenate(blocks, 2)
        blocks1 = lax.psum_scatter(blocks, "dp", scatter_dimension=0, tiled=False)
        d_hidden = ffn_back(dz_all, hidden0, 0)
        d_mn0 = wires.sum_rows(dot_cols(d_hidden, w_in0))
        g_ffn = ffn_grads(active0, dz_all, mn_all0, d_hidden)
        left, right = media_pair(attn1)
        media_sum = dot_rows(left, later(right, zero))
        zero, (d_mn0, *g_ffn) = gate([media_sum, *share1], [d_mn0, *g_ffn])
        share0 = shared(g_ffn)
        d_low0, d_mid0 = middle_back(grad, hat_m0, rstd_m0, d_mn0, 0)
        answer_back(d_mid0, lat_norm0, weights0, 0, attn0)
        g_vo = value_grads(attn0, zero)
        zero, (attn0["shift"],) = gate(g_vo, [attn0["shift"]])
        g_vo = jnp.concatenate([g_vo[0].reshape(dp, shard, quarter), output_blocks(g_vo[1])], 2)
        g_vo = wires.sum_far(g_vo, zero.index)
        d_lat = look_back(lat_norm0, weights0, 0, attn0)
        zero, (d_lat, attn0["d_lift"]) = gate([], [d_lat, attn0["d_lift"]])
        g_vo = wires.sum_near(g_vo[0], later(g_vo[1], zero))
        d_norm0, grad = latents_back(d_low0, d_lat, x_hat0, x_rstd0, 0)
        left, right = media_pair(attn0)
        media_sum = media_sum + dot_rows(left, later(right, zero))
        d_media = norm_back(hat.astype(f32), rstd_media, media_sum)
        send = cut(d_media, half * (1 - y), half).astype(bf16)
        zero, (send, grad, attn0["d_lift"]) = gate([], [send, grad, attn0["d_lift"]])
        got = wires.near_y(send)
        extra = vector_rows(attn0, d_norm0, x_hat0, d_mn0, hat_m0)
        extra += vector_rows(attn1, d_norm1, x_hat1, d_mn1, hat_m1)
        extra = jnp.zeros((128, width), f32).at[: layers * 6].set(jnp.stack(extra)).T
        g_qk = query_grads(lat_norm0, attn0, zero) + [extra.astype(bf16)]
        g_qk = jnp.concatenate(g_qk, 1)
        zero, (g_qk, blocks1, *share1) = gate([], [g_qk, blocks1, *share1])
        step = zero.index
        g_qk = wires.sum_far(g_qk.reshape(dp, shard, g_qk.shape[1]), step)
        x_part = wires.sum_rows(later(x_part, zero).astype(f32))
        blocks1 = lax.all_gather(blocks1, "section", axis=0)
        outer1 = lax.all_gather(share1[1], "section", axis=0, tiled=True)
        zero, (far, grad, share0[0]) = gate([], [g_qk[1], grad, share0[0]])
        step = zero.index
        g_qk = wires.sum_near(g_qk[0], far)
        trade = jnp.concatenate([share1[0], share0[0]], 1)
        trade = wires.trade_near(lambda d: at(trade, d + step))
        blocks1 = later(blocks1, zero).reshape(2, 2, shard, 4 * quarter)
        parts = [blocks1[..., j * quarter : (j + 1) * quarter] for j in range(4)]
        attn_out1 = finish(*parts[:3], output_columns(parts[3]))
        zero, (grad, share0[1], *arrived) = gate([*attn_out1], [grad, share0[1], *g_qk[1]])
        g_qk = (g_qk[0], arrived)
        trade = wires.trade_far(trade, zero)
        outer0 = lax.all_gather(share0[1], "section", axis=0, tiled=True)
        x_out = (mid1 + x_part + zero.value).astype(bf16)

        def summed(mine, parts):
            for v in parts:
                mine = mine + v.astype(f32)
            return mine.astype(bf16)

        def join(v):
            pair = wires.by_y(v[None], wires.near_y(v)[None], 0)
            return wires.by_c(pair[:, None], wires.near_c(pair)[:, None], 1)

        four = join(jnp.concatenate([summed(*g_vo), summed(*g_qk)], 1))
        value, out, query, key = [four[..., i * quarter : (i + 1) * quarter] for i in range(4)]
        sums = jnp.sum(four[..., 4 * quarter :].astype(f32), axis=(0, 1))[:, : layers * 6].T
        inner = []
        for i in range(layers):
            rows_of = slice(i * part, (i + 1) * part)
            blocks = [v[rows_of] for v in trade[0] + list(trade[1])]
            v = lax.all_gather(line_up(blocks, order), "section", axis=0, tiled=True)
            inner.append(v.astype(f32))
        ffn_out = [(inner[1], outer0.astype(f32)), (inner[0], outer1.astype(f32))]
        attn_out0 = finish(query, key, value, output_columns(out))
        media_grad = wires.spread_c(cut(d_media, half * y, half) + later(got, zero).astype(f32))
        return outputs(
            x_out, grad, media_grad, [attn_out0, attn_out1], ffn_out, sums
        )

    return run


def solution(mesh):
    wires = Wires(mesh.shape["dp"], mesh.shape["section"])
    return jax.shard_map(
        shards(wires),
        mesh=mesh,
        in_specs=(
            P("dp", None, "section"),
            P("dp", None, None),
            P("dp"),
            P("dp", None, "section"),
            P(None, "dp", None),
            P(None, "dp", None),
            P(None, "dp", None),
            P(None, "dp", None),
            P(None, "dp", None),
            P(None, None, "dp"),
            P(None, None, "dp"),
        ),
        out_specs=(
            P("dp", None, "section"),
            P("dp", None, "section"),
            P("dp", None, "section"),
            P(None, "dp", None),
            P(None, "dp", None),
            P(None, "dp", None),
            P(None, "dp", None),
            P(None, "dp", None),
            P(None, None, "dp"),
            P(None, None, "dp"),
            P(None, None, "dp"),
        ),
        check_vma=False,
    )
```

time: 1570 us -> 823 us (0.52)
  Pallas kernels: 482 us -> 12.4 us
  waiting for transfers between devices: 427 us -> 247 us
  local copies, waits for them, and re-layouts: 154 us -> 100 us
  between operations: 7.01 us -> 45.1 us
  blocking collectives: 30.6 us -> 0 us
  other arithmetic: 148 us -> 121 us
  starting transfers between devices: 172 us -> 152 us
    pallas_call x9 -> x18, Pallas kernels: 482 us -> 12.4 us  [the longest x16 8.32 us: gate(): pl.pallas_call(kernel, out_shape=[jax.ShapeDtypeStruct((1, 1), f32), jax....]
    ppermute x195 -> x102, waiting for transfers between devices: 427 us -> 244 us  [send(): return lax.ppermute(value, AXES, pairs)]
    all_gather x1 -> x0, blocking collectives: 30.6 us -> none  [run(): vectors = lax.all_gather(vectors, 'dp', axis=1, tiled=True).astype(f32)]
    dynamic_slice x16 -> x2, local copies, waits for them, and re-layouts: 21.9 us -> 0.67 us  [at(): return lax.dynamic_index_in_dim(array, index, axis, keepdims=False)]
    ppermute x195 -> x102, starting transfers between devices: 172 us -> 152 us  [send(): return lax.ppermute(value, AXES, pairs)]
    select_n x28 -> x11, other arithmetic: 28.2 us -> 8.49 us  [by_c(): jnp.where(self.c == 0, jnp.concatenate([mine, other], axis), jnp.concaten...]
    unnamed x630 -> x460, local copies, waits for them, and re-layouts: 41.4 us -> 36.5 us
    dot_general x15 -> x16, matrix products: 39.8 us -> 36.8 us  [dot_rows(): lax.dot_general(left, right, (((0,), (0,)), ((), ())), preferred_element_...]
  transfers between devices with their start and end apart: 195 -> 114, of which waited for: 80 -> 44; matrix products, arithmetic and copies ran while one was open for 25% -> 37% of each run, Pallas kernels for 31% -> 1%
where the time goes in v2:
time: 823 us; the launch traced here: 814 us
  waiting for transfers between devices  247 us (30%)
  starting transfers between devices  152 us (18%)
  matrix products  136 us (17%)
  other arithmetic  121 us (15%)
  local copies, waits for them, and re-layouts  100 us (12%)
  between operations  45.1 us (5%)
  Pallas kernels  12.4 us (2%)
    ppermute x102, waiting for transfers between devices, send(): return lax.ppermute(value, AXES, pairs)  244 us
    ppermute x102, starting transfers between devices, send(): return lax.ppermute(value, AXES, pairs)  152 us
    dot_general x35, matrix products, dot(): return jnp.dot(left, right, preferred_element_type=f32)  54.6 us
    dot_general x29, matrix products, dot_cols(): lax.dot_general(left, right, (((1,), (1,)), ((), ())), preferred_element_...  44.8 us
    dot_general x16, matrix products, dot_rows(): lax.dot_general(left, right, (((0,), (0,)), ((), ())), preferred_element_...  36.8 us
    unnamed x460, local copies, waits for them, and re-layouts  36.5 us
  transfers between devices with their start and end apart: 114, of which 44 were waited for; matrix products, arithmetic and copies ran while one was open for 37% of the time, Pallas kernels for 1%

profile of v2, /device:TPU:0, one launch (start us, length us, event | category | flops | bytes accessed | tf_op | source)
XLA Modules:
  0.0 814.1 jit_solution(3072278050933325972)
XLA Ops:
  15.4 2.9 collective-permute-start.8
  31.1 3.0 fusion.3
  34.1 4.3 fusion.4
  42.2 5.8 collective-permute-done.1
  53.3 2.7 constant_dynamic-slice_fusion.23
  56.0 10.3 %collective-permute-start.5 = (bf16[2,96,768]{2,1,0:T(8,128)(2,1)S(1)}, bf16[2,96,768]{2,1,0:T(8,128)(2,1)S(1)}, u32[]{:S(2)}, u32[]{:S(2)}) collective-permute-start(bf16[2,96,768]{2,1,0:T(8,128)(2,1)S(1)} %pad_maximum_fusion.23), channel_id=1, source_target_pairs={{0,8},{1,9},{2,10},{3,11},{4,12},{5,13},{6,14},{7,15},{8,16},{9,17... | collective-permute-start | bytes 884744 | tf_op jit(solution)/shard_map/ppermute | solution.py:142
  73.9 7.3 collective-permute-done.5.refs_1_
  81.2 20.4 %collective-permute-done.6.refs_2_ = bf16[2,96,768]{2,1,0:T(8,128)(2,1)S(1)} collective-permute-done((bf16[2,96,768]{2,1,0:T(8,128)(2,1)S(1)}, bf16[2,96,768]{2,1,0:T(8,128)(2,1)S(1)}, u32[]{:S(2)}, u32[]{:S(2)}) %collective-permute-start.6) | collective-permute-done | bytes 294944 | tf_op jit(solution)/shard_map/ppermute | solution.py:142
  106.6 2.7 collective-permute-done.10
  118.8 3.5 fusion.412
  122.8 3.1 fusion.383
  138.6 8.6 %collective-permute-done.12.refs_0_ = bf16[4,96,768]{2,1,0:T(8,128)(2,1)} collective-permute-done((bf16[4,96,768]{2,1,0:T(8,128)(2,1)S(1)}, bf16[4,96,768]{2,1,0:T(8,128)(2,1)}, u32[]{:S(2)}, u32[]{:S(2)}) %collective-permute-start.12) | collective-permute-done | bytes 589856 | tf_op jit(solution)/shard_map/ppermute | solution.py:142
  160.5 15.3 %collective-permute-start.18 = (bf16[32,1536]{1,0:T(8,128)(2,1)S(1)}, bf16[32,1536]{1,0:T(8,128)(2,1)S(1)}, u32[]{:S(2)}, u32[]{:S(2)}) collective-permute-start(bf16[32,1536]{1,0:T(8,128)(2,1)S(1)} %get-tuple-element.186), channel_id=1, source_target_pairs={{0,8},{1,9},{2,10},{3,11},{4,12},{5,13},{6,14},{7,15},{8,16},{9,17... | collective-permute-start | bytes 294920 | tf_op jit(solution)/shard_map/ppermute | solution.py:142
  182.4 5.8 collective-permute-done.17
  190.3 9.7 %collective-permute-done.20 = bf16[32,1536]{1,0:T(8,128)(2,1)S(1)} collective-permute-done((bf16[32,1536]{1,0:T(8,128)(2,1)S(1)}, bf16[32,1536]{1,0:T(8,128)(2,1)S(1)}, u32[]{:S(2)}, u32[]{:S(2)}) %collective-permute-start.20) | collective-permute-done | bytes 98336 | tf_op jit(solution)/shard_map/ppermute | solution.py:142
  200.9 3.1 multiply_convert_fusion.7
  206.3 14.5 %collective-permute-done.24 = bf16[128,1536]{1,0:T(8,128)(2,1)S(1)} collective-permute-done((bf16[128,1536]{1,0:T(8,128)(2,1)S(1)}, bf16[128,1536]{1,0:T(8,128)(2,1)S(1)}, u32[]{:S(2)}, u32[]{:S(2)}) %collective-permute-start.24) | collective-permute-done | bytes 393248 | tf_op jit(solution)/shard_map/ppermute | solution.py:142
  225.5 5.1 collective-permute-done.25
  232.0 10.8 %collective-permute-done.26 = bf16[32,1536]{1,0:T(8,128)(2,1)S(1)} collective-permute-done((bf16[32,1536]{1,0:T(8,128)(2,1)S(1)}, bf16[32,1536]{1,0:T(8,128)(2,1)S(1)}, u32[]{:S(2)}, u32[]{:S(2)}) %collective-permute-start.26) | collective-permute-done | bytes 98336 | tf_op jit(solution)/shard_map/ppermute | solution.py:142
  246.5 4.4 fusion.381
  251.5 2.7 collective-permute-start.28
  254.7 3.0 collective-permute-done.28
  257.7 3.8 collective-permute-start.47
  300.9 4.9 collective-permute-done.41
  305.8 5.1 collective-permute-done.42
  313.1 3.8 collective-permute-start.36
  325.9 3.1 collective-permute-start.34
  333.3 8.1 collective-permute-done.45
  348.4 3.1 multiply_convert_fusion.6
  352.3 3.3 convolution_convert_fusion.2.refs_1_
  355.7 4.5 add_convert_fusion.1
  363.1 8.3 %collective-permute-done.51 = bf16[128,1536]{1,0:T(8,128)(2,1)S(1)} collective-permute-done((bf16[128,1536]{1,0:T(8,128)(2,1)S(1)}, bf16[128,1536]{1,0:T(8,128)(2,1)S(1)}, u32[]{:S(2)}, u32[]{:S(2)}) %collective-permute-start.51) | collective-permute-done | bytes 393248 | tf_op jit(solution)/shard_map/ppermute | solution.py:142
  371.5 4.1 collective-permute-start.54
  379.3 4.1 collective-permute-done.53
  390.2 2.9 collective-permute-done.55
  408.9 3.1 fusion.15
  431.7 4.1 maximum_maximum_fusion
  436.9 5.1 collective-permute-done.56
  448.0 5.3 collective-permute-done.63
  453.4 6.2 collective-permute-done.62
  461.7 3.6 collective-permute-done.65
  467.5 4.5 add_convert_fusion
  474.3 5.5 fusion.20.refs_0_
  482.1 3.2 collective-permute-done.68
  485.4 8.1 collective-permute-start.69
  529.8 3.1 convolution_convert_fusion.4.refs_0_
  534.9 3.8 fusion.54
  553.4 9.7 %fusion.368 = (f32[1024]{0:T(1024)S(1)}, f32[1024]{0:T(1024)S(1)}, f32[1024,1536]{1,0:T(8,128)S(1)}) fusion(bf16[1024,1536]{1,0:T(8,128)(2,1)} %fusion.4, f32[1024,1536]{1,0:T(8,128)} %fusion.20.refs_0_, bf16[512,1536]{1,0:T(8,128)(2,1)} %get-tuple-element.211, bf16[512,1536]{1,0:T(8,128)(2,1)} %copy-done.73, bf16[]{:T(256)} %bitcast.93, ...), kind=kOutput, calls=%fused_computation.829 | convolution fusion | flops 3242719232 | bytes 20979714 | tf_op jit(solution)/shard_map/dot_general | solution.py:23
  565.6 2.7 copy-done.4
  592.3 25.5 %collective-permute-done.82.refs_0_ = bf16[4,192,896]{2,1,0:T(8,128)(2,1)} collective-permute-done((bf16[4,192,896]{2,1,0:T(8,128)(2,1)}, bf16[4,192,896]{2,1,0:T(8,128)(2,1)}, u32[]{:S(2)}, u32[]{:S(2)}) %collective-permute-start.82) | collective-permute-done | bytes 1376288 | tf_op jit(solution)/shard_map/ppermute | solution.py:142
  619.0 3.2 fusion.370
  636.2 2.8 fusion.361
  640.8 14.2 %collective-permute-done.84.refs_6_ = bf16[192,896]{1,0:T(8,128)(2,1)S(1)} collective-permute-done((bf16[192,896]{1,0:T(8,128)(2,1)}, bf16[192,896]{1,0:T(8,128)(2,1)S(1)}, u32[]{:S(2)}, u32[]{:S(2)}) %collective-permute-start.84) | collective-permute-done | bytes 344096 | tf_op jit(solution)/shard_map/ppermute | solution.py:142
  658.7 3.0 fusion.369
  682.1 2.9 collective-permute-done.98
  685.9 8.9 %collective-permute-done.99 = bf16[2,96,768]{2,1,0:T(8,128)(2,1)} collective-permute-done((bf16[2,96,768]{2,1,0:T(8,128)(2,1)}, bf16[2,96,768]{2,1,0:T(8,128)(2,1)}, u32[]{:S(2)}, u32[]{:S(2)}) %collective-permute-start.99) | collective-permute-done | bytes 294944 | tf_op jit(solution)/shard_map/ppermute | solution.py:142
  694.8 13.3 %collective-permute-start.94 = (bf16[192,768]{1,0:T(8,128)(2,1)}, bf16[192,768]{1,0:T(8,128)(2,1)}, u32[]{:S(2)}, u32[]{:S(2)}) collective-permute-start(bf16[192,768]{1,0:T(8,128)(2,1)} %get-tuple-element.274), channel_id=1, source_target_pairs={{0,16},{1,17},{2,18},{3,19},{4,20},{5,21},{6,22},{7,23},{8,24},{9,... | collective-permute-start | bytes 884744 | tf_op jit(solution)/shard_map/ppermute | solution.py:142
  716.9 3.7 collective-permute-done.101
  723.6 7.1 collective-permute-start.79
  740.8 2.7 convert_add_fusion
  746.1 18.9 %collective-permute-done.90 = bf16[32,768]{1,0:T(8,128)(2,1)S(1)} collective-permute-done((bf16[32,768]{1,0:T(8,128)(2,1)S(1)}, bf16[32,768]{1,0:T(8,128)(2,1)S(1)}, u32[]{:S(2)}, u32[]{:S(2)}) %collective-permute-start.90) | collective-permute-done | bytes 49184 | tf_op jit(solution)/shard_map/ppermute | solution.py:142
  790.8 2.7 pad_maximum_fusion
  793.5 6.8 maximum_convert_fusion.1
  800.3 6.7 maximum_convert_fusion
  (1065 shorter events, 370.4 us)
Async XLA Ops:
  7.2 115.1 %all-gather.20.cloned.1.call-start = ((), (), s32[]{:S(2)}) async-start(), calls=%async_computation.15 | async-start | bytes 2654208 | tf_op jit(solution)/shard_map/all_gather | solution.py:341
  15.4 57.5 %collective-permute-start.8 = (bf16[192,896]{1,0:T(8,128)(2,1)}, bf16[192,896]{1,0:T(8,128)(2,1)}, u32[]{:S(2)}, u32[]{:S(2)}) collective-permute-start(bf16[192,896]{1,0:T(8,128)(2,1)} %pad_maximum_fusion.20), channel_id=1, source_target_pairs={{0,4},{1,5},{2,6},{3,7},{4,0},{5,1},{6,2},{7,3},{8,12},{9,13},{10,... | collective-permute-start | bytes 1032200 | tf_op jit(solution)/shard_map/ppermute | solution.py:142
  18.3 31.1 %collective-permute-start.4 = (bf16[192,896]{1,0:T(8,128)(2,1)}, bf16[192,896]{1,0:T(8,128)(2,1)S(1)}, u32[]{:S(2)}, u32[]{:S(2)}) collective-permute-start(bf16[192,896]{1,0:T(8,128)(2,1)} %pad_maximum_fusion.20), channel_id=1, source_target_pairs={{0,8},{1,9},{2,10},{3,11},{4,12},{5,13},{6,14},{7,15},{8,16},{9,17... | collective-permute-start | bytes 1032200 | tf_op jit(solution)/shard_map/ppermute | solution.py:142
  19.9 32.1 %collective-permute-start.3 = (bf16[192,896]{1,0:T(8,128)(2,1)}, bf16[192,896]{1,0:T(8,128)(2,1)}, u32[]{:S(2)}, u32[]{:S(2)}) collective-permute-start(bf16[192,896]{1,0:T(8,128)(2,1)} %pad_maximum_fusion.20), channel_id=1, source_target_pairs={{0,16},{1,17},{2,18},{3,19},{4,20},{5,21},{6,22},{7,23},{8,24},{9,... | collective-permute-start | bytes 1032200 | tf_op jit(solution)/shard_map/ppermute | solution.py:142
  22.5 29.6 %collective-permute-start.2 = (bf16[192,896]{1,0:T(8,128)(2,1)}, bf16[192,896]{1,0:T(8,128)(2,1)}, u32[]{:S(2)}, u32[]{:S(2)}) collective-permute-start(bf16[192,896]{1,0:T(8,128)(2,1)} %pad_maximum_fusion.20), channel_id=1, source_target_pairs={{0,24},{1,25},{2,26},{3,27},{4,28},{5,29},{6,30},{7,31},{8,0},{9,1... | collective-permute-start | bytes 1032200 | tf_op jit(solution)/shard_map/ppermute | solution.py:142
  24.5 15.0 %collective-permute-start = (bf16[2,64,384]{2,1,0:T(8,128)(2,1)}, bf16[2,64,384]{2,1,0:T(8,128)(2,1)}, u32[]{:S(2)}, u32[]{:S(2)}) collective-permute-start(bf16[2,64,384]{2,1,0:T(8,128)(2,1)} %get-tuple-element.356), channel_id=1, source_target_pairs={{0,1},{1,0},{2,3},{3,2},{4,5},{5,4},{6,7},{7,6},{8,9},{9,8},{10,11... | collective-permute-start | bytes 294920 | tf_op jit(solution)/shard_map/ppermute | solution.py:142
  27.0 217.0 %all-gather.10.cloned.1.call-start = ((), (), s32[]{:S(2)}) async-start(), calls=%async_computation.5 | async-start | bytes 5308416 | tf_op jit(solution)/shard_map/all_gather | solution.py:627
  56.0 25.3 %collective-permute-start.5 = (bf16[2,96,768]{2,1,0:T(8,128)(2,1)S(1)}, bf16[2,96,768]{2,1,0:T(8,128)(2,1)S(1)}, u32[]{:S(2)}, u32[]{:S(2)}) collective-permute-start(bf16[2,96,768]{2,1,0:T(8,128)(2,1)S(1)} %pad_maximum_fusion.23), channel_id=1, source_target_pairs={{0,8},{1,9},{2,10},{3,11},{4,12},{5,13},{6,14},{7,15},{8,16},{9,17... | collective-permute-start | bytes 884744 | tf_op jit(solution)/shard_map/ppermute | solution.py:142
  66.3 35.4 %collective-permute-start.6 = (bf16[2,96,768]{2,1,0:T(8,128)(2,1)S(1)}, bf16[2,96,768]{2,1,0:T(8,128)(2,1)S(1)}, u32[]{:S(2)}, u32[]{:S(2)}) collective-permute-start(bf16[2,96,768]{2,1,0:T(8,128)(2,1)S(1)} %pad_maximum_fusion.24), channel_id=1, source_target_pairs={{0,16},{1,17},{2,18},{3,19},{4,20},{5,21},{6,22},{7,23},{8,24},{9,... | collective-permute-start | bytes 884744 | tf_op jit(solution)/shard_map/ppermute | solution.py:142
  69.1 32.5 %collective-permute-start.9 = (bf16[3,192,896]{2,1,0:T(8,128)(2,1)S(1)}, bf16[3,192,896]{2,1,0:T(8,128)(2,1)S(1)}, u32[]{:S(2)}, u32[]{:S(2)}) collective-permute-start(bf16[3,192,896]{2,1,0:T(8,128)(2,1)S(1)} %pad_maximum_fusion.15), channel_id=1, source_target_pairs={{0,4},{1,5},{2,6},{3,7},{4,0},{5,1},{6,2},{7,3},{8,12},{9,13},{10,... | collective-permute-start | bytes 3096584 | tf_op jit(solution)/shard_map/ppermute | solution.py:142
  69.7 31.9 %collective-permute-start.7 = (bf16[2,96,768]{2,1,0:T(8,128)(2,1)S(1)}, bf16[2,96,768]{2,1,0:T(8,128)(2,1)S(1)}, u32[]{:S(2)}, u32[]{:S(2)}) collective-permute-start(bf16[2,96,768]{2,1,0:T(8,128)(2,1)S(1)} %pad_maximum_fusion.25), channel_id=1, source_target_pairs={{0,24},{1,25},{2,26},{3,27},{4,28},{5,29},{6,30},{7,31},{8,0},{9,1... | collective-permute-start | bytes 884744 | tf_op jit(solution)/shard_map/ppermute | solution.py:142
  130.3 369.6 %reduce-scatter.8.cloned.1.call-start = ((), (), s32[]{:S(2)}) async-start(), calls=%async_computation.7 | async-start | bytes 2949120 | tf_op jit(solution)/shard_map/reduce_scatter | solution.py:677
  131.4 15.8 %collective-permute-start.12 = (bf16[4,96,768]{2,1,0:T(8,128)(2,1)S(1)}, bf16[4,96,768]{2,1,0:T(8,128)(2,1)}, u32[]{:S(2)}, u32[]{:S(2)}) collective-permute-start(bf16[4,96,768]{2,1,0:T(8,128)(2,1)S(1)} %maximum_add_fusion.4), channel_id=1, source_target_pairs={{0,4},{1,5},{2,6},{3,7},{4,0},{5,1},{6,2},{7,3},{8,12},{9,13},{10,... | collective-permute-start | bytes 1769480 | tf_op jit(solution)/shard_map/ppermute | solution.py:142
  160.5 20.4 %collective-permute-start.18 = (bf16[32,1536]{1,0:T(8,128)(2,1)S(1)}, bf16[32,1536]{1,0:T(8,128)(2,1)S(1)}, u32[]{:S(2)}, u32[]{:S(2)}) collective-permute-start(bf16[32,1536]{1,0:T(8,128)(2,1)S(1)} %get-tuple-element.186), channel_id=1, source_target_pairs={{0,8},{1,9},{2,10},{3,11},{4,12},{5,13},{6,14},{7,15},{8,16},{9,17... | collective-permute-start | bytes 294920 | tf_op jit(solution)/shard_map/ppermute | solution.py:142
  175.8 12.3 %collective-permute-start.17 = (bf16[32,1536]{1,0:T(8,128)(2,1)S(1)}, bf16[32,1536]{1,0:T(8,128)(2,1)S(1)}, u32[]{:S(2)}, u32[]{:S(2)}) collective-permute-start(bf16[32,1536]{1,0:T(8,128)(2,1)S(1)} %get-tuple-element.186), channel_id=1, source_target_pairs={{0,16},{1,17},{2,18},{3,19},{4,20},{5,21},{6,22},{7,23},{8,24},{9,... | collective-permute-start | bytes 294920 | tf_op jit(solution)/shard_map/ppermute | solution.py:142
  176.4 13.3 %collective-permute-start.16 = (bf16[32,1536]{1,0:T(8,128)(2,1)S(1)}, bf16[32,1536]{1,0:T(8,128)(2,1)S(1)}, u32[]{:S(2)}, u32[]{:S(2)}) collective-permute-start(bf16[32,1536]{1,0:T(8,128)(2,1)S(1)} %get-tuple-element.186), channel_id=1, source_target_pairs={{0,24},{1,25},{2,26},{3,27},{4,28},{5,29},{6,30},{7,31},{8,0},{9,1... | collective-permute-start | bytes 294920 | tf_op jit(solution)/shard_map/ppermute | solution.py:142
  179.5 20.5 %collective-permute-start.23 = (bf16[8,96,768]{2,1,0:T(8,128)(2,1)S(1)}, bf16[8,96,768]{2,1,0:T(8,128)(2,1)S(1)}, u32[]{:S(2)}, u32[]{:S(2)}) collective-permute-start(bf16[8,96,768]{2,1,0:T(8,128)(2,1)S(1)} %slice_dynamic-update-slice_fusion.3), channel_id=1, source_target_pairs={{0,1},{1,0},{2,3},{3,2},{4,5},{5,4},{6,7},{7,6},{8,9},{9,8},{10,11... | collective-permute-start | bytes 3538952 | tf_op jit(solution)/shard_map/ppermute | solution.py:142
  181.0 19.0 %collective-permute-start.22 = (bf16[32,1536]{1,0:T(8,128)(2,1)S(1)}, bf16[32,1536]{1,0:T(8,128)(2,1)S(1)}, u32[]{:S(2)}, u32[]{:S(2)}) collective-permute-start(bf16[32,1536]{1,0:T(8,128)(2,1)S(1)} %collective-permute-done.18), channel_id=1, source_target_pairs={{0,4},{1,5},{2,6},{3,7},{4,0},{5,1},{6,2},{7,3},{8,12},{9,13},{10,... | collective-permute-start | bytes 294920 | tf_op jit(solution)/shard_map/ppermute | solution.py:142
  204.8 16.0 %collective-permute-start.24 = (bf16[128,1536]{1,0:T(8,128)(2,1)S(1)}, bf16[128,1536]{1,0:T(8,128)(2,1)S(1)}, u32[]{:S(2)}, u32[]{:S(2)}) collective-permute-start(bf16[128,1536]{1,0:T(8,128)(2,1)S(1)} %slice.1327), channel_id=1, source_target_pairs={{0,4},{1,5},{2,6},{3,7},{4,0},{5,1},{6,2},{7,3},{8,12},{9,13},{10,... | collective-permute-start | bytes 1179656 | tf_op jit(solution)/shard_map/ppermute | solution.py:142
  224.9 17.9 %collective-permute-start.26 = (bf16[32,1536]{1,0:T(8,128)(2,1)S(1)}, bf16[32,1536]{1,0:T(8,128)(2,1)S(1)}, u32[]{:S(2)}, u32[]{:S(2)}) collective-permute-start(bf16[32,1536]{1,0:T(8,128)(2,1)S(1)} %get-tuple-element.332), channel_id=1, source_target_pairs={{0,16},{1,17},{2,18},{3,19},{4,20},{5,21},{6,22},{7,23},{8,24},{9,... | collective-permute-start | bytes 294920 | tf_op jit(solution)/shard_map/ppermute | solution.py:142
  246.5 70.4 %collective-permute-start.49 = (bf16[32,1536]{1,0:T(8,128)(2,1)}, bf16[32,1536]{1,0:T(8,128)(2,1)}, u32[]{:S(2)}, u32[]{:S(2)}) collective-permute-start(bf16[32,1536]{1,0:T(8,128)(2,1)} %add_bitcast_fusion), channel_id=1, source_target_pairs={{0,8},{1,9},{2,10},{3,11},{4,12},{5,13},{6,14},{7,15},{8,16},{9,17... | collective-permute-start | bytes 294920 | tf_op jit(solution)/shard_map/ppermute | solution.py:142
  246.5 72.8 %collective-permute-start.48 = (bf16[32,1536]{1,0:T(8,128)(2,1)}, bf16[32,1536]{1,0:T(8,128)(2,1)}, u32[]{:S(2)}, u32[]{:S(2)}) collective-permute-start(bf16[32,1536]{1,0:T(8,128)(2,1)} %add_bitcast_fusion), channel_id=1, source_target_pairs={{0,16},{1,17},{2,18},{3,19},{4,20},{5,21},{6,22},{7,23},{8,24},{9,... | collective-permute-start | bytes 294920 | tf_op jit(solution)/shard_map/ppermute | solution.py:142
  257.7 61.6 %collective-permute-start.47 = (bf16[32,1536]{1,0:T(8,128)(2,1)}, bf16[32,1536]{1,0:T(8,128)(2,1)}, u32[]{:S(2)}, u32[]{:S(2)}) collective-permute-start(bf16[32,1536]{1,0:T(8,128)(2,1)} %add_bitcast_fusion), channel_id=1, source_target_pairs={{0,24},{1,25},{2,26},{3,27},{4,28},{5,29},{6,30},{7,31},{8,0},{9,1... | collective-permute-start | bytes 294920 | tf_op jit(solution)/shard_map/ppermute | solution.py:142
  261.8 24.7 %collective-permute-start.32 = (bf16[768,768]{1,0:T(8,128)(2,1)S(1)}, bf16[768,768]{1,0:T(8,128)(2,1)}, u32[]{:S(2)}, u32[]{:S(2)}) collective-permute-start(bf16[768,768]{1,0:T(8,128)(2,1)S(1)} %pad_maximum_fusion.10), channel_id=1, source_target_pairs={{0,1},{1,0},{2,3},{3,2},{4,5},{5,4},{6,7},{7,6},{8,9},{9,8},{10,11... | collective-permute-start | bytes 3538952 | tf_op jit(solution)/shard_map/ppermute | solution.py:142
  265.5 16.3 %collective-permute-start.31 = (bf16[1536,384]{1,0:T(8,128)(2,1)}, bf16[1536,384]{1,0:T(8,128)(2,1)}, u32[]{:S(2)}, u32[]{:S(2)}) collective-permute-start(bf16[1536,384]{1,0:T(8,128)(2,1)} %bitcast.52), channel_id=1, source_target_pairs={{0,1},{1,0},{2,3},{3,2},{4,5},{5,4},{6,7},{7,6},{8,9},{9,8},{10,11... | collective-permute-start | bytes 3538952 | tf_op jit(solution)/shard_map/ppermute | solution.py:142
  298.5 12.5 %collective-permute-start.42 = (bf16[2,48,768]{2,1,0:T(8,128)(2,1)S(1)}, bf16[2,48,768]{2,1,0:T(8,128)(2,1)S(1)}, u32[]{:S(2)}, u32[]{:S(2)}) collective-permute-start(bf16[2,48,768]{2,1,0:T(8,128)(2,1)S(1)} %pad_maximum_fusion.33), channel_id=1, source_target_pairs={{0,16},{1,17},{2,18},{3,19},{4,20},{5,21},{6,22},{7,23},{8,24},{9,... | collective-permute-start | bytes 442376 | tf_op jit(solution)/shard_map/ppermute | solution.py:142
  312.3 18.6 %collective-permute-start.44 = (bf16[4,48,768]{2,1,0:T(8,128)(2,1)S(1)}, bf16[4,48,768]{2,1,0:T(8,128)(2,1)S(1)}, u32[]{:S(2)}, u32[]{:S(2)}) collective-permute-start(bf16[4,48,768]{2,1,0:T(8,128)(2,1)S(1)} %maximum_add_fusion.8), channel_id=1, source_target_pairs={{0,4},{1,5},{2,6},{3,7},{4,0},{5,1},{6,2},{7,3},{8,12},{9,13},{10,... | collective-permute-start | bytes 884744 | tf_op jit(solution)/shard_map/ppermute | solution.py:142
  313.1 12.8 %collective-permute-start.36 = (bf16[32,1536]{1,0:T(8,128)(2,1)}, bf16[32,1536]{1,0:T(8,128)(2,1)}, u32[]{:S(2)}, u32[]{:S(2)}) collective-permute-start(bf16[32,1536]{1,0:T(8,128)(2,1)} %get-tuple-element.178), channel_id=1, source_target_pairs={{0,8},{1,9},{2,10},{3,11},{4,12},{5,13},{6,14},{7,15},{8,16},{9,17... | collective-permute-start | bytes 294920 | tf_op jit(solution)/shard_map/ppermute | solution.py:142
  316.9 12.1 %collective-permute-start.35 = (bf16[32,1536]{1,0:T(8,128)(2,1)}, bf16[32,1536]{1,0:T(8,128)(2,1)}, u32[]{:S(2)}, u32[]{:S(2)}) collective-permute-start(bf16[32,1536]{1,0:T(8,128)(2,1)} %get-tuple-element.178), channel_id=1, source_target_pairs={{0,16},{1,17},{2,18},{3,19},{4,20},{5,21},{6,22},{7,23},{8,24},{9,... | collective-permute-start | bytes 294920 | tf_op jit(solution)/shard_map/ppermute | solution.py:142
  323.7 27.8 %collective-permute-start.50 = (bf16[128,1536]{1,0:T(8,128)(2,1)}, bf16[128,1536]{1,0:T(8,128)(2,1)}, u32[]{:S(2)}, u32[]{:S(2)}) collective-permute-start(bf16[128,1536]{1,0:T(8,128)(2,1)} %maximum_add_fusion.7), channel_id=1, source_target_pairs={{0,4},{1,5},{2,6},{3,7},{4,0},{5,1},{6,2},{7,3},{8,12},{9,13},{10,... | collective-permute-start | bytes 1179656 | tf_op jit(solution)/shard_map/ppermute | solution.py:142
  325.8 17.6 %collective-permute-start.37 = (bf16[32,1536]{1,0:T(8,128)(2,1)}, bf16[32,1536]{1,0:T(8,128)(2,1)S(1)}, u32[]{:S(2)}, u32[]{:S(2)}) collective-permute-start(bf16[32,1536]{1,0:T(8,128)(2,1)} %get-tuple-element.178), channel_id=1, source_target_pairs={{0,4},{1,5},{2,6},{3,7},{4,0},{5,1},{6,2},{7,3},{8,12},{9,13},{10,... | collective-permute-start | bytes 294920 | tf_op jit(solution)/shard_map/ppermute | solution.py:142
  329.0 17.1 %collective-permute-start.40 = (bf16[32,1536]{1,0:T(8,128)(2,1)}, bf16[32,1536]{1,0:T(8,128)(2,1)S(1)}, u32[]{:S(2)}, u32[]{:S(2)}) collective-permute-start(bf16[32,1536]{1,0:T(8,128)(2,1)} %collective-permute-done.36), channel_id=1, source_target_pairs={{0,4},{1,5},{2,6},{3,7},{4,0},{5,1},{6,2},{7,3},{8,12},{9,13},{10,... | collective-permute-start | bytes 294920 | tf_op jit(solution)/shard_map/ppermute | solution.py:142
  330.9 15.1 %collective-permute-start.39 = (bf16[32,1536]{1,0:T(8,128)(2,1)}, bf16[32,1536]{1,0:T(8,128)(2,1)S(1)}, u32[]{:S(2)}, u32[]{:S(2)}) collective-permute-start(bf16[32,1536]{1,0:T(8,128)(2,1)} %collective-permute-done.35), channel_id=1, source_target_pairs={{0,4},{1,5},{2,6},{3,7},{4,0},{5,1},{6,2},{7,3},{8,12},{9,13},{10,... | collective-permute-start | bytes 294920 | tf_op jit(solution)/shard_map/ppermute | solution.py:142
  355.6 144.3 %reduce-scatter.6.cloned.1.call-start = ((), (), s32[]{:S(2)}) async-start(), calls=%async_computation.6 | async-start | bytes 2949120 | tf_op jit(solution)/shard_map/reduce_scatter | solution.py:677
  389.9 191.1 %reduce-scatter.10.cloned.1.call-start = ((), (), s32[]{:S(2)}) async-start(), calls=%async_computation.8 | async-start | bytes 5308416 | tf_op jit(solution)/shard_map/reduce_scatter | solution.py:699
  435.8 156.5 %reduce-scatter.12.cloned.1.call-start = ((), (), s32[]{:S(2)}) async-start(), calls=%async_computation.9 | async-start | bytes 2949120 | tf_op jit(solution)/shard_map/reduce_scatter | solution.py:677
  443.8 15.8 %collective-permute-start.62 = (bf16[32,1536]{1,0:T(8,128)(2,1)S(1)}, bf16[32,1536]{1,0:T(8,128)(2,1)S(1)}, u32[]{:S(2)}, u32[]{:S(2)}) collective-permute-start(bf16[32,1536]{1,0:T(8,128)(2,1)S(1)} %get-tuple-element.172), channel_id=1, source_target_pairs={{0,16},{1,17},{2,18},{3,19},{4,20},{5,21},{6,22},{7,23},{8,24},{9,... | collective-permute-start | bytes 294920 | tf_op jit(solution)/shard_map/ppermute | solution.py:142
  445.8 13.8 %collective-permute-start.61 = (bf16[32,1536]{1,0:T(8,128)(2,1)S(1)}, bf16[32,1536]{1,0:T(8,128)(2,1)S(1)}, u32[]{:S(2)}, u32[]{:S(2)}) collective-permute-start(bf16[32,1536]{1,0:T(8,128)(2,1)S(1)} %get-tuple-element.172), channel_id=1, source_target_pairs={{0,24},{1,25},{2,26},{3,27},{4,28},{5,29},{6,30},{7,31},{8,0},{9,1... | collective-permute-start | bytes 294920 | tf_op jit(solution)/shard_map/ppermute | solution.py:142
  447.6 14.0 %collective-permute-start.64 = (bf16[32,1536]{1,0:T(8,128)(2,1)S(1)}, bf16[32,1536]{1,0:T(8,128)(2,1)S(1)}, u32[]{:S(2)}, u32[]{:S(2)}) collective-permute-start(bf16[32,1536]{1,0:T(8,128)(2,1)S(1)} %get-tuple-element.172), channel_id=1, source_target_pairs={{0,4},{1,5},{2,6},{3,7},{4,0},{5,1},{6,2},{7,3},{8,12},{9,13},{10,... | collective-permute-start | bytes 294920 | tf_op jit(solution)/shard_map/ppermute | solution.py:142
  453.3 12.0 %collective-permute-start.67 = (bf16[32,1536]{1,0:T(8,128)(2,1)S(1)}, bf16[32,1536]{1,0:T(8,128)(2,1)S(1)}, u32[]{:S(2)}, u32[]{:S(2)}) collective-permute-start(bf16[32,1536]{1,0:T(8,128)(2,1)S(1)} %collective-permute-done.63), channel_id=1, source_target_pairs={{0,4},{1,5},{2,6},{3,7},{4,0},{5,1},{6,2},{7,3},{8,12},{9,13},{10,... | collective-permute-start | bytes 294920 | tf_op jit(solution)/shard_map/ppermute | solution.py:142
  472.9 12.4 %collective-permute-start.68 = (bf16[128,1536]{1,0:T(8,128)(2,1)S(1)}, bf16[128,1536]{1,0:T(8,128)(2,1)S(1)}, u32[]{:S(2)}, u32[]{:S(2)}) collective-permute-start(bf16[128,1536]{1,0:T(8,128)(2,1)S(1)} %slice.1325), channel_id=1, source_target_pairs={{0,4},{1,5},{2,6},{3,7},{4,0},{5,1},{6,2},{7,3},{8,12},{9,13},{10,... | collective-permute-start | bytes 1179656 | tf_op jit(solution)/shard_map/ppermute | solution.py:142
  515.6 13.7 %collective-permute-start.73 = (bf16[256,1536]{1,0:T(8,128)(2,1)}, bf16[256,1536]{1,0:T(8,128)(2,1)}, u32[]{:S(2)}, u32[]{:S(2)}) collective-permute-start(bf16[256,1536]{1,0:T(8,128)(2,1)} %slice_add_fusion.6), channel_id=1, source_target_pairs={{0,1},{1,0},{2,3},{3,2},{4,5},{5,4},{6,7},{7,6},{8,9},{9,8},{10,11... | collective-permute-start | bytes 2359304 | tf_op jit(solution)/shard_map/ppermute | solution.py:142
  516.1 110.7 %all-gather.22.cloned.1.call-start = ((), (), s32[]{:S(2)}) async-start(), calls=%async_computation.16 | async-start | bytes 2949120 | tf_op jit(solution)/shard_map/all_gather | solution.py:732
  581.6 59.2 %reduce-scatter.14.cloned.1.call-start = ((), (), s32[]{:S(2)}) async-start(), calls=%async_computation.10 | async-start | bytes 2949120 | tf_op jit(solution)/shard_map/reduce_scatter | solution.py:677
  582.3 211.2 %all-gather.18.cloned.1.call-start = ((), (), s32[]{:S(2)}) async-start(), calls=%async_computation.14 | async-start | bytes 2949120 | tf_op jit(solution)/shard_map/all_gather | solution.py:733
  584.5 33.3 %collective-permute-start.82 = (bf16[4,192,896]{2,1,0:T(8,128)(2,1)}, bf16[4,192,896]{2,1,0:T(8,128)(2,1)}, u32[]{:S(2)}, u32[]{:S(2)}) collective-permute-start(bf16[4,192,896]{2,1,0:T(8,128)(2,1)} %dynamic-slice_bitcast_fusion.1), channel_id=1, source_target_pairs={{0,4},{1,5},{2,6},{3,7},{4,0},{5,1},{6,2},{7,3},{8,12},{9,13},{10,... | collective-permute-start | bytes 4128776 | tf_op jit(solution)/shard_map/ppermute | solution.py:142
  591.6 67.0 %collective-permute-start.92 = (bf16[4,192,768]{2,1,0:T(8,128)(2,1)}, bf16[4,192,768]{2,1,0:T(8,128)(2,1)}, u32[]{:S(2)}, u32[]{:S(2)}) collective-permute-start(bf16[4,192,768]{2,1,0:T(8,128)(2,1)} %fusion.89), channel_id=1, source_target_pairs={{0,4},{1,5},{2,6},{3,7},{4,0},{5,1},{6,2},{7,3},{8,12},{9,13},{10,... | collective-permute-start | bytes 3538952 | tf_op jit(solution)/shard_map/ppermute | solution.py:142
  592.3 201.3 %all-gather.16.cloned.1.call-start = ((), (), s32[]{:S(2)}) async-start(), calls=%async_computation.13 | async-start | bytes 2949120 | tf_op jit(solution)/shard_map/all_gather | solution.py:745
  623.2 17.6 %collective-permute-start.85 = (bf16[192,896]{1,0:T(8,128)(2,1)}, bf16[192,896]{1,0:T(8,128)(2,1)S(1)}, u32[]{:S(2)}, u32[]{:S(2)}) collective-permute-start(bf16[192,896]{1,0:T(8,128)(2,1)} %get-tuple-element.254), channel_id=1, source_target_pairs={{0,24},{1,25},{2,26},{3,27},{4,28},{5,29},{6,30},{7,31},{8,0},{9,1... | collective-permute-start | bytes 1032200 | tf_op jit(solution)/shard_map/ppermute | solution.py:142
  625.7 29.3 %collective-permute-start.84 = (bf16[192,896]{1,0:T(8,128)(2,1)}, bf16[192,896]{1,0:T(8,128)(2,1)S(1)}, u32[]{:S(2)}, u32[]{:S(2)}) collective-permute-start(bf16[192,896]{1,0:T(8,128)(2,1)} %get-tuple-element.255), channel_id=1, source_target_pairs={{0,16},{1,17},{2,18},{3,19},{4,20},{5,21},{6,22},{7,23},{8,24},{9,... | collective-permute-start | bytes 1032200 | tf_op jit(solution)/shard_map/ppermute | solution.py:142
  625.7 29.3 %collective-permute-start.83 = (bf16[192,896]{1,0:T(8,128)(2,1)S(1)}, bf16[192,896]{1,0:T(8,128)(2,1)S(1)}, u32[]{:S(2)}, u32[]{:S(2)}) collective-permute-start(bf16[192,896]{1,0:T(8,128)(2,1)S(1)} %get-tuple-element.256), channel_id=1, source_target_pairs={{0,8},{1,9},{2,10},{3,11},{4,12},{5,13},{6,14},{7,15},{8,16},{9,17... | collective-permute-start | bytes 1032200 | tf_op jit(solution)/shard_map/ppermute | solution.py:142
  656.4 143.9 %all-gather.14.cloned.1.call-start = ((), (), s32[]{:S(2)}) async-start(), calls=%async_computation.12 | async-start | bytes 2949120 | tf_op jit(solution)/shard_map/all_gather | solution.py:764
  657.1 83.6 %collective-permute-start.88 = (bf16[1024,768]{1,0:T(8,128)(2,1)}, bf16[1024,768]{1,0:T(8,128)(2,1)}, u32[]{:S(2)}, u32[]{:S(2)}) collective-permute-start(bf16[1024,768]{1,0:T(8,128)(2,1)} %get-tuple-element.118), channel_id=1, source_target_pairs={{0,2},{1,3},{2,0},{3,1},{4,6},{5,7},{6,4},{7,5},{8,10},{9,11},{10,... | collective-permute-start | bytes 4718600 | tf_op jit(solution)/shard_map/ppermute | solution.py:142
  662.7 68.1 %collective-permute-start.93 = (bf16[192,768]{1,0:T(8,128)(2,1)}, bf16[192,768]{1,0:T(8,128)(2,1)}, u32[]{:S(2)}, u32[]{:S(2)}) collective-permute-start(bf16[192,768]{1,0:T(8,128)(2,1)} %get-tuple-element.272), channel_id=1, source_target_pairs={{0,8},{1,9},{2,10},{3,11},{4,12},{5,13},{6,14},{7,15},{8,16},{9,17... | collective-permute-start | bytes 884744 | tf_op jit(solution)/shard_map/ppermute | solution.py:142
  672.9 12.2 %collective-permute-start.98 = (bf16[2,96,768]{2,1,0:T(8,128)(2,1)}, bf16[2,96,768]{2,1,0:T(8,128)(2,1)}, u32[]{:S(2)}, u32[]{:S(2)}) collective-permute-start(bf16[2,96,768]{2,1,0:T(8,128)(2,1)} %pad_maximum_fusion.27), channel_id=1, source_target_pairs={{0,8},{1,9},{2,10},{3,11},{4,12},{5,13},{6,14},{7,15},{8,16},{9,17... | collective-permute-start | bytes 884744 | tf_op jit(solution)/shard_map/ppermute | solution.py:142
  676.1 18.8 %collective-permute-start.99 = (bf16[2,96,768]{2,1,0:T(8,128)(2,1)}, bf16[2,96,768]{2,1,0:T(8,128)(2,1)}, u32[]{:S(2)}, u32[]{:S(2)}) collective-permute-start(bf16[2,96,768]{2,1,0:T(8,128)(2,1)} %pad_maximum_fusion.28), channel_id=1, source_target_pairs={{0,16},{1,17},{2,18},{3,19},{4,20},{5,21},{6,22},{7,23},{8,24},{9,... | collective-permute-start | bytes 884744 | tf_op jit(solution)/shard_map/ppermute | solution.py:142
  678.7 30.4 %collective-permute-start.100 = (bf16[2,96,768]{2,1,0:T(8,128)(2,1)}, bf16[2,96,768]{2,1,0:T(8,128)(2,1)}, u32[]{:S(2)}, u32[]{:S(2)}) collective-permute-start(bf16[2,96,768]{2,1,0:T(8,128)(2,1)} %pad_maximum_fusion.29), channel_id=1, source_target_pairs={{0,24},{1,25},{2,26},{3,27},{4,28},{5,29},{6,30},{7,31},{8,0},{9,1... | collective-permute-start | bytes 884744 | tf_op jit(solution)/shard_map/ppermute | solution.py:142
  685.0 45.9 %collective-permute-start.95 = (bf16[192,768]{1,0:T(8,128)(2,1)}, bf16[192,768]{1,0:T(8,128)(2,1)}, u32[]{:S(2)}, u32[]{:S(2)}) collective-permute-start(bf16[192,768]{1,0:T(8,128)(2,1)} %get-tuple-element.273), channel_id=1, source_target_pairs={{0,24},{1,25},{2,26},{3,27},{4,28},{5,29},{6,30},{7,31},{8,0},{9,1... | collective-permute-start | bytes 884744 | tf_op jit(solution)/shard_map/ppermute | solution.py:142
  694.8 37.6 %collective-permute-start.94 = (bf16[192,768]{1,0:T(8,128)(2,1)}, bf16[192,768]{1,0:T(8,128)(2,1)}, u32[]{:S(2)}, u32[]{:S(2)}) collective-permute-start(bf16[192,768]{1,0:T(8,128)(2,1)} %get-tuple-element.274), channel_id=1, source_target_pairs={{0,16},{1,17},{2,18},{3,19},{4,20},{5,21},{6,22},{7,23},{8,24},{9,... | collective-permute-start | bytes 884744 | tf_op jit(solution)/shard_map/ppermute | solution.py:142
  723.6 76.7 %all-gather.12.cloned.1.call-start = ((), (), s32[]{:S(2)}) async-start(), calls=%async_computation.11 | async-start | bytes 2949120 | tf_op jit(solution)/shard_map/all_gather | solution.py:764
  739.4 25.6 %collective-permute-start.96 = (bf16[192,1664]{1,0:T(8,128)(2,1)S(1)}, bf16[192,1664]{1,0:T(8,128)(2,1)S(1)}, u32[]{:S(2)}, u32[]{:S(2)}) collective-permute-start(bf16[192,1664]{1,0:T(8,128)(2,1)S(1)} %get-tuple-element.302), channel_id=1, source_target_pairs={{0,2},{1,3},{2,0},{3,1},{4,6},{5,7},{6,4},{7,5},{8,10},{9,11},{10,... | collective-permute-start | bytes 1916936 | tf_op jit(solution)/shard_map/ppermute | solution.py:142
  744.6 20.4 %collective-permute-start.90 = (bf16[32,768]{1,0:T(8,128)(2,1)S(1)}, bf16[32,768]{1,0:T(8,128)(2,1)S(1)}, u32[]{:S(2)}, u32[]{:S(2)}) collective-permute-start(bf16[32,768]{1,0:T(8,128)(2,1)S(1)} %dynamic-slice_convert_fusion.3), channel_id=1, source_target_pairs={{0,2},{1,3},{2,0},{3,1},{4,6},{5,7},{6,4},{7,5},{8,10},{9,11},{10,... | collective-permute-start | bytes 147464 | tf_op jit(solution)/shard_map/ppermute | solution.py:142
  745.4 27.8 %collective-permute-start.89 = (bf16[1024,384]{1,0:T(8,128)(2,1)}, bf16[1024,384]{1,0:T(8,128)(2,1)}, u32[]{:S(2)}, u32[]{:S(2)}) collective-permute-start(bf16[1024,384]{1,0:T(8,128)(2,1)} %dynamic-slice_convert_fusion.1), channel_id=1, source_target_pairs={{0,1},{1,0},{2,3},{3,2},{4,5},{5,4},{6,7},{7,6},{8,9},{9,8},{10,11... | collective-permute-start | bytes 2359304 | tf_op jit(solution)/shard_map/ppermute | solution.py:142
  745.5 21.4 %collective-permute-start.87 = (bf16[64,384]{1,0:T(8,128)(2,1)S(1)}, bf16[64,384]{1,0:T(8,128)(2,1)S(1)}, u32[]{:S(2)}, u32[]{:S(2)}) collective-permute-start(bf16[64,384]{1,0:T(8,128)(2,1)S(1)} %get-tuple-element.364), channel_id=1, source_target_pairs={{0,1},{1,0},{2,3},{3,2},{4,5},{5,4},{6,7},{7,6},{8,9},{9,8},{10,11... | collective-permute-start | bytes 147464 | tf_op jit(solution)/shard_map/ppermute | solution.py:142
  (273 other events, 1751.9 us)
Sparse Core Ops, SparseCore 0:
  27.1 79.3 all-gather.19
  130.5 113.4 all-gather.9
  355.8 34.3 reduce-scatter.7
  393.2 35.1 reduce-scatter.5
  436.0 102.3 reduce-scatter.9
  541.3 34.9 reduce-scatter.11
  581.7 23.2 all-gather.21
  607.7 33.0 reduce-scatter.13
  642.4 30.2 all-gather.17
  674.0 38.7 all-gather.15
  723.7 39.5 all-gather.13
  771.8 24.6 all-gather.11

commit v3 on v2

--- a/solution.py
+++ b/solution.py
@@ -224,8 +224,8 @@
         return got
 
     def trade_far(self, got, zero):
-        far = later(jnp.stack([pair[1] for pair in got]), zero)
-        return [pair[0] for pair in got], self.send(far, self.swap_x)
+        far = jnp.stack([at(pair, 1 + zero.index) for pair in got])
+        return [at(pair, zero.index) for pair in got], self.send(far, self.swap_x)
 
     def trade_order(self):
         n = self.depth
@@ -235,16 +235,17 @@
         mine = jnp.stack([blocks(d) for d in range(self.dp)])
         return lax.all_to_all(mine, "dp", 0, 0, tiled=True)
 
-    def spread(self, rows, fill):
-        half = rows.shape[1] // 2
-        got = self.near_y(cut(rows, half * (1 - self.y), half).astype(bf16)).astype(fill)
-        mine = cut(rows, half * self.y, half).astype(fill)
-        return self.spread_c(self.by_y(mine, got, 0))
+    def spread(self, rows):
+        half = rows.shape[2] // 2
+        got = self.near_y(cut(rows, half * (1 - self.y), half, 2).astype(bf16)).astype(f32)
+        return self.spread_c(self.by_y(cut(rows, half * self.y, half, 2), got, 1))
 
     def spread_c(self, cols):
-        half = cols.shape[1] // 2
-        got = self.near_c(cut(cols, half * (1 - self.c), half).astype(bf16)).astype(cols.dtype)
-        return self.by_c(cut(cols, half * self.c, half)[None], got[None], 0)
+        axis = cols.ndim - 1
+        half = cols.shape[axis] // 2
+        got = self.near_c(cut(cols, half * (1 - self.c), half, axis).astype(bf16))
+        mine = cut(cols, half * self.c, half, axis)
+        return self.by_c(mine[None], got.astype(cols.dtype)[None], 0)
 
 
 def expand(value, heads):
@@ -340,6 +341,8 @@
             out_piece = jnp.concatenate([out_piece[..., :quarter], out_piece[..., quarter:]], 1)
             second = lax.all_gather(jnp.stack([picked[0, 2], out_piece[0]]), "dp", axis=1)
             zero, _ = gate(first[1:])
+            piece = jnp.concatenate([picked[1], out_piece[1][None]], 0)
+            rest = lax.all_gather(later(piece, zero), "dp", axis=1)
             inner0 = wires.trade_near(inner_block(0, 2, c, zero.index))
             first = wires.gather_far(first)
             first = [first[:, :, i * quarter : (i + 1) * quarter] for i in range(2)] + [
@@ -542,14 +545,13 @@
             left = jnp.concatenate([attn["ds"], attn["low"]], 0)
             return left, jnp.concatenate([attn["key_g"], attn["val_g"]], 0)
 
-        def outputs(x_low, grad, media_grad, attn_out, ffn_out, sums):
+        def outputs(x_low, grad, media_grad, outs, sums):
             sums = sums.reshape(layers, 2, 3, shard)
-            outs = [jnp.stack([attn_out[level][i] for level in range(layers)]) for i in range(3)]
-            outs += [jnp.stack([ffn_out[level][i] for level in range(layers)]) for i in range(2)]
+            both = wires.spread(jnp.stack([x_low.astype(f32), grad]))
             return (
-                wires.spread(x_low, bf16),
+                both[:, 0].astype(bf16),
                 media_grad,
-                wires.spread(grad, f32),
+                both[:, 1],
                 *outs,
                 sums[:, 0, :2],
                 sums[:, 1, :2],
@@ -617,14 +619,14 @@
             media_grad = wires.spread_c(cut(d_media, half * y, half) + got.astype(f32))
             extra = lax.psum(jnp.stack(vector_grads), "section")
             sums = lax.psum_scatter(extra, "dp", scatter_dimension=1, tiled=True)
-            return outputs(x_low, grad, media_grad, attn_out, ffn_out, sums)
+            outs = [jnp.stack([attn_out[level][i] for level in range(layers)]) for i in range(3)]
+            outs += [jnp.stack([ffn_out[level][i] for level in range(layers)]) for i in range(2)]
+            return outputs(x_low, grad, media_grad, outs, sums)
 
         order = wires.trade_order()
         w_q, w_k = [weights_of(v) for v in first[:2]]
         attn0 = look(lat_norm0, w_q, w_k, 0)
-        zero, (second,) = gate([attn0["low"]] + inner0[1:], [second])
-        piece = jnp.concatenate([picked[1], out_piece[1][None]], 0)
-        rest = lax.all_gather(later(piece, zero), "dp", axis=1)
+        zero, (second,) = gate([attn0["low"]], [second])
         inner0 = wires.trade_far(inner0, zero)
         w_v, w_o = [weights_of(v) for v in (second[0], joined(second[1]))]
         weights0 = [w_q, w_k, w_v, w_o]
@@ -712,14 +714,15 @@
         g_vo = wires.sum_far(g_vo, zero.index)
         d_lat = look_back(lat_norm0, weights0, 0, attn0)
         zero, (d_lat, attn0["d_lift"]) = gate([], [d_lat, attn0["d_lift"]])
-        g_vo = wires.sum_near(g_vo[0], later(g_vo[1], zero))
         d_norm0, grad = latents_back(d_low0, d_lat, x_hat0, x_rstd0, 0)
         left, right = media_pair(attn0)
         media_sum = media_sum + dot_rows(left, later(right, zero))
         d_media = norm_back(hat.astype(f32), rstd_media, media_sum)
         send = cut(d_media, half * (1 - y), half).astype(bf16)
-        zero, (send, grad, attn0["d_lift"]) = gate([], [send, grad, attn0["d_lift"]])
+        zero, (send, grad, attn0["d_lift"]) = gate([g_vo[1]], [send, grad, attn0["d_lift"]])
         got = wires.near_y(send)
+        g_vo = wires.sum_near(g_vo[0], later(g_vo[1], zero))
+        x_part = wires.sum_rows(later(x_part, zero).astype(f32))
         extra = vector_rows(attn0, d_norm0, x_hat0, d_mn0, hat_m0)
         extra += vector_rows(attn1, d_norm1, x_hat1, d_mn1, hat_m1)
         extra = jnp.zeros((128, width), f32).at[: layers * 6].set(jnp.stack(extra)).T
@@ -728,21 +731,24 @@
         zero, (g_qk, blocks1, *share1) = gate([], [g_qk, blocks1, *share1])
         step = zero.index
         g_qk = wires.sum_far(g_qk.reshape(dp, shard, g_qk.shape[1]), step)
-        x_part = wires.sum_rows(later(x_part, zero).astype(f32))
         blocks1 = lax.all_gather(blocks1, "section", axis=0)
         outer1 = lax.all_gather(share1[1], "section", axis=0, tiled=True)
-        zero, (far, grad, share0[0]) = gate([], [g_qk[1], grad, share0[0]])
+        zero, (far, grad, share0[0]) = gate([*g_vo[1], x_part], [g_qk[1], grad, share0[0]])
         step = zero.index
         g_qk = wires.sum_near(g_qk[0], far)
-        trade = jnp.concatenate([share1[0], share0[0]], 1)
-        trade = wires.trade_near(lambda d: at(trade, d + step))
         blocks1 = later(blocks1, zero).reshape(2, 2, shard, 4 * quarter)
         parts = [blocks1[..., j * quarter : (j + 1) * quarter] for j in range(4)]
         attn_out1 = finish(*parts[:3], output_columns(parts[3]))
-        zero, (grad, share0[1], *arrived) = gate([*attn_out1], [grad, share0[1], *g_qk[1]])
+        zero, (outer0,) = gate(attn_out1, [share0[1]])
+        outer0 = lax.all_gather(outer0, "section", axis=0, tiled=True)
+        step = zero.index
+        trade = jnp.concatenate([share1[0], share0[0]], 1)
+        trade = wires.trade_near(lambda d: at(trade, d + step))
+        outs = [jnp.zeros((layers,) + v.shape, f32).at[1].set(v) for v in attn_out1]
+        zero, (grad, *arrived) = gate([], [grad, *g_qk[1], *outs])
+        arrived, outs = arrived[:-3], arrived[-3:]
         g_qk = (g_qk[0], arrived)
         trade = wires.trade_far(trade, zero)
-        outer0 = lax.all_gather(share0[1], "section", axis=0, tiled=True)
         x_out = (mid1 + x_part + zero.value).astype(bf16)
 
         def summed(mine, parts):
@@ -750,25 +756,26 @@
                 mine = mine + v.astype(f32)
             return mine.astype(bf16)
 
-        def join(v):
-            pair = wires.by_y(v[None], wires.near_y(v)[None], 0)
-            return wires.by_c(pair[:, None], wires.near_c(pair)[:, None], 1)
-
-        four = join(jnp.concatenate([summed(*g_vo), summed(*g_qk)], 1))
-        value, out, query, key = [four[..., i * quarter : (i + 1) * quarter] for i in range(4)]
-        sums = jnp.sum(four[..., 4 * quarter :].astype(f32), axis=(0, 1))[:, : layers * 6].T
+        four = jnp.concatenate([summed(*g_vo), summed(*g_qk)], 1)
+        four_y = wires.near_y(four)
         inner = []
         for i in range(layers):
             rows_of = slice(i * part, (i + 1) * part)
-            blocks = [v[rows_of] for v in trade[0] + list(trade[1])]
-            v = lax.all_gather(line_up(blocks, order), "section", axis=0, tiled=True)
-            inner.append(v.astype(f32))
+            inner.append(line_up([v[rows_of] for v in trade[0] + list(trade[1])], order))
+        inner = jnp.stack(inner)
+        zero, _ = gate([inner])
+        inner = lax.all_gather(inner, "section", axis=0)
+        four = wires.by_y(four[None], later(four_y, zero)[None], 0)
+        four = wires.by_c(four[:, None], wires.near_c(four)[:, None], 1)
+        value, out, query, key = [four[..., i * quarter : (i + 1) * quarter] for i in range(4)]
+        sums = jnp.sum(four[..., 4 * quarter :].astype(f32), axis=(0, 1))[:, : layers * 6].T
+        inner = [inner[:, i].reshape(shard, dp * span).astype(f32) for i in range(layers)]
         ffn_out = [(inner[1], outer0.astype(f32)), (inner[0], outer1.astype(f32))]
         attn_out0 = finish(query, key, value, output_columns(out))
         media_grad = wires.spread_c(cut(d_media, half * y, half) + later(got, zero).astype(f32))
-        return outputs(
-            x_out, grad, media_grad, [attn_out0, attn_out1], ffn_out, sums
-        )
+        outs = [v.at[0].set(u) for v, u in zip(outs, attn_out0)]
+        outs += [jnp.stack([ffn_out[level][i] for level in range(layers)]) for i in range(2)]
+        return outputs(x_out, grad, media_grad, outs, sums)
 
     return run
 

time: 823 us -> 756 us (0.919)
  waiting for transfers between devices: 247 us -> 163 us
  local copies, waits for them, and re-layouts: 100 us -> 114 us
  between operations: 45.1 us -> 54.3 us
  matrix products: 136 us -> 127 us
    ppermute x102 -> x100, waiting for transfers between devices: 244 us -> 144 us  [send(): return lax.ppermute(value, AXES, pairs)]
    all_gather x3 -> x2, waiting for transfers between devices: 0.01 us -> 17.2 us  [the longest x1 17.2 us: run(): inner = lax.all_gather(inner, 'section', axis=0)]
    dynamic_slice x2 -> x11, local copies, waits for them, and re-layouts: 0.67 us -> 8.98 us  [at(): return lax.dynamic_index_in_dim(array, index, axis, keepdims=False)]
    another operation x9 -> x8, other arithmetic: 24.3 us -> 16.3 us  [the longest x2 11.1 us: run(): jnp.stack([ffn_out[level][i] for level in range(layers)])]
    unnamed x460 -> x504, local copies, waits for them, and re-layouts: 36.5 us -> 34.4 us
    ppermute x102 -> x100, starting transfers between devices: 152 us -> 153 us  [send(): return lax.ppermute(value, AXES, pairs)]
  transfers between devices with their start and end apart: 114 -> 111, of which waited for: 44 -> 40; matrix products, arithmetic and copies ran while one was open for 37% -> 42% of each run, Pallas kernels for 1% -> 2%
where the time goes in v3:
time: 756 us; the launch traced here: 746 us
  waiting for transfers between devices  163 us (22%)
  starting transfers between devices  154 us (20%)
  matrix products  127 us (17%)
  other arithmetic  121 us (16%)
  local copies, waits for them, and re-layouts  114 us (15%)
  between operations  54.3 us (7%)
  Pallas kernels  13.4 us (2%)
    ppermute x100, starting transfers between devices, send(): return lax.ppermute(value, AXES, pairs)  153 us
    ppermute x100, waiting for transfers between devices, send(): return lax.ppermute(value, AXES, pairs)  144 us
    dot_general x35, matrix products, dot(): return jnp.dot(left, right, preferred_element_type=f32)  47.6 us
    dot_general x29, matrix products, dot_cols(): lax.dot_general(left, right, (((1,), (1,)), ((), ())), preferred_element_...  43.8 us
    dot_general x16, matrix products, dot_rows(): lax.dot_general(left, right, (((0,), (0,)), ((), ())), preferred_element_...  35.8 us
    unnamed x504, local copies, waits for them, and re-layouts  34.4 us
    all_gather x1, waiting for transfers between devices, run(): inner = lax.all_gather(inner, 'section', axis=0)  17.2 us
  transfers between devices with their start and end apart: 111, of which 40 were waited for; matrix products, arithmetic and copies ran while one was open for 42% of the time, Pallas kernels for 2%

profile of v3, /device:TPU:0, one launch (start us, length us, event | category | flops | bytes accessed | tf_op | source)
XLA Modules:
  0.0 746.2 jit_solution(8564279916743350442)
XLA Ops:
  15.6 2.9 collective-permute-start.5
  20.1 2.6 collective-permute-start.3
  29.7 2.9 fusion.3
  36.3 4.4 fusion.4
  43.3 5.8 collective-permute-done.1
  56.9 2.9 constant_dynamic-slice_fusion.29
  60.5 10.2 %collective-permute-start.9 = (bf16[2,96,768]{2,1,0:T(8,128)(2,1)}, bf16[2,96,768]{2,1,0:T(8,128)(2,1)}, u32[]{:S(2)}, u32[]{:S(2)}) collective-permute-start(bf16[2,96,768]{2,1,0:T(8,128)(2,1)} %pad_maximum_fusion.25), channel_id=1, source_target_pairs={{0,8},{1,9},{2,10},{3,11},{4,12},{5,13},{6,14},{7,15},{8,16},{9,17... | collective-permute-start | bytes 884744 | tf_op jit(solution)/shard_map/ppermute | solution.py:142
  79.8 14.2 %collective-permute-done.6 = bf16[3,192,896]{2,1,0:T(8,128)(2,1)} collective-permute-done((bf16[3,192,896]{2,1,0:T(8,128)(2,1)}, bf16[3,192,896]{2,1,0:T(8,128)(2,1)}, u32[]{:S(2)}, u32[]{:S(2)}) %collective-permute-start.6) | collective-permute-done | bytes 1032224 | tf_op jit(solution)/shard_map/ppermute | solution.py:142
  101.2 2.7 collective-permute-done.7
  118.4 3.1 fusion.404
  139.5 7.8 %collective-permute-done.12.refs_0_ = bf16[4,96,768]{2,1,0:T(8,128)(2,1)} collective-permute-done((bf16[4,96,768]{2,1,0:T(8,128)(2,1)}, bf16[4,96,768]{2,1,0:T(8,128)(2,1)}, u32[]{:S(2)}, u32[]{:S(2)}) %collective-permute-start.12) | collective-permute-done | bytes 589856 | tf_op jit(solution)/shard_map/ppermute | solution.py:142
  161.9 13.5 %collective-permute-start.18 = (bf16[32,1536]{1,0:T(8,128)(2,1)S(1)}, bf16[32,1536]{1,0:T(8,128)(2,1)S(1)}, u32[]{:S(2)}, u32[]{:S(2)}) collective-permute-start(bf16[32,1536]{1,0:T(8,128)(2,1)S(1)} %get-tuple-element.270), channel_id=1, source_target_pairs={{0,8},{1,9},{2,10},{3,11},{4,12},{5,13},{6,14},{7,15},{8,16},{9,17... | collective-permute-start | bytes 294920 | tf_op jit(solution)/shard_map/ppermute | solution.py:142
  183.4 4.2 collective-permute-done.17
  189.7 4.3 collective-permute-done.20
  195.0 3.1 multiply_convert_fusion.7
  200.4 8.5 %collective-permute-done.24 = bf16[128,1536]{1,0:T(8,128)(2,1)S(1)} collective-permute-done((bf16[128,1536]{1,0:T(8,128)(2,1)S(1)}, bf16[128,1536]{1,0:T(8,128)(2,1)S(1)}, u32[]{:S(2)}, u32[]{:S(2)}) %collective-permute-start.24) | collective-permute-done | bytes 393248 | tf_op jit(solution)/shard_map/ppermute | solution.py:142
  209.0 7.1 collective-permute-start.25
  221.2 2.6 collective-permute-done.26
  227.1 3.2 collective-permute-start.48
  230.3 4.4 fusion.402
  241.0 3.3 collective-permute-start.47
  272.2 2.6 collective-permute-start.43
  279.2 4.0 collective-permute-done.33
  291.9 3.1 collective-permute-start.34
  300.6 9.6 %collective-permute-done.45 = bf16[8,48,768]{2,1,0:T(8,128)(2,1)S(1)} collective-permute-done((bf16[8,48,768]{2,1,0:T(8,128)(2,1)S(1)}, bf16[8,48,768]{2,1,0:T(8,128)(2,1)S(1)}, u32[]{:S(2)}, u32[]{:S(2)}) %collective-permute-start.45) | collective-permute-done | bytes 589856 | tf_op jit(solution)/shard_map/ppermute | solution.py:142
  310.8 4.0 collective-permute-done.38
  317.2 3.1 multiply_convert_fusion.6
  321.1 3.3 convolution_convert_fusion.2.refs_1_
  324.5 4.5 add_convert_fusion.1
  330.3 8.3 %collective-permute-done.51 = bf16[128,1536]{1,0:T(8,128)(2,1)S(1)} collective-permute-done((bf16[128,1536]{1,0:T(8,128)(2,1)S(1)}, bf16[128,1536]{1,0:T(8,128)(2,1)S(1)}, u32[]{:S(2)}, u32[]{:S(2)}) %collective-permute-start.51) | collective-permute-done | bytes 393248 | tf_op jit(solution)/shard_map/ppermute | solution.py:142
  371.7 3.1 fusion.15
  375.5 2.7 fusion.132
  381.9 2.5 fusion.56.refs_0_
  395.0 3.7 maximum_maximum_fusion
  400.4 4.5 collective-permute-done.60
  413.3 3.0 collective-permute-done.63
  416.3 2.8 collective-permute-start.67
  419.1 3.5 collective-permute-done.62
  424.9 4.6 collective-permute-done.65
  431.7 4.4 add_convert_fusion
  438.7 5.5 fusion.16.refs_0_
  446.5 3.4 collective-permute-done.68
  450.0 8.3 %collective-permute-start.69 = (bf16[32,1536]{1,0:T(8,128)(2,1)S(1)}, bf16[32,1536]{1,0:T(8,128)(2,1)S(1)}, u32[]{:S(2)}, u32[]{:S(2)}) collective-permute-start(bf16[32,1536]{1,0:T(8,128)(2,1)S(1)} %get-tuple-element.412), channel_id=1, source_target_pairs={{0,8},{1,9},{2,10},{3,11},{4,12},{5,13},{6,14},{7,15},{8,16},{9,17... | collective-permute-start | bytes 294920 | tf_op jit(solution)/shard_map/ppermute | solution.py:142
  494.4 3.2 convolution_convert_fusion.4.refs_0_
  502.2 4.7 fusion.57
  520.3 10.3 %fusion.388 = (f32[1024]{0:T(1024)S(1)}, f32[1024]{0:T(1024)S(1)}, f32[1024,1536]{1,0:T(8,128)S(1)}) fusion(bf16[1024,1536]{1,0:T(8,128)(2,1)} %fusion.4, f32[1024,1536]{1,0:T(8,128)} %fusion.16.refs_0_, bf16[512,1536]{1,0:T(8,128)(2,1)} %get-tuple-element.297, bf16[512,1536]{1,0:T(8,128)(2,1)} %copy-done.88, bf16[]{:T(256)} %bitcast.100, ...), kind=kOutput, calls=%fused_computation.871 | convolution fusion | flops 3242719232 | bytes 20979714 | tf_op jit(solution)/shard_map/dot_general | solution.py:23
  534.3 2.7 copy-done.4
  550.1 2.6 fusion.35
  553.7 3.3 fusion.390
  558.0 3.3 collective-permute-start.83
  569.1 15.6 %collective-permute-start.78 = (bf16[32,1536]{1,0:T(8,128)(2,1)S(1)}, bf16[32,1536]{1,0:T(8,128)(2,1)S(1)}, u32[]{:S(2)}, u32[]{:S(2)}) collective-permute-start(bf16[32,1536]{1,0:T(8,128)(2,1)S(1)} %get-tuple-element.409), channel_id=1, source_target_pairs={{0,8},{1,9},{2,10},{3,11},{4,12},{5,13},{6,14},{7,15},{8,16},{9,17... | collective-permute-start | bytes 294920 | tf_op jit(solution)/shard_map/ppermute | solution.py:142
  584.7 5.2 collective-permute-done.82.refs_1_
  600.1 3.2 fusion.389
  604.3 3.2 collective-permute-start.89
  627.4 2.7 scatter.35.refs_5_
  631.7 5.0 collective-permute-done.88.refs_2_
  646.9 2.9 collective-permute-start.95
  658.5 3.6 collective-permute-done.95
  671.0 10.1 %collective-permute-done.96 = bf16[4,96,768]{2,1,0:T(8,128)(2,1)S(1)} collective-permute-done((bf16[4,96,768]{2,1,0:T(8,128)(2,1)S(1)}, bf16[4,96,768]{2,1,0:T(8,128)(2,1)S(1)}, u32[]{:S(2)}, u32[]{:S(2)}) %collective-permute-start.96) | collective-permute-done | bytes 589856 | tf_op jit(solution)/shard_map/ppermute | solution.py:142
  689.6 2.7 convert_add_fusion
  708.5 6.8 maximum_convert_fusion.1
  715.3 17.2 %all-gather.20.cloned.1.call-done = bf16[8,48,6144]{2,1,0:T(8,128)(2,1)} async-done(((bf16[2,48,6144]{2,1,0:T(8,128)(2,1)}), bf16[8,48,6144]{2,1,0:T(8,128)(2,1)}) %all-gather.20.cloned.1.call-update) | async-done | bytes 4718608 | tf_op jit(solution)/shard_map/all_gather | solution.py:767
  732.5 2.7 fusion.401
  735.2 4.4 maximum_convert_fusion
  (1107 shorter events, 368.3 us)
Async XLA Ops:
  7.2 110.7 %all-gather.16.cloned.1.call-start = ((), (), s32[]{:S(2)}) async-start(), calls=%async_computation.13 | async-start | bytes 2654208 | tf_op jit(solution)/shard_map/all_gather | solution.py:342
  15.6 63.2 %collective-permute-start.5 = (bf16[192,896]{1,0:T(8,128)(2,1)}, bf16[192,896]{1,0:T(8,128)(2,1)}, u32[]{:S(2)}, u32[]{:S(2)}) collective-permute-start(bf16[192,896]{1,0:T(8,128)(2,1)} %pad_maximum_fusion.21), channel_id=1, source_target_pairs={{0,4},{1,5},{2,6},{3,7},{4,0},{5,1},{6,2},{7,3},{8,12},{9,13},{10,... | collective-permute-start | bytes 1032200 | tf_op jit(solution)/shard_map/ppermute | solution.py:142
  18.5 32.0 %collective-permute-start.4 = (bf16[192,896]{1,0:T(8,128)(2,1)}, bf16[192,896]{1,0:T(8,128)(2,1)S(1)}, u32[]{:S(2)}, u32[]{:S(2)}) collective-permute-start(bf16[192,896]{1,0:T(8,128)(2,1)} %pad_maximum_fusion.21), channel_id=1, source_target_pairs={{0,8},{1,9},{2,10},{3,11},{4,12},{5,13},{6,14},{7,15},{8,16},{9,17... | collective-permute-start | bytes 1032200 | tf_op jit(solution)/shard_map/ppermute | solution.py:142
  20.1 32.1 %collective-permute-start.3 = (bf16[192,896]{1,0:T(8,128)(2,1)}, bf16[192,896]{1,0:T(8,128)(2,1)}, u32[]{:S(2)}, u32[]{:S(2)}) collective-permute-start(bf16[192,896]{1,0:T(8,128)(2,1)} %pad_maximum_fusion.21), channel_id=1, source_target_pairs={{0,16},{1,17},{2,18},{3,19},{4,20},{5,21},{6,22},{7,23},{8,24},{9,... | collective-permute-start | bytes 1032200 | tf_op jit(solution)/shard_map/ppermute | solution.py:142
  22.7 29.6 %collective-permute-start.2 = (bf16[192,896]{1,0:T(8,128)(2,1)}, bf16[192,896]{1,0:T(8,128)(2,1)}, u32[]{:S(2)}, u32[]{:S(2)}) collective-permute-start(bf16[192,896]{1,0:T(8,128)(2,1)} %pad_maximum_fusion.21), channel_id=1, source_target_pairs={{0,24},{1,25},{2,26},{3,27},{4,28},{5,29},{6,30},{7,31},{8,0},{9,1... | collective-permute-start | bytes 1032200 | tf_op jit(solution)/shard_map/ppermute | solution.py:142
  24.7 16.0 %collective-permute-start = (bf16[2,64,384]{2,1,0:T(8,128)(2,1)}, bf16[2,64,384]{2,1,0:T(8,128)(2,1)}, u32[]{:S(2)}, u32[]{:S(2)}) collective-permute-start(bf16[2,64,384]{2,1,0:T(8,128)(2,1)} %get-tuple-element.446), channel_id=1, source_target_pairs={{0,1},{1,0},{2,3},{3,2},{4,5},{5,4},{6,7},{7,6},{8,9},{9,8},{10,11... | collective-permute-start | bytes 294920 | tf_op jit(solution)/shard_map/ppermute | solution.py:142
  27.2 197.4 %all-gather.10.cloned.1.call-start = ((), (), s32[]{:S(2)}) async-start(), calls=%async_computation.5 | async-start | bytes 5308416 | tf_op jit(solution)/shard_map/all_gather | solution.py:345
  56.3 37.6 %collective-permute-start.6 = (bf16[3,192,896]{2,1,0:T(8,128)(2,1)}, bf16[3,192,896]{2,1,0:T(8,128)(2,1)}, u32[]{:S(2)}, u32[]{:S(2)}) collective-permute-start(bf16[3,192,896]{2,1,0:T(8,128)(2,1)} %pad_maximum_fusion.14), channel_id=1, source_target_pairs={{0,4},{1,5},{2,6},{3,7},{4,0},{5,1},{6,2},{7,3},{8,12},{9,13},{10,... | collective-permute-start | bytes 3096584 | tf_op jit(solution)/shard_map/ppermute | solution.py:142
  60.5 66.4 %collective-permute-start.9 = (bf16[2,96,768]{2,1,0:T(8,128)(2,1)}, bf16[2,96,768]{2,1,0:T(8,128)(2,1)}, u32[]{:S(2)}, u32[]{:S(2)}) collective-permute-start(bf16[2,96,768]{2,1,0:T(8,128)(2,1)} %pad_maximum_fusion.25), channel_id=1, source_target_pairs={{0,8},{1,9},{2,10},{3,11},{4,12},{5,13},{6,14},{7,15},{8,16},{9,17... | collective-permute-start | bytes 884744 | tf_op jit(solution)/shard_map/ppermute | solution.py:142
  71.4 53.8 %collective-permute-start.10 = (bf16[2,96,768]{2,1,0:T(8,128)(2,1)}, bf16[2,96,768]{2,1,0:T(8,128)(2,1)}, u32[]{:S(2)}, u32[]{:S(2)}) collective-permute-start(bf16[2,96,768]{2,1,0:T(8,128)(2,1)} %pad_maximum_fusion.26), channel_id=1, source_target_pairs={{0,16},{1,17},{2,18},{3,19},{4,20},{5,21},{6,22},{7,23},{8,24},{9,... | collective-permute-start | bytes 884744 | tf_op jit(solution)/shard_map/ppermute | solution.py:142
  73.7 50.6 %collective-permute-start.11 = (bf16[2,96,768]{2,1,0:T(8,128)(2,1)}, bf16[2,96,768]{2,1,0:T(8,128)(2,1)}, u32[]{:S(2)}, u32[]{:S(2)}) collective-permute-start(bf16[2,96,768]{2,1,0:T(8,128)(2,1)} %pad_maximum_fusion.27), channel_id=1, source_target_pairs={{0,24},{1,25},{2,26},{3,27},{4,28},{5,29},{6,30},{7,31},{8,0},{9,1... | collective-permute-start | bytes 884744 | tf_op jit(solution)/shard_map/ppermute | solution.py:142
  76.4 388.3 %reduce-scatter.8.cloned.1.call-start = ((), (), s32[]{:S(2)}) async-start(), calls=%async_computation.7 | async-start | bytes 2949120 | tf_op jit(solution)/shard_map/reduce_scatter | solution.py:679
  121.5 13.3 %collective-permute-start.13 = (bf16[1536,384]{1,0:T(8,128)(2,1)}, bf16[1536,384]{1,0:T(8,128)(2,1)}, u32[]{:S(2)}, u32[]{:S(2)}) collective-permute-start(bf16[1536,384]{1,0:T(8,128)(2,1)} %bitcast.34), channel_id=1, source_target_pairs={{0,1},{1,0},{2,3},{3,2},{4,5},{5,4},{6,7},{7,6},{8,9},{9,8},{10,11... | collective-permute-start | bytes 3538952 | tf_op jit(solution)/shard_map/ppermute | solution.py:142
  123.1 14.0 %collective-permute-start.14 = (bf16[768,768]{1,0:T(8,128)(2,1)S(1)}, bf16[768,768]{1,0:T(8,128)(2,1)}, u32[]{:S(2)}, u32[]{:S(2)}) collective-permute-start(bf16[768,768]{1,0:T(8,128)(2,1)S(1)} %pad_maximum_fusion.7), channel_id=1, source_target_pairs={{0,1},{1,0},{2,3},{3,2},{4,5},{5,4},{6,7},{7,6},{8,9},{9,8},{10,11... | collective-permute-start | bytes 3538952 | tf_op jit(solution)/shard_map/ppermute | solution.py:142
  131.7 15.6 %collective-permute-start.12 = (bf16[4,96,768]{2,1,0:T(8,128)(2,1)}, bf16[4,96,768]{2,1,0:T(8,128)(2,1)}, u32[]{:S(2)}, u32[]{:S(2)}) collective-permute-start(bf16[4,96,768]{2,1,0:T(8,128)(2,1)} %pad_maximum_fusion.17), channel_id=1, source_target_pairs={{0,4},{1,5},{2,6},{3,7},{4,0},{5,1},{6,2},{7,3},{8,12},{9,13},{10,... | collective-permute-start | bytes 1769480 | tf_op jit(solution)/shard_map/ppermute | solution.py:142
  161.9 20.9 %collective-permute-start.18 = (bf16[32,1536]{1,0:T(8,128)(2,1)S(1)}, bf16[32,1536]{1,0:T(8,128)(2,1)S(1)}, u32[]{:S(2)}, u32[]{:S(2)}) collective-permute-start(bf16[32,1536]{1,0:T(8,128)(2,1)S(1)} %get-tuple-element.270), channel_id=1, source_target_pairs={{0,8},{1,9},{2,10},{3,11},{4,12},{5,13},{6,14},{7,15},{8,16},{9,17... | collective-permute-start | bytes 294920 | tf_op jit(solution)/shard_map/ppermute | solution.py:142
  175.4 12.2 %collective-permute-start.17 = (bf16[32,1536]{1,0:T(8,128)(2,1)S(1)}, bf16[32,1536]{1,0:T(8,128)(2,1)S(1)}, u32[]{:S(2)}, u32[]{:S(2)}) collective-permute-start(bf16[32,1536]{1,0:T(8,128)(2,1)S(1)} %get-tuple-element.270), channel_id=1, source_target_pairs={{0,16},{1,17},{2,18},{3,19},{4,20},{5,21},{6,22},{7,23},{8,24},{9,... | collective-permute-start | bytes 294920 | tf_op jit(solution)/shard_map/ppermute | solution.py:142
  180.6 13.5 %collective-permute-start.23 = (bf16[8,96,768]{2,1,0:T(8,128)(2,1)S(1)}, bf16[8,96,768]{2,1,0:T(8,128)(2,1)S(1)}, u32[]{:S(2)}, u32[]{:S(2)}) collective-permute-start(bf16[8,96,768]{2,1,0:T(8,128)(2,1)S(1)} %slice_dynamic-update-slice_fusion.3), channel_id=1, source_target_pairs={{0,1},{1,0},{2,3},{3,2},{4,5},{5,4},{6,7},{7,6},{8,9},{9,8},{10,11... | collective-permute-start | bytes 3538952 | tf_op jit(solution)/shard_map/ppermute | solution.py:142
  182.9 11.2 %collective-permute-start.22 = (bf16[32,1536]{1,0:T(8,128)(2,1)S(1)}, bf16[32,1536]{1,0:T(8,128)(2,1)S(1)}, u32[]{:S(2)}, u32[]{:S(2)}) collective-permute-start(bf16[32,1536]{1,0:T(8,128)(2,1)S(1)} %collective-permute-done.18), channel_id=1, source_target_pairs={{0,4},{1,5},{2,6},{3,7},{4,0},{5,1},{6,2},{7,3},{8,12},{9,13},{10,... | collective-permute-start | bytes 294920 | tf_op jit(solution)/shard_map/ppermute | solution.py:142
  227.1 57.3 %collective-permute-start.49 = (bf16[32,1536]{1,0:T(8,128)(2,1)}, bf16[32,1536]{1,0:T(8,128)(2,1)}, u32[]{:S(2)}, u32[]{:S(2)}) collective-permute-start(bf16[32,1536]{1,0:T(8,128)(2,1)} %add_bitcast_fusion.2), channel_id=1, source_target_pairs={{0,8},{1,9},{2,10},{3,11},{4,12},{5,13},{6,14},{7,15},{8,16},{9,17... | collective-permute-start | bytes 294920 | tf_op jit(solution)/shard_map/ppermute | solution.py:142
  227.1 58.2 %collective-permute-start.48 = (bf16[32,1536]{1,0:T(8,128)(2,1)}, bf16[32,1536]{1,0:T(8,128)(2,1)}, u32[]{:S(2)}, u32[]{:S(2)}) collective-permute-start(bf16[32,1536]{1,0:T(8,128)(2,1)} %add_bitcast_fusion.2), channel_id=1, source_target_pairs={{0,16},{1,17},{2,18},{3,19},{4,20},{5,21},{6,22},{7,23},{8,24},{9,... | collective-permute-start | bytes 294920 | tf_op jit(solution)/shard_map/ppermute | solution.py:142
  236.3 12.2 %collective-permute-start.30 = (bf16[1536,384]{1,0:T(8,128)(2,1)}, bf16[1536,384]{1,0:T(8,128)(2,1)}, u32[]{:S(2)}, u32[]{:S(2)}) collective-permute-start(bf16[1536,384]{1,0:T(8,128)(2,1)} %bitcast.50), channel_id=1, source_target_pairs={{0,1},{1,0},{2,3},{3,2},{4,5},{5,4},{6,7},{7,6},{8,9},{9,8},{10,11... | collective-permute-start | bytes 3538952 | tf_op jit(solution)/shard_map/ppermute | solution.py:142
  241.0 44.3 %collective-permute-start.47 = (bf16[32,1536]{1,0:T(8,128)(2,1)}, bf16[32,1536]{1,0:T(8,128)(2,1)}, u32[]{:S(2)}, u32[]{:S(2)}) collective-permute-start(bf16[32,1536]{1,0:T(8,128)(2,1)} %add_bitcast_fusion.2), channel_id=1, source_target_pairs={{0,24},{1,25},{2,26},{3,27},{4,28},{5,29},{6,30},{7,31},{8,0},{9,1... | collective-permute-start | bytes 294920 | tf_op jit(solution)/shard_map/ppermute | solution.py:142
  244.6 18.9 %collective-permute-start.32 = (bf16[768,768]{1,0:T(8,128)(2,1)S(1)}, bf16[768,768]{1,0:T(8,128)(2,1)S(1)}, u32[]{:S(2)}, u32[]{:S(2)}) collective-permute-start(bf16[768,768]{1,0:T(8,128)(2,1)S(1)} %pad_maximum_fusion.8), channel_id=1, source_target_pairs={{0,1},{1,0},{2,3},{3,2},{4,5},{5,4},{6,7},{7,6},{8,9},{9,8},{10,11... | collective-permute-start | bytes 3538952 | tf_op jit(solution)/shard_map/ppermute | solution.py:142
  248.5 12.7 %collective-permute-start.31 = (bf16[1536,384]{1,0:T(8,128)(2,1)S(1)}, bf16[1536,384]{1,0:T(8,128)(2,1)S(1)}, u32[]{:S(2)}, u32[]{:S(2)}) collective-permute-start(bf16[1536,384]{1,0:T(8,128)(2,1)S(1)} %bitcast.568), channel_id=1, source_target_pairs={{0,1},{1,0},{2,3},{3,2},{4,5},{5,4},{6,7},{7,6},{8,9},{9,8},{10,11... | collective-permute-start | bytes 3538952 | tf_op jit(solution)/shard_map/ppermute | solution.py:142
  261.2 11.0 %collective-permute-start.41 = (bf16[2,48,768]{2,1,0:T(8,128)(2,1)}, bf16[2,48,768]{2,1,0:T(8,128)(2,1)}, u32[]{:S(2)}, u32[]{:S(2)}) collective-permute-start(bf16[2,48,768]{2,1,0:T(8,128)(2,1)} %pad_maximum_fusion.34), channel_id=1, source_target_pairs={{0,8},{1,9},{2,10},{3,11},{4,12},{5,13},{6,14},{7,15},{8,16},{9,17... | collective-permute-start | bytes 442376 | tf_op jit(solution)/shard_map/ppermute | solution.py:142
  263.5 15.0 %collective-permute-start.42 = (bf16[2,48,768]{2,1,0:T(8,128)(2,1)}, bf16[2,48,768]{2,1,0:T(8,128)(2,1)S(1)}, u32[]{:S(2)}, u32[]{:S(2)}) collective-permute-start(bf16[2,48,768]{2,1,0:T(8,128)(2,1)} %pad_maximum_fusion.35), channel_id=1, source_target_pairs={{0,16},{1,17},{2,18},{3,19},{4,20},{5,21},{6,22},{7,23},{8,24},{9,... | collective-permute-start | bytes 442376 | tf_op jit(solution)/shard_map/ppermute | solution.py:142
  279.1 15.9 %collective-permute-start.44 = (bf16[4,48,768]{2,1,0:T(8,128)(2,1)S(1)}, bf16[4,48,768]{2,1,0:T(8,128)(2,1)S(1)}, u32[]{:S(2)}, u32[]{:S(2)}) collective-permute-start(bf16[4,48,768]{2,1,0:T(8,128)(2,1)S(1)} %pad_maximum_fusion.28), channel_id=1, source_target_pairs={{0,4},{1,5},{2,6},{3,7},{4,0},{5,1},{6,2},{7,3},{8,12},{9,13},{10,... | collective-permute-start | bytes 884744 | tf_op jit(solution)/shard_map/ppermute | solution.py:142
  289.8 30.6 %collective-permute-start.50 = (bf16[128,1536]{1,0:T(8,128)(2,1)}, bf16[128,1536]{1,0:T(8,128)(2,1)}, u32[]{:S(2)}, u32[]{:S(2)}) collective-permute-start(bf16[128,1536]{1,0:T(8,128)(2,1)} %maximum_add_fusion.5), channel_id=1, source_target_pairs={{0,4},{1,5},{2,6},{3,7},{4,0},{5,1},{6,2},{7,3},{8,12},{9,13},{10,... | collective-permute-start | bytes 1179656 | tf_op jit(solution)/shard_map/ppermute | solution.py:142
  290.4 20.2 %collective-permute-start.37 = (bf16[32,1536]{1,0:T(8,128)(2,1)}, bf16[32,1536]{1,0:T(8,128)(2,1)S(1)}, u32[]{:S(2)}, u32[]{:S(2)}) collective-permute-start(bf16[32,1536]{1,0:T(8,128)(2,1)} %get-tuple-element.262), channel_id=1, source_target_pairs={{0,4},{1,5},{2,6},{3,7},{4,0},{5,1},{6,2},{7,3},{8,12},{9,13},{10,... | collective-permute-start | bytes 294920 | tf_op jit(solution)/shard_map/ppermute | solution.py:142
  295.0 19.9 %collective-permute-start.40 = (bf16[32,1536]{1,0:T(8,128)(2,1)}, bf16[32,1536]{1,0:T(8,128)(2,1)S(1)}, u32[]{:S(2)}, u32[]{:S(2)}) collective-permute-start(bf16[32,1536]{1,0:T(8,128)(2,1)} %collective-permute-done.36), channel_id=1, source_target_pairs={{0,4},{1,5},{2,6},{3,7},{4,0},{5,1},{6,2},{7,3},{8,12},{9,13},{10,... | collective-permute-start | bytes 294920 | tf_op jit(solution)/shard_map/ppermute | solution.py:142
  295.0 19.7 %collective-permute-start.39 = (bf16[32,1536]{1,0:T(8,128)(2,1)}, bf16[32,1536]{1,0:T(8,128)(2,1)S(1)}, u32[]{:S(2)}, u32[]{:S(2)}) collective-permute-start(bf16[32,1536]{1,0:T(8,128)(2,1)} %collective-permute-done.35), channel_id=1, source_target_pairs={{0,4},{1,5},{2,6},{3,7},{4,0},{5,1},{6,2},{7,3},{8,12},{9,13},{10,... | collective-permute-start | bytes 294920 | tf_op jit(solution)/shard_map/ppermute | solution.py:142
  298.3 11.9 %collective-permute-start.45 = (bf16[8,48,768]{2,1,0:T(8,128)(2,1)S(1)}, bf16[8,48,768]{2,1,0:T(8,128)(2,1)S(1)}, u32[]{:S(2)}, u32[]{:S(2)}) collective-permute-start(bf16[8,48,768]{2,1,0:T(8,128)(2,1)S(1)} %slice_dynamic-update-slice_fusion.7), channel_id=1, source_target_pairs={{0,2},{1,3},{2,0},{3,1},{4,6},{5,7},{6,4},{7,5},{8,10},{9,11},{10,... | collective-permute-start | bytes 1769480 | tf_op jit(solution)/shard_map/ppermute | solution.py:142
  324.5 140.2 %reduce-scatter.6.cloned.1.call-start = ((), (), s32[]{:S(2)}) async-start(), calls=%async_computation.6 | async-start | bytes 2949120 | tf_op jit(solution)/shard_map/reduce_scatter | solution.py:679
  355.7 192.3 %reduce-scatter.10.cloned.1.call-start = ((), (), s32[]{:S(2)}) async-start(), calls=%async_computation.8 | async-start | bytes 5308416 | tf_op jit(solution)/shard_map/reduce_scatter | solution.py:701
  398.8 200.1 %reduce-scatter.12.cloned.1.call-start = ((), (), s32[]{:S(2)}) async-start(), calls=%async_computation.9 | async-start | bytes 2949120 | tf_op jit(solution)/shard_map/reduce_scatter | solution.py:679
  407.2 15.3 %collective-permute-start.62 = (bf16[32,1536]{1,0:T(8,128)(2,1)S(1)}, bf16[32,1536]{1,0:T(8,128)(2,1)S(1)}, u32[]{:S(2)}, u32[]{:S(2)}) collective-permute-start(bf16[32,1536]{1,0:T(8,128)(2,1)S(1)} %get-tuple-element.256), channel_id=1, source_target_pairs={{0,16},{1,17},{2,18},{3,19},{4,20},{5,21},{6,22},{7,23},{8,24},{9,... | collective-permute-start | bytes 294920 | tf_op jit(solution)/shard_map/ppermute | solution.py:142
  409.8 15.1 %collective-permute-start.61 = (bf16[32,1536]{1,0:T(8,128)(2,1)S(1)}, bf16[32,1536]{1,0:T(8,128)(2,1)S(1)}, u32[]{:S(2)}, u32[]{:S(2)}) collective-permute-start(bf16[32,1536]{1,0:T(8,128)(2,1)S(1)} %get-tuple-element.256), channel_id=1, source_target_pairs={{0,24},{1,25},{2,26},{3,27},{4,28},{5,29},{6,30},{7,31},{8,0},{9,1... | collective-permute-start | bytes 294920 | tf_op jit(solution)/shard_map/ppermute | solution.py:142
  411.1 13.8 %collective-permute-start.64 = (bf16[32,1536]{1,0:T(8,128)(2,1)S(1)}, bf16[32,1536]{1,0:T(8,128)(2,1)S(1)}, u32[]{:S(2)}, u32[]{:S(2)}) collective-permute-start(bf16[32,1536]{1,0:T(8,128)(2,1)S(1)} %get-tuple-element.256), channel_id=1, source_target_pairs={{0,4},{1,5},{2,6},{3,7},{4,0},{5,1},{6,2},{7,3},{8,12},{9,13},{10,... | collective-permute-start | bytes 294920 | tf_op jit(solution)/shard_map/ppermute | solution.py:142
  416.3 13.3 %collective-permute-start.67 = (bf16[32,1536]{1,0:T(8,128)(2,1)S(1)}, bf16[32,1536]{1,0:T(8,128)(2,1)S(1)}, u32[]{:S(2)}, u32[]{:S(2)}) collective-permute-start(bf16[32,1536]{1,0:T(8,128)(2,1)S(1)} %collective-permute-done.63), channel_id=1, source_target_pairs={{0,4},{1,5},{2,6},{3,7},{4,0},{5,1},{6,2},{7,3},{8,12},{9,13},{10,... | collective-permute-start | bytes 294920 | tf_op jit(solution)/shard_map/ppermute | solution.py:142
  437.1 12.8 %collective-permute-start.68 = (bf16[128,1536]{1,0:T(8,128)(2,1)S(1)}, bf16[128,1536]{1,0:T(8,128)(2,1)S(1)}, u32[]{:S(2)}, u32[]{:S(2)}) collective-permute-start(bf16[128,1536]{1,0:T(8,128)(2,1)S(1)} %slice.1367), channel_id=1, source_target_pairs={{0,4},{1,5},{2,6},{3,7},{4,0},{5,1},{6,2},{7,3},{8,12},{9,13},{10,... | collective-permute-start | bytes 1179656 | tf_op jit(solution)/shard_map/ppermute | solution.py:142
  450.0 12.1 %collective-permute-start.69 = (bf16[32,1536]{1,0:T(8,128)(2,1)S(1)}, bf16[32,1536]{1,0:T(8,128)(2,1)S(1)}, u32[]{:S(2)}, u32[]{:S(2)}) collective-permute-start(bf16[32,1536]{1,0:T(8,128)(2,1)S(1)} %get-tuple-element.412), channel_id=1, source_target_pairs={{0,8},{1,9},{2,10},{3,11},{4,12},{5,13},{6,14},{7,15},{8,16},{9,17... | collective-permute-start | bytes 294920 | tf_op jit(solution)/shard_map/ppermute | solution.py:142
  480.2 14.1 %collective-permute-start.72 = (bf16[256,1536]{1,0:T(8,128)(2,1)}, bf16[256,1536]{1,0:T(8,128)(2,1)}, u32[]{:S(2)}, u32[]{:S(2)}) collective-permute-start(bf16[256,1536]{1,0:T(8,128)(2,1)} %slice_add_fusion.6), channel_id=1, source_target_pairs={{0,1},{1,0},{2,3},{3,2},{4,5},{5,4},{6,7},{7,6},{8,9},{9,8},{10,11... | collective-permute-start | bytes 2359304 | tf_op jit(solution)/shard_map/ppermute | solution.py:142
  480.7 128.2 %all-gather.18.cloned.1.call-start = ((), (), s32[]{:S(2)}) async-start(), calls=%async_computation.14 | async-start | bytes 2949120 | tf_op jit(solution)/shard_map/all_gather | solution.py:734
  500.4 39.6 %collective-permute-start.75 = (bf16[4,192,768]{2,1,0:T(8,128)(2,1)}, bf16[4,192,768]{2,1,0:T(8,128)(2,1)}, u32[]{:S(2)}, u32[]{:S(2)}) collective-permute-start(bf16[4,192,768]{2,1,0:T(8,128)(2,1)} %fusion.96), channel_id=1, source_target_pairs={{0,4},{1,5},{2,6},{3,7},{4,0},{5,1},{6,2},{7,3},{8,12},{9,13},{10,... | collective-permute-start | bytes 3538952 | tf_op jit(solution)/shard_map/ppermute | solution.py:142
  548.6 71.4 %reduce-scatter.14.cloned.1.call-start = ((), (), s32[]{:S(2)}) async-start(), calls=%async_computation.10 | async-start | bytes 2949120 | tf_op jit(solution)/shard_map/reduce_scatter | solution.py:679
  549.4 159.1 %all-gather.14.cloned.1.call-start = ((), (), s32[]{:S(2)}) async-start(), calls=%async_computation.12 | async-start | bytes 2949120 | tf_op jit(solution)/shard_map/all_gather | solution.py:735
  553.7 11.7 %collective-permute-start.77 = (bf16[128,1536]{1,0:T(8,128)(2,1)}, bf16[128,1536]{1,0:T(8,128)(2,1)}, u32[]{:S(2)}, u32[]{:S(2)}) collective-permute-start(bf16[128,1536]{1,0:T(8,128)(2,1)} %slice.1094), channel_id=1, source_target_pairs={{0,4},{1,5},{2,6},{3,7},{4,0},{5,1},{6,2},{7,3},{8,12},{9,13},{10,... | collective-permute-start | bytes 1179656 | tf_op jit(solution)/shard_map/ppermute | solution.py:142
  558.0 11.1 %collective-permute-start.83 = (bf16[192,768]{1,0:T(8,128)(2,1)}, bf16[192,768]{1,0:T(8,128)(2,1)}, u32[]{:S(2)}, u32[]{:S(2)}) collective-permute-start(bf16[192,768]{1,0:T(8,128)(2,1)} %get-tuple-element.368), channel_id=1, source_target_pairs={{0,24},{1,25},{2,26},{3,27},{4,28},{5,29},{6,30},{7,31},{8,0},{9,1... | collective-permute-start | bytes 884744 | tf_op jit(solution)/shard_map/ppermute | solution.py:142
  561.3 28.6 %collective-permute-start.82 = (bf16[192,768]{1,0:T(8,128)(2,1)}, bf16[192,768]{1,0:T(8,128)(2,1)}, u32[]{:S(2)}, u32[]{:S(2)}) collective-permute-start(bf16[192,768]{1,0:T(8,128)(2,1)} %get-tuple-element.369), channel_id=1, source_target_pairs={{0,16},{1,17},{2,18},{3,19},{4,20},{5,21},{6,22},{7,23},{8,24},{9,... | collective-permute-start | bytes 884744 | tf_op jit(solution)/shard_map/ppermute | solution.py:142
  561.3 28.6 %collective-permute-start.81 = (bf16[192,768]{1,0:T(8,128)(2,1)}, bf16[192,768]{1,0:T(8,128)(2,1)}, u32[]{:S(2)}, u32[]{:S(2)}) collective-permute-start(bf16[192,768]{1,0:T(8,128)(2,1)} %get-tuple-element.370), channel_id=1, source_target_pairs={{0,8},{1,9},{2,10},{3,11},{4,12},{5,13},{6,14},{7,15},{8,16},{9,17... | collective-permute-start | bytes 884744 | tf_op jit(solution)/shard_map/ppermute | solution.py:142
  562.0 127.6 %collective-permute-start.92 = (bf16[1024,768]{1,0:T(8,128)(2,1)}, bf16[1024,768]{1,0:T(8,128)(2,1)}, u32[]{:S(2)}, u32[]{:S(2)}) collective-permute-start(bf16[1024,768]{1,0:T(8,128)(2,1)} %get-tuple-element.198), channel_id=1, source_target_pairs={{0,2},{1,3},{2,0},{3,1},{4,6},{5,7},{6,4},{7,5},{8,10},{9,11},{10,... | collective-permute-start | bytes 4718600 | tf_op jit(solution)/shard_map/ppermute | solution.py:142
  565.4 33.5 %collective-permute-start.86 = (bf16[4,192,896]{2,1,0:T(8,128)(2,1)}, bf16[4,192,896]{2,1,0:T(8,128)(2,1)}, u32[]{:S(2)}, u32[]{:S(2)}) collective-permute-start(bf16[4,192,896]{2,1,0:T(8,128)(2,1)} %dynamic-slice_bitcast_fusion.1), channel_id=1, source_target_pairs={{0,4},{1,5},{2,6},{3,7},{4,0},{5,1},{6,2},{7,3},{8,12},{9,13},{10,... | collective-permute-start | bytes 4128776 | tf_op jit(solution)/shard_map/ppermute | solution.py:142
  569.1 23.8 %collective-permute-start.78 = (bf16[32,1536]{1,0:T(8,128)(2,1)S(1)}, bf16[32,1536]{1,0:T(8,128)(2,1)S(1)}, u32[]{:S(2)}, u32[]{:S(2)}) collective-permute-start(bf16[32,1536]{1,0:T(8,128)(2,1)S(1)} %get-tuple-element.409), channel_id=1, source_target_pairs={{0,8},{1,9},{2,10},{3,11},{4,12},{5,13},{6,14},{7,15},{8,16},{9,17... | collective-permute-start | bytes 294920 | tf_op jit(solution)/shard_map/ppermute | solution.py:142
  598.0 110.5 %all-gather.12.cloned.1.call-start = ((), (), s32[]{:S(2)}) async-start(), calls=%async_computation.11 | async-start | bytes 2949120 | tf_op jit(solution)/shard_map/all_gather | solution.py:743
  604.3 27.4 %collective-permute-start.89 = (bf16[192,896]{1,0:T(8,128)(2,1)}, bf16[192,896]{1,0:T(8,128)(2,1)}, u32[]{:S(2)}, u32[]{:S(2)}) collective-permute-start(bf16[192,896]{1,0:T(8,128)(2,1)} %get-tuple-element.341), channel_id=1, source_target_pairs={{0,24},{1,25},{2,26},{3,27},{4,28},{5,29},{6,30},{7,31},{8,0},{9,1... | collective-permute-start | bytes 1032200 | tf_op jit(solution)/shard_map/ppermute | solution.py:142
  607.5 29.2 %collective-permute-start.88 = (bf16[192,896]{1,0:T(8,128)(2,1)}, bf16[192,896]{1,0:T(8,128)(2,1)}, u32[]{:S(2)}, u32[]{:S(2)}) collective-permute-start(bf16[192,896]{1,0:T(8,128)(2,1)} %get-tuple-element.342), channel_id=1, source_target_pairs={{0,16},{1,17},{2,18},{3,19},{4,20},{5,21},{6,22},{7,23},{8,24},{9,... | collective-permute-start | bytes 1032200 | tf_op jit(solution)/shard_map/ppermute | solution.py:142
  607.5 29.2 %collective-permute-start.87 = (bf16[192,896]{1,0:T(8,128)(2,1)}, bf16[192,896]{1,0:T(8,128)(2,1)}, u32[]{:S(2)}, u32[]{:S(2)}) collective-permute-start(bf16[192,896]{1,0:T(8,128)(2,1)} %get-tuple-element.343), channel_id=1, source_target_pairs={{0,8},{1,9},{2,10},{3,11},{4,12},{5,13},{6,14},{7,15},{8,16},{9,17... | collective-permute-start | bytes 1032200 | tf_op jit(solution)/shard_map/ppermute | solution.py:142
  642.2 23.6 %collective-permute-start.93 = (bf16[2,96,768]{2,1,0:T(8,128)(2,1)}, bf16[2,96,768]{2,1,0:T(8,128)(2,1)S(1)}, u32[]{:S(2)}, u32[]{:S(2)}) collective-permute-start(bf16[2,96,768]{2,1,0:T(8,128)(2,1)} %pad_maximum_fusion.29), channel_id=1, source_target_pairs={{0,8},{1,9},{2,10},{3,11},{4,12},{5,13},{6,14},{7,15},{8,16},{9,17... | collective-permute-start | bytes 884744 | tf_op jit(solution)/shard_map/ppermute | solution.py:142
  644.2 20.6 %collective-permute-start.94 = (bf16[2,96,768]{2,1,0:T(8,128)(2,1)}, bf16[2,96,768]{2,1,0:T(8,128)(2,1)}, u32[]{:S(2)}, u32[]{:S(2)}) collective-permute-start(bf16[2,96,768]{2,1,0:T(8,128)(2,1)} %pad_maximum_fusion.30), channel_id=1, source_target_pairs={{0,16},{1,17},{2,18},{3,19},{4,20},{5,21},{6,22},{7,23},{8,24},{9,... | collective-permute-start | bytes 884744 | tf_op jit(solution)/shard_map/ppermute | solution.py:142
  646.9 15.2 %collective-permute-start.95 = (bf16[2,96,768]{2,1,0:T(8,128)(2,1)}, bf16[2,96,768]{2,1,0:T(8,128)(2,1)}, u32[]{:S(2)}, u32[]{:S(2)}) collective-permute-start(bf16[2,96,768]{2,1,0:T(8,128)(2,1)} %pad_maximum_fusion.31), channel_id=1, source_target_pairs={{0,24},{1,25},{2,26},{3,27},{4,28},{5,29},{6,30},{7,31},{8,0},{9,1... | collective-permute-start | bytes 884744 | tf_op jit(solution)/shard_map/ppermute | solution.py:142
  650.5 82.0 %all-gather.20.cloned.1.call-start = ((), (), s32[]{:S(2)}) async-start(), calls=%async_computation.15 | async-start | bytes 5898240 | tf_op jit(solution)/shard_map/all_gather | solution.py:767
  656.2 36.2 %collective-permute-start.98 = (bf16[192,1664]{1,0:T(8,128)(2,1)S(1)}, bf16[192,1664]{1,0:T(8,128)(2,1)S(1)}, u32[]{:S(2)}, u32[]{:S(2)}) collective-permute-start(bf16[192,1664]{1,0:T(8,128)(2,1)S(1)} %get-tuple-element.388), channel_id=1, source_target_pairs={{0,2},{1,3},{2,0},{3,1},{4,6},{5,7},{6,4},{7,5},{8,10},{9,11},{10,... | collective-permute-start | bytes 1916936 | tf_op jit(solution)/shard_map/ppermute | solution.py:142
  665.9 15.2 %collective-permute-start.96 = (bf16[4,96,768]{2,1,0:T(8,128)(2,1)S(1)}, bf16[4,96,768]{2,1,0:T(8,128)(2,1)S(1)}, u32[]{:S(2)}, u32[]{:S(2)}) collective-permute-start(bf16[4,96,768]{2,1,0:T(8,128)(2,1)S(1)} %pad_maximum_fusion.18), channel_id=1, source_target_pairs={{0,4},{1,5},{2,6},{3,7},{4,0},{5,1},{6,2},{7,3},{8,12},{9,13},{10,... | collective-permute-start | bytes 1769480 | tf_op jit(solution)/shard_map/ppermute | solution.py:142
  (289 other events, 1856.1 us)
Sparse Core Ops, SparseCore 0:
  27.3 76.0 all-gather.15
  106.1 94.1 all-gather.9
  324.6 31.9 reduce-scatter.7
  359.7 33.1 reduce-scatter.5
  398.9 105.0 reduce-scatter.9
  507.0 34.9 reduce-scatter.11
  548.7 30.4 all-gather.17
  581.9 36.7 reduce-scatter.13
  620.3 24.1 all-gather.13
  650.6 33.1 all-gather.11
  689.0 43.4 all-gather.19

commit v4 on v3

--- a/solution.py
+++ b/solution.py
@@ -206,8 +206,9 @@
             return lax.psum_scatter(partial, "dp", scatter_dimension=0, tiled=True)
         n = self.depth
         half = partial.shape[0] // 2
-        got = self.send(partial[half:].astype(bf16), self.swap_x)
-        near = partial[:half] + got.astype(f32)
+        partial = partial.astype(bf16)
+        got = self.send(partial[half:], self.swap_x)
+        near = partial[:half].astype(f32) + got.astype(f32)
         low = near.astype(bf16).reshape((n, half // n) + partial.shape[1:])
         total = near[: half // n]
         for k in range(1, n):

time: 756 us -> 756 us (level)
  no operation moved by 1% of the time
where the time goes in v4:
time: 756 us; the launch traced here: 746 us
  waiting for transfers between devices  163 us (22%)
  starting transfers between devices  154 us (20%)
  matrix products  127 us (17%)
  other arithmetic  121 us (16%)
  local copies, waits for them, and re-layouts  114 us (15%)
  between operations  54.3 us (7%)
  Pallas kernels  13.4 us (2%)
    ppermute x100, starting transfers between devices, send(): return lax.ppermute(value, AXES, pairs)  153 us
    ppermute x100, waiting for transfers between devices, send(): return lax.ppermute(value, AXES, pairs)  145 us
    dot_general x35, matrix products, dot(): return jnp.dot(left, right, preferred_element_type=f32)  47.6 us
    dot_general x29, matrix products, dot_cols(): lax.dot_general(left, right, (((1,), (1,)), ((), ())), preferred_element_...  43.8 us
    dot_general x16, matrix products, dot_rows(): lax.dot_general(left, right, (((0,), (0,)), ((), ())), preferred_element_...  35.8 us
    unnamed x504, local copies, waits for them, and re-layouts  34.4 us
    all_gather x1, waiting for transfers between devices, run(): inner = lax.all_gather(inner, 'section', axis=0)  17.2 us
  transfers between devices with their start and end apart: 111, of which 40 were waited for; matrix products, arithmetic and copies ran while one was open for 42% of the time, Pallas kernels for 2%

profile of v4, /device:TPU:0, one launch (start us, length us, event | category | flops | bytes accessed | tf_op | source)
XLA Modules:
  0.0 746.2 jit_solution(11222577802910512051)
XLA Ops:
  15.6 2.9 collective-permute-start.5
  20.1 2.6 collective-permute-start.3
  29.7 2.9 fusion.3
  36.3 4.4 fusion.4
  43.3 5.8 collective-permute-done.1
  56.9 2.9 constant_dynamic-slice_fusion.29
  60.5 10.2 %collective-permute-start.9 = (bf16[2,96,768]{2,1,0:T(8,128)(2,1)}, bf16[2,96,768]{2,1,0:T(8,128)(2,1)}, u32[]{:S(2)}, u32[]{:S(2)}) collective-permute-start(bf16[2,96,768]{2,1,0:T(8,128)(2,1)} %pad_maximum_fusion.25), channel_id=1, source_target_pairs={{0,8},{1,9},{2,10},{3,11},{4,12},{5,13},{6,14},{7,15},{8,16},{9,17... | collective-permute-start | bytes 884744 | tf_op jit(solution)/shard_map/ppermute | solution.py:142
  79.8 14.2 %collective-permute-done.6 = bf16[3,192,896]{2,1,0:T(8,128)(2,1)} collective-permute-done((bf16[3,192,896]{2,1,0:T(8,128)(2,1)}, bf16[3,192,896]{2,1,0:T(8,128)(2,1)}, u32[]{:S(2)}, u32[]{:S(2)}) %collective-permute-start.6) | collective-permute-done | bytes 1032224 | tf_op jit(solution)/shard_map/ppermute | solution.py:142
  101.2 2.7 collective-permute-done.7
  118.4 3.1 fusion.403
  139.5 7.8 %collective-permute-done.12.refs_0_ = bf16[4,96,768]{2,1,0:T(8,128)(2,1)} collective-permute-done((bf16[4,96,768]{2,1,0:T(8,128)(2,1)}, bf16[4,96,768]{2,1,0:T(8,128)(2,1)}, u32[]{:S(2)}, u32[]{:S(2)}) %collective-permute-start.12) | collective-permute-done | bytes 589856 | tf_op jit(solution)/shard_map/ppermute | solution.py:142
  161.9 13.5 %collective-permute-start.18 = (bf16[32,1536]{1,0:T(8,128)(2,1)S(1)}, bf16[32,1536]{1,0:T(8,128)(2,1)S(1)}, u32[]{:S(2)}, u32[]{:S(2)}) collective-permute-start(bf16[32,1536]{1,0:T(8,128)(2,1)S(1)} %get-tuple-element.264), channel_id=1, source_target_pairs={{0,8},{1,9},{2,10},{3,11},{4,12},{5,13},{6,14},{7,15},{8,16},{9,17... | collective-permute-start | bytes 294920 | tf_op jit(solution)/shard_map/ppermute | solution.py:142
  183.4 4.2 collective-permute-done.17
  189.7 4.3 collective-permute-done.20
  195.0 3.1 multiply_convert_fusion.7
  200.3 8.5 %collective-permute-done.24 = bf16[128,1536]{1,0:T(8,128)(2,1)S(1)} collective-permute-done((bf16[128,1536]{1,0:T(8,128)(2,1)S(1)}, bf16[128,1536]{1,0:T(8,128)(2,1)S(1)}, u32[]{:S(2)}, u32[]{:S(2)}) %collective-permute-start.24) | collective-permute-done | bytes 393248 | tf_op jit(solution)/shard_map/ppermute | solution.py:142
  209.0 7.1 collective-permute-start.25
  221.2 2.6 collective-permute-done.26
  227.1 3.2 collective-permute-start.48
  230.3 4.4 fusion.401
  241.0 3.3 collective-permute-start.47
  272.2 2.6 collective-permute-start.43
  279.2 4.0 collective-permute-done.33
  291.9 3.1 collective-permute-start.34
  300.6 9.6 %collective-permute-done.45 = bf16[8,48,768]{2,1,0:T(8,128)(2,1)S(1)} collective-permute-done((bf16[8,48,768]{2,1,0:T(8,128)(2,1)S(1)}, bf16[8,48,768]{2,1,0:T(8,128)(2,1)S(1)}, u32[]{:S(2)}, u32[]{:S(2)}) %collective-permute-start.45) | collective-permute-done | bytes 589856 | tf_op jit(solution)/shard_map/ppermute | solution.py:142
  310.7 4.0 collective-permute-done.38
  317.2 3.1 multiply_convert_fusion.6
  321.1 3.3 convolution_convert_fusion.2.refs_1_
  324.5 4.5 add_convert_fusion.1
  330.3 8.3 %collective-permute-done.51 = bf16[128,1536]{1,0:T(8,128)(2,1)S(1)} collective-permute-done((bf16[128,1536]{1,0:T(8,128)(2,1)S(1)}, bf16[128,1536]{1,0:T(8,128)(2,1)S(1)}, u32[]{:S(2)}, u32[]{:S(2)}) %collective-permute-start.51) | collective-permute-done | bytes 393248 | tf_op jit(solution)/shard_map/ppermute | solution.py:142
  371.7 3.1 fusion.15
  375.5 2.7 fusion.131
  395.0 3.7 maximum_maximum_fusion
  400.4 4.5 collective-permute-done.60
  413.4 3.0 collective-permute-done.63
  416.3 2.7 collective-permute-start.67
  419.1 3.5 collective-permute-done.62
  425.0 4.6 collective-permute-done.65
  431.8 4.4 add_convert_fusion
  438.7 5.5 fusion.16.refs_0_
  446.5 3.3 collective-permute-done.68
  450.0 8.3 %collective-permute-start.69 = (bf16[32,1536]{1,0:T(8,128)(2,1)S(1)}, bf16[32,1536]{1,0:T(8,128)(2,1)S(1)}, u32[]{:S(2)}, u32[]{:S(2)}) collective-permute-start(bf16[32,1536]{1,0:T(8,128)(2,1)S(1)} %get-tuple-element.412), channel_id=1, source_target_pairs={{0,8},{1,9},{2,10},{3,11},{4,12},{5,13},{6,14},{7,15},{8,16},{9,17... | collective-permute-start | bytes 294920 | tf_op jit(solution)/shard_map/ppermute | solution.py:142
  494.4 3.2 convolution_convert_fusion.4.refs_0_
  502.2 4.7 fusion.56
  520.3 10.3 %fusion.390 = (f32[1024]{0:T(1024)S(1)}, f32[1024]{0:T(1024)S(1)}, f32[1024,1536]{1,0:T(8,128)S(1)}) fusion(bf16[1024,1536]{1,0:T(8,128)(2,1)} %fusion.4, f32[1024,1536]{1,0:T(8,128)} %fusion.16.refs_0_, bf16[512,1536]{1,0:T(8,128)(2,1)} %get-tuple-element.291, bf16[512,1536]{1,0:T(8,128)(2,1)} %copy-done.88, bf16[]{:T(256)} %bitcast.100, ...), kind=kOutput, calls=%fused_computation.873 | convolution fusion | flops 3242719232 | bytes 20979714 | tf_op jit(solution)/shard_map/dot_general | solution.py:23
  534.2 2.7 copy-done.4
  550.1 2.6 fusion.35
  553.7 3.3 fusion.392
  558.0 3.3 collective-permute-start.83
  569.0 15.6 %collective-permute-start.78 = (bf16[32,1536]{1,0:T(8,128)(2,1)S(1)}, bf16[32,1536]{1,0:T(8,128)(2,1)S(1)}, u32[]{:S(2)}, u32[]{:S(2)}) collective-permute-start(bf16[32,1536]{1,0:T(8,128)(2,1)S(1)} %get-tuple-element.409), channel_id=1, source_target_pairs={{0,8},{1,9},{2,10},{3,11},{4,12},{5,13},{6,14},{7,15},{8,16},{9,17... | collective-permute-start | bytes 294920 | tf_op jit(solution)/shard_map/ppermute | solution.py:142
  584.7 5.2 collective-permute-done.82.refs_1_
  592.9 2.6 collective-permute-done.80
  600.1 3.2 fusion.391
  604.4 3.2 collective-permute-start.89
  627.4 2.7 scatter.35.refs_5_
  631.8 5.0 collective-permute-done.88.refs_2_
  646.9 2.9 collective-permute-start.95
  658.5 3.6 collective-permute-done.95
  671.0 10.2 %collective-permute-done.96 = bf16[4,96,768]{2,1,0:T(8,128)(2,1)S(1)} collective-permute-done((bf16[4,96,768]{2,1,0:T(8,128)(2,1)S(1)}, bf16[4,96,768]{2,1,0:T(8,128)(2,1)S(1)}, u32[]{:S(2)}, u32[]{:S(2)}) %collective-permute-start.96) | collective-permute-done | bytes 589856 | tf_op jit(solution)/shard_map/ppermute | solution.py:142
  689.6 2.7 convert_add_fusion
  708.5 6.8 maximum_convert_fusion.1
  715.3 17.2 %all-gather.20.cloned.1.call-done = bf16[8,48,6144]{2,1,0:T(8,128)(2,1)} async-done(((bf16[2,48,6144]{2,1,0:T(8,128)(2,1)}), bf16[8,48,6144]{2,1,0:T(8,128)(2,1)}) %all-gather.20.cloned.1.call-update) | async-done | bytes 4718608 | tf_op jit(solution)/shard_map/all_gather | solution.py:768
  732.5 2.7 fusion.400
  735.2 4.4 maximum_convert_fusion
  (1107 shorter events, 368.3 us)
Async XLA Ops:
  7.2 110.7 %all-gather.16.cloned.1.call-start = ((), (), s32[]{:S(2)}) async-start(), calls=%async_computation.13 | async-start | bytes 2654208 | tf_op jit(solution)/shard_map/all_gather | solution.py:343
  15.6 63.2 %collective-permute-start.5 = (bf16[192,896]{1,0:T(8,128)(2,1)}, bf16[192,896]{1,0:T(8,128)(2,1)}, u32[]{:S(2)}, u32[]{:S(2)}) collective-permute-start(bf16[192,896]{1,0:T(8,128)(2,1)} %pad_maximum_fusion.21), channel_id=1, source_target_pairs={{0,4},{1,5},{2,6},{3,7},{4,0},{5,1},{6,2},{7,3},{8,12},{9,13},{10,... | collective-permute-start | bytes 1032200 | tf_op jit(solution)/shard_map/ppermute | solution.py:142
  18.5 32.0 %collective-permute-start.4 = (bf16[192,896]{1,0:T(8,128)(2,1)}, bf16[192,896]{1,0:T(8,128)(2,1)S(1)}, u32[]{:S(2)}, u32[]{:S(2)}) collective-permute-start(bf16[192,896]{1,0:T(8,128)(2,1)} %pad_maximum_fusion.21), channel_id=1, source_target_pairs={{0,8},{1,9},{2,10},{3,11},{4,12},{5,13},{6,14},{7,15},{8,16},{9,17... | collective-permute-start | bytes 1032200 | tf_op jit(solution)/shard_map/ppermute | solution.py:142
  20.1 32.1 %collective-permute-start.3 = (bf16[192,896]{1,0:T(8,128)(2,1)}, bf16[192,896]{1,0:T(8,128)(2,1)}, u32[]{:S(2)}, u32[]{:S(2)}) collective-permute-start(bf16[192,896]{1,0:T(8,128)(2,1)} %pad_maximum_fusion.21), channel_id=1, source_target_pairs={{0,16},{1,17},{2,18},{3,19},{4,20},{5,21},{6,22},{7,23},{8,24},{9,... | collective-permute-start | bytes 1032200 | tf_op jit(solution)/shard_map/ppermute | solution.py:142
  22.7 29.6 %collective-permute-start.2 = (bf16[192,896]{1,0:T(8,128)(2,1)}, bf16[192,896]{1,0:T(8,128)(2,1)}, u32[]{:S(2)}, u32[]{:S(2)}) collective-permute-start(bf16[192,896]{1,0:T(8,128)(2,1)} %pad_maximum_fusion.21), channel_id=1, source_target_pairs={{0,24},{1,25},{2,26},{3,27},{4,28},{5,29},{6,30},{7,31},{8,0},{9,1... | collective-permute-start | bytes 1032200 | tf_op jit(solution)/shard_map/ppermute | solution.py:142
  24.7 16.0 %collective-permute-start = (bf16[2,64,384]{2,1,0:T(8,128)(2,1)}, bf16[2,64,384]{2,1,0:T(8,128)(2,1)}, u32[]{:S(2)}, u32[]{:S(2)}) collective-permute-start(bf16[2,64,384]{2,1,0:T(8,128)(2,1)} %get-tuple-element.446), channel_id=1, source_target_pairs={{0,1},{1,0},{2,3},{3,2},{4,5},{5,4},{6,7},{7,6},{8,9},{9,8},{10,11... | collective-permute-start | bytes 294920 | tf_op jit(solution)/shard_map/ppermute | solution.py:142
  27.2 197.4 %all-gather.10.cloned.1.call-start = ((), (), s32[]{:S(2)}) async-start(), calls=%async_computation.5 | async-start | bytes 5308416 | tf_op jit(solution)/shard_map/all_gather | solution.py:346
  56.3 37.6 %collective-permute-start.6 = (bf16[3,192,896]{2,1,0:T(8,128)(2,1)}, bf16[3,192,896]{2,1,0:T(8,128)(2,1)}, u32[]{:S(2)}, u32[]{:S(2)}) collective-permute-start(bf16[3,192,896]{2,1,0:T(8,128)(2,1)} %pad_maximum_fusion.14), channel_id=1, source_target_pairs={{0,4},{1,5},{2,6},{3,7},{4,0},{5,1},{6,2},{7,3},{8,12},{9,13},{10,... | collective-permute-start | bytes 3096584 | tf_op jit(solution)/shard_map/ppermute | solution.py:142
  60.5 66.4 %collective-permute-start.9 = (bf16[2,96,768]{2,1,0:T(8,128)(2,1)}, bf16[2,96,768]{2,1,0:T(8,128)(2,1)}, u32[]{:S(2)}, u32[]{:S(2)}) collective-permute-start(bf16[2,96,768]{2,1,0:T(8,128)(2,1)} %pad_maximum_fusion.25), channel_id=1, source_target_pairs={{0,8},{1,9},{2,10},{3,11},{4,12},{5,13},{6,14},{7,15},{8,16},{9,17... | collective-permute-start | bytes 884744 | tf_op jit(solution)/shard_map/ppermute | solution.py:142
  71.4 53.8 %collective-permute-start.10 = (bf16[2,96,768]{2,1,0:T(8,128)(2,1)}, bf16[2,96,768]{2,1,0:T(8,128)(2,1)}, u32[]{:S(2)}, u32[]{:S(2)}) collective-permute-start(bf16[2,96,768]{2,1,0:T(8,128)(2,1)} %pad_maximum_fusion.26), channel_id=1, source_target_pairs={{0,16},{1,17},{2,18},{3,19},{4,20},{5,21},{6,22},{7,23},{8,24},{9,... | collective-permute-start | bytes 884744 | tf_op jit(solution)/shard_map/ppermute | solution.py:142
  73.7 50.6 %collective-permute-start.11 = (bf16[2,96,768]{2,1,0:T(8,128)(2,1)}, bf16[2,96,768]{2,1,0:T(8,128)(2,1)}, u32[]{:S(2)}, u32[]{:S(2)}) collective-permute-start(bf16[2,96,768]{2,1,0:T(8,128)(2,1)} %pad_maximum_fusion.27), channel_id=1, source_target_pairs={{0,24},{1,25},{2,26},{3,27},{4,28},{5,29},{6,30},{7,31},{8,0},{9,1... | collective-permute-start | bytes 884744 | tf_op jit(solution)/shard_map/ppermute | solution.py:142
  76.4 388.3 %reduce-scatter.8.cloned.1.call-start = ((), (), s32[]{:S(2)}) async-start(), calls=%async_computation.7 | async-start | bytes 2949120 | tf_op jit(solution)/shard_map/reduce_scatter | solution.py:680
  121.5 13.3 %collective-permute-start.13 = (bf16[1536,384]{1,0:T(8,128)(2,1)}, bf16[1536,384]{1,0:T(8,128)(2,1)}, u32[]{:S(2)}, u32[]{:S(2)}) collective-permute-start(bf16[1536,384]{1,0:T(8,128)(2,1)} %bitcast.34), channel_id=1, source_target_pairs={{0,1},{1,0},{2,3},{3,2},{4,5},{5,4},{6,7},{7,6},{8,9},{9,8},{10,11... | collective-permute-start | bytes 3538952 | tf_op jit(solution)/shard_map/ppermute | solution.py:142
  123.1 14.0 %collective-permute-start.14 = (bf16[768,768]{1,0:T(8,128)(2,1)S(1)}, bf16[768,768]{1,0:T(8,128)(2,1)}, u32[]{:S(2)}, u32[]{:S(2)}) collective-permute-start(bf16[768,768]{1,0:T(8,128)(2,1)S(1)} %pad_maximum_fusion.7), channel_id=1, source_target_pairs={{0,1},{1,0},{2,3},{3,2},{4,5},{5,4},{6,7},{7,6},{8,9},{9,8},{10,11... | collective-permute-start | bytes 3538952 | tf_op jit(solution)/shard_map/ppermute | solution.py:142
  131.7 15.6 %collective-permute-start.12 = (bf16[4,96,768]{2,1,0:T(8,128)(2,1)}, bf16[4,96,768]{2,1,0:T(8,128)(2,1)}, u32[]{:S(2)}, u32[]{:S(2)}) collective-permute-start(bf16[4,96,768]{2,1,0:T(8,128)(2,1)} %pad_maximum_fusion.17), channel_id=1, source_target_pairs={{0,4},{1,5},{2,6},{3,7},{4,0},{5,1},{6,2},{7,3},{8,12},{9,13},{10,... | collective-permute-start | bytes 1769480 | tf_op jit(solution)/shard_map/ppermute | solution.py:142
  161.9 20.9 %collective-permute-start.18 = (bf16[32,1536]{1,0:T(8,128)(2,1)S(1)}, bf16[32,1536]{1,0:T(8,128)(2,1)S(1)}, u32[]{:S(2)}, u32[]{:S(2)}) collective-permute-start(bf16[32,1536]{1,0:T(8,128)(2,1)S(1)} %get-tuple-element.264), channel_id=1, source_target_pairs={{0,8},{1,9},{2,10},{3,11},{4,12},{5,13},{6,14},{7,15},{8,16},{9,17... | collective-permute-start | bytes 294920 | tf_op jit(solution)/shard_map/ppermute | solution.py:142
  175.4 12.2 %collective-permute-start.17 = (bf16[32,1536]{1,0:T(8,128)(2,1)S(1)}, bf16[32,1536]{1,0:T(8,128)(2,1)S(1)}, u32[]{:S(2)}, u32[]{:S(2)}) collective-permute-start(bf16[32,1536]{1,0:T(8,128)(2,1)S(1)} %get-tuple-element.264), channel_id=1, source_target_pairs={{0,16},{1,17},{2,18},{3,19},{4,20},{5,21},{6,22},{7,23},{8,24},{9,... | collective-permute-start | bytes 294920 | tf_op jit(solution)/shard_map/ppermute | solution.py:142
  180.6 13.5 %collective-permute-start.23 = (bf16[8,96,768]{2,1,0:T(8,128)(2,1)S(1)}, bf16[8,96,768]{2,1,0:T(8,128)(2,1)S(1)}, u32[]{:S(2)}, u32[]{:S(2)}) collective-permute-start(bf16[8,96,768]{2,1,0:T(8,128)(2,1)S(1)} %slice_dynamic-update-slice_fusion.3), channel_id=1, source_target_pairs={{0,1},{1,0},{2,3},{3,2},{4,5},{5,4},{6,7},{7,6},{8,9},{9,8},{10,11... | collective-permute-start | bytes 3538952 | tf_op jit(solution)/shard_map/ppermute | solution.py:142
  182.9 11.2 %collective-permute-start.22 = (bf16[32,1536]{1,0:T(8,128)(2,1)S(1)}, bf16[32,1536]{1,0:T(8,128)(2,1)S(1)}, u32[]{:S(2)}, u32[]{:S(2)}) collective-permute-start(bf16[32,1536]{1,0:T(8,128)(2,1)S(1)} %collective-permute-done.18), channel_id=1, source_target_pairs={{0,4},{1,5},{2,6},{3,7},{4,0},{5,1},{6,2},{7,3},{8,12},{9,13},{10,... | collective-permute-start | bytes 294920 | tf_op jit(solution)/shard_map/ppermute | solution.py:142
  227.1 57.3 %collective-permute-start.49 = (bf16[32,1536]{1,0:T(8,128)(2,1)}, bf16[32,1536]{1,0:T(8,128)(2,1)}, u32[]{:S(2)}, u32[]{:S(2)}) collective-permute-start(bf16[32,1536]{1,0:T(8,128)(2,1)} %add_bitcast_fusion.2), channel_id=1, source_target_pairs={{0,8},{1,9},{2,10},{3,11},{4,12},{5,13},{6,14},{7,15},{8,16},{9,17... | collective-permute-start | bytes 294920 | tf_op jit(solution)/shard_map/ppermute | solution.py:142
  227.1 58.2 %collective-permute-start.48 = (bf16[32,1536]{1,0:T(8,128)(2,1)}, bf16[32,1536]{1,0:T(8,128)(2,1)}, u32[]{:S(2)}, u32[]{:S(2)}) collective-permute-start(bf16[32,1536]{1,0:T(8,128)(2,1)} %add_bitcast_fusion.2), channel_id=1, source_target_pairs={{0,16},{1,17},{2,18},{3,19},{4,20},{5,21},{6,22},{7,23},{8,24},{9,... | collective-permute-start | bytes 294920 | tf_op jit(solution)/shard_map/ppermute | solution.py:142
  236.3 12.2 %collective-permute-start.30 = (bf16[1536,384]{1,0:T(8,128)(2,1)}, bf16[1536,384]{1,0:T(8,128)(2,1)}, u32[]{:S(2)}, u32[]{:S(2)}) collective-permute-start(bf16[1536,384]{1,0:T(8,128)(2,1)} %bitcast.50), channel_id=1, source_target_pairs={{0,1},{1,0},{2,3},{3,2},{4,5},{5,4},{6,7},{7,6},{8,9},{9,8},{10,11... | collective-permute-start | bytes 3538952 | tf_op jit(solution)/shard_map/ppermute | solution.py:142
  241.0 44.3 %collective-permute-start.47 = (bf16[32,1536]{1,0:T(8,128)(2,1)}, bf16[32,1536]{1,0:T(8,128)(2,1)}, u32[]{:S(2)}, u32[]{:S(2)}) collective-permute-start(bf16[32,1536]{1,0:T(8,128)(2,1)} %add_bitcast_fusion.2), channel_id=1, source_target_pairs={{0,24},{1,25},{2,26},{3,27},{4,28},{5,29},{6,30},{7,31},{8,0},{9,1... | collective-permute-start | bytes 294920 | tf_op jit(solution)/shard_map/ppermute | solution.py:142
  244.6 18.9 %collective-permute-start.32 = (bf16[768,768]{1,0:T(8,128)(2,1)S(1)}, bf16[768,768]{1,0:T(8,128)(2,1)S(1)}, u32[]{:S(2)}, u32[]{:S(2)}) collective-permute-start(bf16[768,768]{1,0:T(8,128)(2,1)S(1)} %pad_maximum_fusion.8), channel_id=1, source_target_pairs={{0,1},{1,0},{2,3},{3,2},{4,5},{5,4},{6,7},{7,6},{8,9},{9,8},{10,11... | collective-permute-start | bytes 3538952 | tf_op jit(solution)/shard_map/ppermute | solution.py:142
  248.5 12.7 %collective-permute-start.31 = (bf16[1536,384]{1,0:T(8,128)(2,1)S(1)}, bf16[1536,384]{1,0:T(8,128)(2,1)S(1)}, u32[]{:S(2)}, u32[]{:S(2)}) collective-permute-start(bf16[1536,384]{1,0:T(8,128)(2,1)S(1)} %bitcast.564), channel_id=1, source_target_pairs={{0,1},{1,0},{2,3},{3,2},{4,5},{5,4},{6,7},{7,6},{8,9},{9,8},{10,11... | collective-permute-start | bytes 3538952 | tf_op jit(solution)/shard_map/ppermute | solution.py:142
  261.2 11.0 %collective-permute-start.41 = (bf16[2,48,768]{2,1,0:T(8,128)(2,1)}, bf16[2,48,768]{2,1,0:T(8,128)(2,1)}, u32[]{:S(2)}, u32[]{:S(2)}) collective-permute-start(bf16[2,48,768]{2,1,0:T(8,128)(2,1)} %pad_maximum_fusion.34), channel_id=1, source_target_pairs={{0,8},{1,9},{2,10},{3,11},{4,12},{5,13},{6,14},{7,15},{8,16},{9,17... | collective-permute-start | bytes 442376 | tf_op jit(solution)/shard_map/ppermute | solution.py:142
  263.5 15.0 %collective-permute-start.42 = (bf16[2,48,768]{2,1,0:T(8,128)(2,1)}, bf16[2,48,768]{2,1,0:T(8,128)(2,1)S(1)}, u32[]{:S(2)}, u32[]{:S(2)}) collective-permute-start(bf16[2,48,768]{2,1,0:T(8,128)(2,1)} %pad_maximum_fusion.35), channel_id=1, source_target_pairs={{0,16},{1,17},{2,18},{3,19},{4,20},{5,21},{6,22},{7,23},{8,24},{9,... | collective-permute-start | bytes 442376 | tf_op jit(solution)/shard_map/ppermute | solution.py:142
  279.1 15.9 %collective-permute-start.44 = (bf16[4,48,768]{2,1,0:T(8,128)(2,1)S(1)}, bf16[4,48,768]{2,1,0:T(8,128)(2,1)S(1)}, u32[]{:S(2)}, u32[]{:S(2)}) collective-permute-start(bf16[4,48,768]{2,1,0:T(8,128)(2,1)S(1)} %pad_maximum_fusion.28), channel_id=1, source_target_pairs={{0,4},{1,5},{2,6},{3,7},{4,0},{5,1},{6,2},{7,3},{8,12},{9,13},{10,... | collective-permute-start | bytes 884744 | tf_op jit(solution)/shard_map/ppermute | solution.py:142
  289.8 30.6 %collective-permute-start.50 = (bf16[128,1536]{1,0:T(8,128)(2,1)}, bf16[128,1536]{1,0:T(8,128)(2,1)}, u32[]{:S(2)}, u32[]{:S(2)}) collective-permute-start(bf16[128,1536]{1,0:T(8,128)(2,1)} %maximum_add_fusion.5), channel_id=1, source_target_pairs={{0,4},{1,5},{2,6},{3,7},{4,0},{5,1},{6,2},{7,3},{8,12},{9,13},{10,... | collective-permute-start | bytes 1179656 | tf_op jit(solution)/shard_map/ppermute | solution.py:142
  290.4 20.2 %collective-permute-start.37 = (bf16[32,1536]{1,0:T(8,128)(2,1)}, bf16[32,1536]{1,0:T(8,128)(2,1)S(1)}, u32[]{:S(2)}, u32[]{:S(2)}) collective-permute-start(bf16[32,1536]{1,0:T(8,128)(2,1)} %get-tuple-element.258), channel_id=1, source_target_pairs={{0,4},{1,5},{2,6},{3,7},{4,0},{5,1},{6,2},{7,3},{8,12},{9,13},{10,... | collective-permute-start | bytes 294920 | tf_op jit(solution)/shard_map/ppermute | solution.py:142
  294.9 19.9 %collective-permute-start.40 = (bf16[32,1536]{1,0:T(8,128)(2,1)}, bf16[32,1536]{1,0:T(8,128)(2,1)S(1)}, u32[]{:S(2)}, u32[]{:S(2)}) collective-permute-start(bf16[32,1536]{1,0:T(8,128)(2,1)} %collective-permute-done.36), channel_id=1, source_target_pairs={{0,4},{1,5},{2,6},{3,7},{4,0},{5,1},{6,2},{7,3},{8,12},{9,13},{10,... | collective-permute-start | bytes 294920 | tf_op jit(solution)/shard_map/ppermute | solution.py:142
  295.0 19.7 %collective-permute-start.39 = (bf16[32,1536]{1,0:T(8,128)(2,1)}, bf16[32,1536]{1,0:T(8,128)(2,1)S(1)}, u32[]{:S(2)}, u32[]{:S(2)}) collective-permute-start(bf16[32,1536]{1,0:T(8,128)(2,1)} %collective-permute-done.35), channel_id=1, source_target_pairs={{0,4},{1,5},{2,6},{3,7},{4,0},{5,1},{6,2},{7,3},{8,12},{9,13},{10,... | collective-permute-start | bytes 294920 | tf_op jit(solution)/shard_map/ppermute | solution.py:142
  298.3 11.9 %collective-permute-start.45 = (bf16[8,48,768]{2,1,0:T(8,128)(2,1)S(1)}, bf16[8,48,768]{2,1,0:T(8,128)(2,1)S(1)}, u32[]{:S(2)}, u32[]{:S(2)}) collective-permute-start(bf16[8,48,768]{2,1,0:T(8,128)(2,1)S(1)} %slice_dynamic-update-slice_fusion.7), channel_id=1, source_target_pairs={{0,2},{1,3},{2,0},{3,1},{4,6},{5,7},{6,4},{7,5},{8,10},{9,11},{10,... | collective-permute-start | bytes 1769480 | tf_op jit(solution)/shard_map/ppermute | solution.py:142
  324.5 140.2 %reduce-scatter.6.cloned.1.call-start = ((), (), s32[]{:S(2)}) async-start(), calls=%async_computation.6 | async-start | bytes 2949120 | tf_op jit(solution)/shard_map/reduce_scatter | solution.py:680
  355.7 192.3 %reduce-scatter.10.cloned.1.call-start = ((), (), s32[]{:S(2)}) async-start(), calls=%async_computation.8 | async-start | bytes 5308416 | tf_op jit(solution)/shard_map/reduce_scatter | solution.py:702
  398.8 200.1 %reduce-scatter.12.cloned.1.call-start = ((), (), s32[]{:S(2)}) async-start(), calls=%async_computation.9 | async-start | bytes 2949120 | tf_op jit(solution)/shard_map/reduce_scatter | solution.py:680
  407.2 15.4 %collective-permute-start.62 = (bf16[32,1536]{1,0:T(8,128)(2,1)S(1)}, bf16[32,1536]{1,0:T(8,128)(2,1)S(1)}, u32[]{:S(2)}, u32[]{:S(2)}) collective-permute-start(bf16[32,1536]{1,0:T(8,128)(2,1)S(1)} %get-tuple-element.254), channel_id=1, source_target_pairs={{0,16},{1,17},{2,18},{3,19},{4,20},{5,21},{6,22},{7,23},{8,24},{9,... | collective-permute-start | bytes 294920 | tf_op jit(solution)/shard_map/ppermute | solution.py:142
  409.8 15.2 %collective-permute-start.61 = (bf16[32,1536]{1,0:T(8,128)(2,1)S(1)}, bf16[32,1536]{1,0:T(8,128)(2,1)S(1)}, u32[]{:S(2)}, u32[]{:S(2)}) collective-permute-start(bf16[32,1536]{1,0:T(8,128)(2,1)S(1)} %get-tuple-element.254), channel_id=1, source_target_pairs={{0,24},{1,25},{2,26},{3,27},{4,28},{5,29},{6,30},{7,31},{8,0},{9,1... | collective-permute-start | bytes 294920 | tf_op jit(solution)/shard_map/ppermute | solution.py:142
  411.1 13.9 %collective-permute-start.64 = (bf16[32,1536]{1,0:T(8,128)(2,1)S(1)}, bf16[32,1536]{1,0:T(8,128)(2,1)S(1)}, u32[]{:S(2)}, u32[]{:S(2)}) collective-permute-start(bf16[32,1536]{1,0:T(8,128)(2,1)S(1)} %get-tuple-element.254), channel_id=1, source_target_pairs={{0,4},{1,5},{2,6},{3,7},{4,0},{5,1},{6,2},{7,3},{8,12},{9,13},{10,... | collective-permute-start | bytes 294920 | tf_op jit(solution)/shard_map/ppermute | solution.py:142
  416.3 13.3 %collective-permute-start.67 = (bf16[32,1536]{1,0:T(8,128)(2,1)S(1)}, bf16[32,1536]{1,0:T(8,128)(2,1)S(1)}, u32[]{:S(2)}, u32[]{:S(2)}) collective-permute-start(bf16[32,1536]{1,0:T(8,128)(2,1)S(1)} %collective-permute-done.63), channel_id=1, source_target_pairs={{0,4},{1,5},{2,6},{3,7},{4,0},{5,1},{6,2},{7,3},{8,12},{9,13},{10,... | collective-permute-start | bytes 294920 | tf_op jit(solution)/shard_map/ppermute | solution.py:142
  437.1 12.7 %collective-permute-start.68 = (bf16[128,1536]{1,0:T(8,128)(2,1)S(1)}, bf16[128,1536]{1,0:T(8,128)(2,1)S(1)}, u32[]{:S(2)}, u32[]{:S(2)}) collective-permute-start(bf16[128,1536]{1,0:T(8,128)(2,1)S(1)} %slice.1071), channel_id=1, source_target_pairs={{0,4},{1,5},{2,6},{3,7},{4,0},{5,1},{6,2},{7,3},{8,12},{9,13},{10,... | collective-permute-start | bytes 1179656 | tf_op jit(solution)/shard_map/ppermute | solution.py:142
  450.0 12.1 %collective-permute-start.69 = (bf16[32,1536]{1,0:T(8,128)(2,1)S(1)}, bf16[32,1536]{1,0:T(8,128)(2,1)S(1)}, u32[]{:S(2)}, u32[]{:S(2)}) collective-permute-start(bf16[32,1536]{1,0:T(8,128)(2,1)S(1)} %get-tuple-element.412), channel_id=1, source_target_pairs={{0,8},{1,9},{2,10},{3,11},{4,12},{5,13},{6,14},{7,15},{8,16},{9,17... | collective-permute-start | bytes 294920 | tf_op jit(solution)/shard_map/ppermute | solution.py:142
  480.2 14.1 %collective-permute-start.72 = (bf16[256,1536]{1,0:T(8,128)(2,1)}, bf16[256,1536]{1,0:T(8,128)(2,1)}, u32[]{:S(2)}, u32[]{:S(2)}) collective-permute-start(bf16[256,1536]{1,0:T(8,128)(2,1)} %slice_add_fusion.3), channel_id=1, source_target_pairs={{0,1},{1,0},{2,3},{3,2},{4,5},{5,4},{6,7},{7,6},{8,9},{9,8},{10,11... | collective-permute-start | bytes 2359304 | tf_op jit(solution)/shard_map/ppermute | solution.py:142
  480.7 128.2 %all-gather.18.cloned.1.call-start = ((), (), s32[]{:S(2)}) async-start(), calls=%async_computation.14 | async-start | bytes 2949120 | tf_op jit(solution)/shard_map/all_gather | solution.py:735
  500.3 39.6 %collective-permute-start.75 = (bf16[4,192,768]{2,1,0:T(8,128)(2,1)}, bf16[4,192,768]{2,1,0:T(8,128)(2,1)}, u32[]{:S(2)}, u32[]{:S(2)}) collective-permute-start(bf16[4,192,768]{2,1,0:T(8,128)(2,1)} %fusion.95), channel_id=1, source_target_pairs={{0,4},{1,5},{2,6},{3,7},{4,0},{5,1},{6,2},{7,3},{8,12},{9,13},{10,... | collective-permute-start | bytes 3538952 | tf_op jit(solution)/shard_map/ppermute | solution.py:142
  548.6 71.4 %reduce-scatter.14.cloned.1.call-start = ((), (), s32[]{:S(2)}) async-start(), calls=%async_computation.10 | async-start | bytes 2949120 | tf_op jit(solution)/shard_map/reduce_scatter | solution.py:680
  549.3 159.2 %all-gather.14.cloned.1.call-start = ((), (), s32[]{:S(2)}) async-start(), calls=%async_computation.12 | async-start | bytes 2949120 | tf_op jit(solution)/shard_map/all_gather | solution.py:736
  553.7 11.7 %collective-permute-start.77 = (bf16[128,1536]{1,0:T(8,128)(2,1)}, bf16[128,1536]{1,0:T(8,128)(2,1)}, u32[]{:S(2)}, u32[]{:S(2)}) collective-permute-start(bf16[128,1536]{1,0:T(8,128)(2,1)} %slice.1086), channel_id=1, source_target_pairs={{0,4},{1,5},{2,6},{3,7},{4,0},{5,1},{6,2},{7,3},{8,12},{9,13},{10,... | collective-permute-start | bytes 1179656 | tf_op jit(solution)/shard_map/ppermute | solution.py:142
  558.0 11.1 %collective-permute-start.83 = (bf16[192,768]{1,0:T(8,128)(2,1)}, bf16[192,768]{1,0:T(8,128)(2,1)}, u32[]{:S(2)}, u32[]{:S(2)}) collective-permute-start(bf16[192,768]{1,0:T(8,128)(2,1)} %get-tuple-element.362), channel_id=1, source_target_pairs={{0,24},{1,25},{2,26},{3,27},{4,28},{5,29},{6,30},{7,31},{8,0},{9,1... | collective-permute-start | bytes 884744 | tf_op jit(solution)/shard_map/ppermute | solution.py:142
  561.3 28.6 %collective-permute-start.82 = (bf16[192,768]{1,0:T(8,128)(2,1)}, bf16[192,768]{1,0:T(8,128)(2,1)}, u32[]{:S(2)}, u32[]{:S(2)}) collective-permute-start(bf16[192,768]{1,0:T(8,128)(2,1)} %get-tuple-element.363), channel_id=1, source_target_pairs={{0,16},{1,17},{2,18},{3,19},{4,20},{5,21},{6,22},{7,23},{8,24},{9,... | collective-permute-start | bytes 884744 | tf_op jit(solution)/shard_map/ppermute | solution.py:142
  561.3 28.6 %collective-permute-start.81 = (bf16[192,768]{1,0:T(8,128)(2,1)}, bf16[192,768]{1,0:T(8,128)(2,1)}, u32[]{:S(2)}, u32[]{:S(2)}) collective-permute-start(bf16[192,768]{1,0:T(8,128)(2,1)} %get-tuple-element.364), channel_id=1, source_target_pairs={{0,8},{1,9},{2,10},{3,11},{4,12},{5,13},{6,14},{7,15},{8,16},{9,17... | collective-permute-start | bytes 884744 | tf_op jit(solution)/shard_map/ppermute | solution.py:142
  562.0 127.6 %collective-permute-start.92 = (bf16[1024,768]{1,0:T(8,128)(2,1)}, bf16[1024,768]{1,0:T(8,128)(2,1)}, u32[]{:S(2)}, u32[]{:S(2)}) collective-permute-start(bf16[1024,768]{1,0:T(8,128)(2,1)} %get-tuple-element.198), channel_id=1, source_target_pairs={{0,2},{1,3},{2,0},{3,1},{4,6},{5,7},{6,4},{7,5},{8,10},{9,11},{10,... | collective-permute-start | bytes 4718600 | tf_op jit(solution)/shard_map/ppermute | solution.py:142
  565.4 33.5 %collective-permute-start.86 = (bf16[4,192,896]{2,1,0:T(8,128)(2,1)}, bf16[4,192,896]{2,1,0:T(8,128)(2,1)}, u32[]{:S(2)}, u32[]{:S(2)}) collective-permute-start(bf16[4,192,896]{2,1,0:T(8,128)(2,1)} %dynamic-slice_bitcast_fusion.1), channel_id=1, source_target_pairs={{0,4},{1,5},{2,6},{3,7},{4,0},{5,1},{6,2},{7,3},{8,12},{9,13},{10,... | collective-permute-start | bytes 4128776 | tf_op jit(solution)/shard_map/ppermute | solution.py:142
  569.0 23.8 %collective-permute-start.78 = (bf16[32,1536]{1,0:T(8,128)(2,1)S(1)}, bf16[32,1536]{1,0:T(8,128)(2,1)S(1)}, u32[]{:S(2)}, u32[]{:S(2)}) collective-permute-start(bf16[32,1536]{1,0:T(8,128)(2,1)S(1)} %get-tuple-element.409), channel_id=1, source_target_pairs={{0,8},{1,9},{2,10},{3,11},{4,12},{5,13},{6,14},{7,15},{8,16},{9,17... | collective-permute-start | bytes 294920 | tf_op jit(solution)/shard_map/ppermute | solution.py:142
  598.0 110.5 %all-gather.12.cloned.1.call-start = ((), (), s32[]{:S(2)}) async-start(), calls=%async_computation.11 | async-start | bytes 2949120 | tf_op jit(solution)/shard_map/all_gather | solution.py:744
  604.4 27.4 %collective-permute-start.89 = (bf16[192,896]{1,0:T(8,128)(2,1)}, bf16[192,896]{1,0:T(8,128)(2,1)}, u32[]{:S(2)}, u32[]{:S(2)}) collective-permute-start(bf16[192,896]{1,0:T(8,128)(2,1)} %get-tuple-element.335), channel_id=1, source_target_pairs={{0,24},{1,25},{2,26},{3,27},{4,28},{5,29},{6,30},{7,31},{8,0},{9,1... | collective-permute-start | bytes 1032200 | tf_op jit(solution)/shard_map/ppermute | solution.py:142
  607.5 29.2 %collective-permute-start.88 = (bf16[192,896]{1,0:T(8,128)(2,1)}, bf16[192,896]{1,0:T(8,128)(2,1)}, u32[]{:S(2)}, u32[]{:S(2)}) collective-permute-start(bf16[192,896]{1,0:T(8,128)(2,1)} %get-tuple-element.336), channel_id=1, source_target_pairs={{0,16},{1,17},{2,18},{3,19},{4,20},{5,21},{6,22},{7,23},{8,24},{9,... | collective-permute-start | bytes 1032200 | tf_op jit(solution)/shard_map/ppermute | solution.py:142
  607.5 29.2 %collective-permute-start.87 = (bf16[192,896]{1,0:T(8,128)(2,1)}, bf16[192,896]{1,0:T(8,128)(2,1)}, u32[]{:S(2)}, u32[]{:S(2)}) collective-permute-start(bf16[192,896]{1,0:T(8,128)(2,1)} %get-tuple-element.337), channel_id=1, source_target_pairs={{0,8},{1,9},{2,10},{3,11},{4,12},{5,13},{6,14},{7,15},{8,16},{9,17... | collective-permute-start | bytes 1032200 | tf_op jit(solution)/shard_map/ppermute | solution.py:142
  642.2 23.6 %collective-permute-start.93 = (bf16[2,96,768]{2,1,0:T(8,128)(2,1)}, bf16[2,96,768]{2,1,0:T(8,128)(2,1)S(1)}, u32[]{:S(2)}, u32[]{:S(2)}) collective-permute-start(bf16[2,96,768]{2,1,0:T(8,128)(2,1)} %pad_maximum_fusion.29), channel_id=1, source_target_pairs={{0,8},{1,9},{2,10},{3,11},{4,12},{5,13},{6,14},{7,15},{8,16},{9,17... | collective-permute-start | bytes 884744 | tf_op jit(solution)/shard_map/ppermute | solution.py:142
  644.3 20.6 %collective-permute-start.94 = (bf16[2,96,768]{2,1,0:T(8,128)(2,1)}, bf16[2,96,768]{2,1,0:T(8,128)(2,1)}, u32[]{:S(2)}, u32[]{:S(2)}) collective-permute-start(bf16[2,96,768]{2,1,0:T(8,128)(2,1)} %pad_maximum_fusion.30), channel_id=1, source_target_pairs={{0,16},{1,17},{2,18},{3,19},{4,20},{5,21},{6,22},{7,23},{8,24},{9,... | collective-permute-start | bytes 884744 | tf_op jit(solution)/shard_map/ppermute | solution.py:142
  646.9 15.2 %collective-permute-start.95 = (bf16[2,96,768]{2,1,0:T(8,128)(2,1)}, bf16[2,96,768]{2,1,0:T(8,128)(2,1)}, u32[]{:S(2)}, u32[]{:S(2)}) collective-permute-start(bf16[2,96,768]{2,1,0:T(8,128)(2,1)} %pad_maximum_fusion.31), channel_id=1, source_target_pairs={{0,24},{1,25},{2,26},{3,27},{4,28},{5,29},{6,30},{7,31},{8,0},{9,1... | collective-permute-start | bytes 884744 | tf_op jit(solution)/shard_map/ppermute | solution.py:142
  650.5 82.0 %all-gather.20.cloned.1.call-start = ((), (), s32[]{:S(2)}) async-start(), calls=%async_computation.15 | async-start | bytes 5898240 | tf_op jit(solution)/shard_map/all_gather | solution.py:768
  656.2 36.3 %collective-permute-start.98 = (bf16[192,1664]{1,0:T(8,128)(2,1)S(1)}, bf16[192,1664]{1,0:T(8,128)(2,1)S(1)}, u32[]{:S(2)}, u32[]{:S(2)}) collective-permute-start(bf16[192,1664]{1,0:T(8,128)(2,1)S(1)} %get-tuple-element.388), channel_id=1, source_target_pairs={{0,2},{1,3},{2,0},{3,1},{4,6},{5,7},{6,4},{7,5},{8,10},{9,11},{10,... | collective-permute-start | bytes 1916936 | tf_op jit(solution)/shard_map/ppermute | solution.py:142
  665.9 15.2 %collective-permute-start.96 = (bf16[4,96,768]{2,1,0:T(8,128)(2,1)S(1)}, bf16[4,96,768]{2,1,0:T(8,128)(2,1)S(1)}, u32[]{:S(2)}, u32[]{:S(2)}) collective-permute-start(bf16[4,96,768]{2,1,0:T(8,128)(2,1)S(1)} %pad_maximum_fusion.18), channel_id=1, source_target_pairs={{0,4},{1,5},{2,6},{3,7},{4,0},{5,1},{6,2},{7,3},{8,12},{9,13},{10,... | collective-permute-start | bytes 1769480 | tf_op jit(solution)/shard_map/ppermute | solution.py:142
  (289 other events, 1860.9 us)
Sparse Core Ops, SparseCore 0:
  27.3 76.0 all-gather.15
  106.1 94.1 all-gather.9
  324.6 31.8 reduce-scatter.7
  359.6 33.2 reduce-scatter.5
  398.9 105.0 reduce-scatter.9
  506.9 34.8 reduce-scatter.11
  548.7 30.4 all-gather.17
  581.9 36.7 reduce-scatter.13
  620.2 24.0 all-gather.13
  650.6 33.1 all-gather.11
  689.0 43.3 all-gather.19
